TPU v7x, 128 devices: a whole 4x4x4 slice. The times are simulated.
128 devices in a mesh: seq: 32 (over y, z, core), head: 4 (over x).
Axes of the slice: x: 4, y: 4, z: 4, core: 2. Of those that a mesh axis runs over, the one named last changes fastest.
Arguments:
- x_quant: bfloat16 [4096, 8192], P('seq', 'head'), may hold values from -6 to 6
- scale_exp: int32 [64, 4096], P('head', 'seq'), may hold values from -2 to 1
- dt_raw: bfloat16 [128, 4096], P('head', 'seq'), may hold values from -5 to 5
- dt_bias: float32 [128], P('head'), may hold values from -3 to -1
- a_log: float32 [128], P('head')
- skip_weight: float32 [128], P('head'), may hold values from 0.5 to 1.5
- b_proj: bfloat16 [4096, 128], P('seq'), may hold values from -4 to 4
- c_proj: bfloat16 [4096, 128], P('seq'), may hold values from -0.5 to 0.5
- doc_starts: int32 [32, 2], P('seq'), may hold values from 0 to 128, as said below
- grad_out: bfloat16 [4096, 8192], P('seq', 'head'), may hold values from -6 to 6
Outputs:
- grad_x: bfloat16 [4096, 8192], P('seq', 'head')
- grad_dt: float32 [128, 4096], P('head', 'seq')
- grad_bc: float32 [2, 4096, 128], P(None, 'seq')
- head_grads: float32 [2, 128], P(None, 'head')
Inputs may be any that keep to these rules, and one draw needn't show every extreme that they name: `doc_starts`: each entry is the offset within its slab of 128 tokens of a token that begins a document, or 128 for an unused entry; a slab's entries are in no order and may repeat.
All inputs are finite; a program needn't handle non-finite values.
Results may differ from a plain program's by a relative error of at most 0.0024.
Values sent between devices are 32-bit elements; how exact they have to be, the bound alone decides.
No kernel may reach another device: no remote copies, remote signals or barrier semaphores. Data moves between devices by JAX's collectives and lax.ppermute only.
A program may use at most 128 MiB of HBM per device.

v0:
```python
import math

import jax
import jax.numpy as jnp
from jax import lax
from jax.sharding import PartitionSpec as P

HEAD_DIM = 64
SPAN = 256


def carried_in(part, axis, combine, identity, reverse):
    count = lax.axis_size(axis)
    place = lax.axis_index(axis)
    ahead = count - 1 - place if reverse else place
    gathered = jax.tree.map(lambda a: lax.all_gather(a, axis), part)
    state = jax.tree.map(lambda a, e: jnp.zeros_like(a) + jnp.asarray(e, a.dtype), part, identity)

    def one(lap, state):
        source = count - 1 - lap if reverse else lap
        return combine(
            state, jax.tree.map(lambda a: lax.dynamic_index_in_dim(a, source, 0, False), gathered)
        )

    return lax.fori_loop(0, ahead, one, state)


def chain_step(earlier, latter):
    return (earlier[0] * latter[0], latter[1] + latter[0][:, None, None] * earlier[1])


def local(
    x_quant, scale_exp, dt_raw, dt_bias, a_log, skip_weight, b_proj, c_proj, doc_starts, grad_out
):
    highest = lax.Precision.HIGHEST
    tokens_here = x_quant.shape[0]
    heads_here = dt_raw.shape[0]
    head_width = HEAD_DIM
    state_width = b_proj.shape[1]
    scale_blocks = scale_exp.shape[0]
    span_len = min(SPAN, tokens_here)
    block_count = tokens_here // span_len
    factor = jnp.left_shift(jnp.int32(1), scale_exp + 8).astype(jnp.float32) / 256.0
    x_vals = (
        (x_quant.astype(jnp.float32).reshape(tokens_here, scale_blocks, 128) * factor.T[:, :, None])
        .reshape(tokens_here, heads_here * head_width)
        .astype(jnp.bfloat16)
    )
    x_heads = (
        x_vals.astype(jnp.float32)
        .reshape(tokens_here, heads_here, head_width)
        .transpose(1, 0, 2)
        .reshape(heads_here, block_count, span_len, head_width)
    )
    g_heads = (
        grad_out.astype(jnp.float32)
        .reshape(tokens_here, heads_here, head_width)
        .transpose(1, 0, 2)
        .reshape(heads_here, block_count, span_len, head_width)
    )
    position = jnp.arange(tokens_here, dtype=jnp.int32)
    resets = jnp.any(position[:, None] == doc_starts[0][None, :], axis=1)
    segment = jnp.cumsum(resets.astype(jnp.int32).reshape(block_count, span_len), axis=1)
    offsets = jnp.arange(span_len, dtype=jnp.int32)
    same_doc = (offsets[:, None] >= offsets[None, :])[None] & (
        segment[:, :, None] == segment[:, None, :]
    )
    pre_act = dt_raw.astype(jnp.float32) + dt_bias[:, None]
    step_size = jax.nn.softplus(pre_act)
    decay_rate = jnp.exp(a_log)
    step_blocks = step_size.reshape(heads_here, block_count, span_len)
    cumulative = jnp.cumsum(-decay_rate[:, None, None] * step_blocks, axis=2)
    first_doc = (segment == 0).astype(jnp.float32)
    last_doc = (segment == segment[:, -1:]).astype(jnp.float32)
    enter_decay = jnp.exp(cumulative) * first_doc[None]
    exit_decay = jnp.exp(cumulative[:, :, -1:] - cumulative) * last_doc[None]
    block_decay = jnp.exp(cumulative[:, :, -1]) * first_doc[None, :, -1]
    b_blocks = b_proj.astype(jnp.float32).reshape(block_count, span_len, state_width)
    c_blocks = c_proj.astype(jnp.float32).reshape(block_count, span_len, state_width)
    scaled_input = x_heads * step_blocks[:, :, :, None]
    kernel = jnp.einsum(
        "qtn,qsn->qts",
        c_proj.reshape(block_count, span_len, state_width),
        b_proj.reshape(block_count, span_len, state_width),
        preferred_element_type=jnp.float32,
    )
    block_state = jnp.einsum(
        "hqsp,qsn->hqpn", exit_decay[:, :, :, None] * scaled_input, b_blocks, precision=highest
    )
    block_grad = jnp.einsum(
        "hqtp,qtn->hqpn", enter_decay[:, :, :, None] * g_heads, c_blocks, precision=highest
    )
    local_state = block_state[:, 0]
    slab_decay = block_decay[:, 0]
    local_grad = block_grad[:, block_count - 1]
    identity = (jnp.ones_like(slab_decay), jnp.zeros_like(local_state))
    state_entry = carried_in((slab_decay, local_state), "seq", chain_step, identity, False)[1]
    grad_exit = carried_in((slab_decay, local_grad), "seq", chain_step, identity, True)[1]
    carried = state_entry
    number = 0
    entries = [carried]
    carried = block_decay[:, number][:, None, None] * carried + block_state[:, number]
    exits = [carried] * block_count
    carried = grad_exit
    number = 0
    exits[number] = carried
    entry_states = jnp.stack(entries, 1)
    exit_grads = jnp.stack(exits, 1)
    group_size = math.gcd(heads_here, max(1, (1 << 21) // (span_len * span_len)))
    group_count = heads_here // group_size
    number = 0

    def within_block(groups, doc_mask=same_doc[number], kern=kernel[number]):
        cumul_group, inputs_group, grads_group = groups
        log_gap = cumul_group[:, :, None] - cumul_group[:, None, :]
        decay_mat = jnp.exp(jnp.where(doc_mask[None], log_gap, -1e30))
        weighted = decay_mat * kern[None]
        input_grad = jnp.einsum("hts,htp->hsp", weighted, grads_group, precision=highest)
        scores = jnp.einsum("htp,hsp->hts", grads_group, inputs_group, precision=highest)
        kernel_part = decay_mat * scores
        flow_terms = kernel_part * kern[None]
        return (
            input_grad,
            jnp.sum(kernel_part, 0),
            jnp.sum(flow_terms, 2) - jnp.sum(flow_terms, 1),
        )

    input_grad, kernel_grad, cumul_grad = lax.map(
        within_block,
        (
            cumulative[:, number].reshape(group_count, group_size, span_len),
            scaled_input[:, number].reshape(group_count, group_size, span_len, head_width),
            g_heads[:, number].reshape(group_count, group_size, span_len, head_width),
        ),
    )
    input_parts = [input_grad.reshape(heads_here, span_len, head_width)]
    kernel_parts = [jnp.sum(kernel_grad, 0)]
    cumul_parts = [cumul_grad.reshape(heads_here, span_len)]
    inner_grad = jnp.stack(input_parts, 1)
    kernel_grad = jnp.stack(kernel_parts, 0)
    cumul_grad = jnp.stack(cumul_parts, 1)
    state_read = jnp.einsum("hqpn,qtn->hqtp", entry_states, c_blocks, precision=highest)
    enter_grad = jnp.sum(g_heads * state_read, axis=3)
    c_extra = jnp.einsum(
        "hqtp,hqpn->qtn", enter_decay[:, :, :, None] * g_heads, entry_states, precision=highest
    )
    back_proj = jnp.einsum("hqpn,qsn->hqsp", exit_grads, b_blocks, precision=highest)
    input_total = inner_grad + exit_decay[:, :, :, None] * back_proj
    exit_grad = jnp.sum(scaled_input * back_proj, axis=3)
    b_extra = jnp.einsum(
        "hqsp,hqpn->qsn", exit_decay[:, :, :, None] * scaled_input, exit_grads, precision=highest
    )
    block_scalar = jnp.sum(exit_grads * entry_states, axis=(2, 3))
    grad_b = (
        jnp.einsum("qts,qtn->qsn", kernel_grad, c_blocks, precision=highest) + b_extra
    ).reshape(tokens_here, state_width)
    grad_c = (
        jnp.einsum("qts,qsn->qtn", kernel_grad, b_blocks, precision=highest) + c_extra
    ).reshape(tokens_here, state_width)
    cumul_total = cumul_grad + enter_grad * enter_decay - exit_grad * exit_decay
    last_terms = jnp.sum(exit_grad * exit_decay, axis=2) + block_scalar * block_decay
    cumul_total = cumul_total.at[:, :, -1].add(last_terms)
    decay_grad = jnp.flip(jnp.cumsum(jnp.flip(cumul_total, 2), 2), 2).reshape(
        heads_here, tokens_here
    )
    step_grad = (
        jnp.sum(input_total * x_heads, axis=3).reshape(heads_here, tokens_here)
        - decay_rate[:, None] * decay_grad
    )
    grad_dt = step_grad * jax.nn.sigmoid(pre_act)
    alog_part = -jnp.sum(decay_grad * step_size, axis=1) * decay_rate
    skip_part = jnp.sum(g_heads * x_heads, axis=(1, 2, 3))
    grad_heads = (
        input_total * step_blocks[:, :, :, None] + skip_weight[:, None, None, None] * g_heads
    )
    grad_x = (
        grad_heads.reshape(heads_here, tokens_here, head_width)
        .transpose(1, 0, 2)
        .reshape(tokens_here, heads_here * head_width)
        .astype(jnp.bfloat16)
    )
    grad_bc = lax.psum(jnp.stack([grad_b, grad_c]), "head")
    totals = lax.psum(jnp.stack([alog_part, skip_part]), "seq")
    total_tokens = tokens_here * lax.axis_size("seq")
    head_grads = totals / math.sqrt(total_tokens * head_width)
    return (grad_x, grad_dt, grad_bc, head_grads)


def solution(mesh):
    in_specs = (
        P("seq", "head"),
        P("head", "seq"),
        P("head", "seq"),
        P("head"),
        P("head"),
        P("head"),
        P("seq", None),
        P("seq", None),
        P("seq", None),
        P("seq", "head"),
    )
    out_specs = (P("seq", "head"), P("head", "seq"), P(None, "seq", None), P(None, "head"))
    return jax.shard_map(local, mesh=mesh, in_specs=in_specs, out_specs=out_specs, check_vma=False)
```

profile of v0, /device:TPU:0, one launch (start us, length us, event | category | flops | bytes accessed | tf_op | source)
XLA Modules:
  0.0 455.5 jit_solution(3068617859672034983)
XLA Ops:
  12.7 2.4 convolution_bitcast_fusion.3
  18.1 69.9 %all-reduce = f32[1024]{0:T(1024)S(1)} all-reduce(f32[1024]{0:T(1024)S(1)} %dynamic-update-slice.3), channel_id=3, replica_groups=mesh['seq'=32,'head'=4] {'seq'}, use_global_device_ids=true, to_apply=%add | all-reduce | flops 1024 | bytes 8192
  89.3 42.8 %all-gather.6.cloned.1.call-done = f32[1024,1,64,128]{3,2,1,0:T(8,128)} async-done(((f32[32,1,64,128]{3,2,1,0:T(8,128)}), f32[1024,1,64,128]{3,2,1,0:T(8,128)}) %all-gather.6.cloned.1.call-update) | async-done | bytes 33554448 | tf_op jit(solution)/shard_map/all_gather | solution.py:16
  132.3 46.3 %while.33 = (s32[]{:T(128)}, f32[32,64,128]{2,1,0:T(8,128)S(1)}, s32[]{:T(128)}, f32[32,32,64,128]{3,2,1,0:T(8,128)}, f32[32,32]{1,0:T(8,128)S(1)}, /*index=5*/s32[]{:T(128)}, s32[]{:T(128)}, s32[]{:T(128)}, s32[]{:T(128)}) while((s32[]{:T(128)}, f32[32,64,128]{2,1,0:T(8,128)S(1)}, s32[]{:T(128)}, f32[32,32,64,128]{3,2,1,0:T(8,128)}, ...), condition=%wide.region_4.5_spmd, body=%wide.region_3.4_spmd.sunk | while | flops 524294 | bytes 3146267 | solution.py:25
  138.3 1.4 bitcast_add_fusion.4
  145.8 1.4 bitcast_add_fusion.4
  147.3 1.4 bitcast_add_fusion.4
  154.7 1.4 bitcast_add_fusion.4
  156.2 1.4 bitcast_add_fusion.4
  159.2 1.4 bitcast_add_fusion.4
  165.2 1.4 bitcast_add_fusion.4
  166.7 1.4 bitcast_add_fusion.4
  168.2 1.4 bitcast_add_fusion.4
  169.7 1.4 bitcast_add_fusion.4
  178.6 1.6 fusion.19
  180.4 1.7 convolution_bitcast_fusion.1
  182.7 3.1 multiply_reduce_fusion
  185.8 2.6 multiply_reduce_fusion.3
  189.5 1.8 convolution_bitcast_fusion.4
  191.5 100.9 %all-gather.8.cloned.1.call-done = f32[1024,1,64,128]{3,2,1,0:T(8,128)} async-done(((f32[32,1,64,128]{3,2,1,0:T(8,128)}), f32[1024,1,64,128]{3,2,1,0:T(8,128)}) %all-gather.8.cloned.1.call-update) | async-done | bytes 33554448 | tf_op jit(solution)/shard_map/all_gather | solution.py:16
  293.7 1.8 fusion.11
  297.5 111.6 %psum.15 = f32[2,32]{1,0:T(2,128)S(1)} all-reduce(f32[2,32]{1,0:T(2,128)S(1)} %pad_maximum_fusion.1), channel_id=1, replica_groups=mesh['seq'=32,'head'=4] {'seq'}, use_global_device_ids=true, to_apply=%region_19.20 | all-reduce | flops 64 | bytes 512 | tf_op jit(solution)/shard_map/psum | solution.py:183
  410.4 36.9 %all-reduce.3.cloned.1.call-done = f32[2,128,128]{2,1,0:T(8,128)} async-done(((f32[2,128,128]{2,1,0:T(8,128)}), f32[2,128,128]{2,1,0:T(8,128)}) %all-reduce.3.cloned.1.call-update) | async-done | bytes 131088 | tf_op jit(solution)/shard_map/psum | solution.py:182
  447.4 1.6 copy.73
  (125 shorter events, 45.8 us)
Async XLA Ops:
  7.2 171.4 %copy-start = (bf16[128,128]{1,0:T(8,128)(2,1)S(1)}, bf16[128,128]{1,0:T(8,128)(2,1)}, u32[]{:S(2)}) copy-start(bf16[128,128]{1,0:T(8,128)(2,1)} %param.22) | copy-start | bytes 98308
  7.2 9.2 %copy-start.9 = (u32[128]{0:T(128)S(1)}, u32[128]{0:T(128)}, u32[]{:S(2)}) copy-start(u32[128]{0:T(128)} %constant.140) | copy-start | bytes 1540
  7.2 80.9 %copy-start.5 = (s32[16,128]{1,0:T(8,128)S(1)}, s32[16,128]{1,0:T(8,128)}, u32[]{:S(2)}) copy-start(s32[16,128]{1,0:T(8,128)} %param.17) | copy-start | bytes 24580
  7.2 125.0 %all-gather.6.cloned.1.call-start = ((), (), s32[]{:S(2)}) async-start(), calls=%async_computation.1 | async-start | bytes 34603008 | tf_op jit(solution)/shard_map/all_gather | solution.py:16
  11.5 77.0 %copy-start.2 = (bf16[128,2048]{1,0:T(8,128)(2,1)S(1)}, bf16[128,2048]{1,0:T(8,128)(2,1)}, u32[]{:S(2)}) copy-start(bf16[128,2048]{1,0:T(8,128)(2,1)} %param.16) | copy-start | bytes 1572868
  15.1 277.3 %all-gather.8.cloned.1.call-start = ((), (), s32[]{:S(2)}) async-start(), calls=%async_computation.2 | async-start | bytes 34603008 | tf_op jit(solution)/shard_map/all_gather | solution.py:16
  180.4 2.2 copy-start.3
  182.1 265.3 %all-reduce.3.cloned.1.call-start = ((), (), s32[]{:S(2)}) async-start(), calls=%async_computation | async-start | bytes 262144 | tf_op jit(solution)/shard_map/psum | solution.py:182
  182.7 3.1 copy-start.1
  182.7 3.1 copy-start.7
  293.1 3.6 copy-start.4
  293.1 3.6 copy-start.6
  293.1 4.4 copy-start.8
Sparse Core Ops, SparseCore 0:
  15.2 116.8 all-gather.5
  182.2 110.1 all-gather.7
  410.0 37.3 all-reduce.2
where the time goes:
time: 457 us; the launch traced here: 455 us
  blocking collectives  182 us (40%)
  waiting for transfers between devices  181 us (40%)
  other arithmetic  52.5 us (11%)
  matrix products  16.2 us (4%)
  between operations  15.3 us (3%)
  local copies, waits for them, and re-layouts  7.87 us (2%)
    all_gather x2, waiting for transfers between devices, carried_in(): gathered = jax.tree.map(lambda a: lax.all_gather(a, axis), part)  144 us
    psum x1, blocking collectives, local(): totals = lax.psum(jnp.stack([alog_part, skip_part]), 'seq')  112 us
    unnamed x1, blocking collectives  69.9 us
    add x31, other arithmetic, chain_step(): latter[1] + latter[0][:, None, None] * earlier[1]  44.9 us
    psum x1, waiting for transfers between devices, local(): grad_bc = lax.psum(jnp.stack([grad_b, grad_c]), 'head')  36.9 us
  transfers between devices with their start and end apart: 3, of which 3 were waited for; matrix products, arithmetic and copies ran while one was open for 3% of the time, Pallas kernels for 0%

commit v1 on v0

v1 whole, which is shorter than its diff:
```python
import functools
import math

import jax
import jax.numpy as jnp
from jax import lax
from jax.experimental import pallas as pl
from jax.experimental.pallas import tpu as pltpu
from jax.sharding import PartitionSpec as P

F32 = jnp.float32
BF16 = jnp.bfloat16
HIGHEST = lax.Precision.HIGHEST
PARTS = 2
ROWS, CHIPS = 4, 4
TOK = 128
HEADS = 32
PAIRS = 16
PART_PAIRS = PAIRS // PARTS
CHUNK_PAIRS = PART_PAIRS // CHIPS
PART_ROWS = PART_PAIRS * TOK
CHUNK_ROWS = CHUNK_PAIRS * TOK
VMEM = pl.BlockSpec(memory_space=pltpu.VMEM)
SMEM = pl.BlockSpec(memory_space=pltpu.SMEM)
VMEM_LIMIT = 24 << 20


def nn(a, b, precision=None):
    return lax.dot_general(
        a, b, (((1,), (0,)), ((), ())), preferred_element_type=F32, precision=precision
    )


def nt(a, b, precision=None):
    return lax.dot_general(
        a, b, (((1,), (1,)), ((), ())), preferred_element_type=F32, precision=precision
    )


def halves(v):
    high = v.astype(BF16)
    return high, (v - high.astype(F32)).astype(BF16)


def iota(shape, axis):
    return lax.broadcasted_iota(jnp.int32, shape, axis)


def column(row, count):
    on = iota((count, count), 0) == iota((count, count), 1)
    return jnp.sum(jnp.where(on, jnp.broadcast_to(row, (count, count)), 0.0), axis=1, keepdims=True)


def pair_column(cols, first, lanes):
    shape = (TOK, 128)
    return jnp.where(
        lanes,
        jnp.broadcast_to(cols[:, first : first + 1], shape),
        jnp.broadcast_to(cols[:, first + 1 : first + 2], shape),
    )


def states_kernel(
    place, doc, xq, scale, dt, bias, alog, b, c, g, x_out, rows_out, cols_out, decay_out, *parts
):
    core = place[0]
    sends, keeps = parts[:PARTS], parts[PARTS:]
    doc0, doc1 = doc[0, 0], doc[0, 1]
    token = iota((HEADS, TOK), 1)
    seg = (token >= doc0).astype(jnp.int32) + (token >= doc1).astype(jnp.int32)
    seg_last = (doc0 < TOK).astype(jnp.int32) + (doc1 < TOK).astype(jnp.int32)
    pre = dt[...].astype(F32) + column(bias[...], HEADS)
    step = jnp.maximum(pre, 0.0) + jnp.log1p(jnp.exp(-jnp.abs(pre)))
    rate = jnp.exp(column(alog[...], HEADS))
    upto = (iota((TOK, TOK), 0) <= iota((TOK, TOK), 1)).astype(F32)
    total = nn(-rate * step, upto, HIGHEST)
    last = jnp.broadcast_to(total[:, TOK - 1 :], (HEADS, TOK))
    enter = jnp.where(seg == 0, jnp.exp(total), 0.0)
    leave = jnp.where(seg == seg_last, jnp.exp(last - total), 0.0)
    block = jnp.where(seg_last == 0, jnp.exp(last), 0.0)
    rows_out[0] = step
    rows_out[1] = total
    rows_out[2] = enter
    rows_out[3] = leave
    rows_out[4] = pre
    rows_out[5] = block
    cols = jnp.concatenate([enter, leave * step, total, step], 0).T
    cols_out[...] = cols
    lanes = iota((TOK, 128), 1) < 64
    pick = iota((PAIRS, HEADS), 1) - 2 * iota((PAIRS, HEADS), 0)
    decay = jnp.where(
        iota((PAIRS, 128), 1) < 64,
        nn((pick == 0).astype(F32), block, HIGHEST),
        nn((pick == 1).astype(F32), block, HIGHEST),
    )
    decay_out[...] = decay
    factor = (jnp.left_shift(jnp.int32(1), scale[...] + 8).astype(F32) / 256.0).T
    b_t = b[...].astype(F32).T.astype(BF16)
    c_t = c[...].astype(F32).T.astype(BF16)
    b_t = jnp.concatenate([b_t, b_t], 1)
    c_t = jnp.concatenate([c_t, c_t], 1)
    for j in range(0, PAIRS, 2):
        left, right = [], []
        for i in (j, j + 1):
            at = slice(128 * i, 128 * i + 128)
            x_pair = xq[:, at].astype(F32) * jnp.broadcast_to(factor[:, i : i + 1], (TOK, 128))
            x_out[:, at] = x_pair.astype(BF16)
            left.append(
                jnp.concatenate(halves(pair_column(cols, HEADS + 2 * i, lanes) * x_pair), 0)
            )
            right.append(
                jnp.concatenate(
                    halves(pair_column(cols, 2 * i, lanes) * g[:, at].astype(F32)), 0
                )
            )
        state = nn(b_t, jnp.concatenate(left, 1))
        grad = nn(c_t, jnp.concatenate(right, 1))
        part = j // PART_PAIRS
        for i in (0, 1):
            at = slice(128 * i, 128 * i + 128)
            to = slice((j + i - part * PART_PAIRS) * 128, (j + i + 1 - part * PART_PAIRS) * 128)
            sends[part][to, :] = jnp.where(core == 0, state[:, at], grad[:, at])
            keeps[part][to, :] = jnp.where(core == 0, grad[:, at], state[:, at])
    for part in range(PARTS):
        own = decay[part * PART_PAIRS : (part + 1) * PART_PAIRS]
        if PART_PAIRS < 8:
            own = jnp.concatenate([own, jnp.zeros((8 - PART_PAIRS, 128), F32)], 0)
        sends[part][PART_ROWS:, :] = own
        keeps[part][PART_ROWS:, :] = own


def chip_kernel(place, keep, recv, *outs):
    spot = place[1]
    own = keep[PART_ROWS:, :]
    both = own * recv[PART_ROWS:, :]
    for distance in range(CHIPS):
        target = (spot + distance) % CHIPS
        first = pl.multiple_of(target * CHUNK_ROWS, CHUNK_ROWS)
        decay = jnp.zeros((CHUNK_PAIRS, 128), F32)
        chip = jnp.zeros((CHUNK_PAIRS, 128), F32)
        for i in range(CHIPS):
            here = slice(i * CHUNK_PAIRS, (i + 1) * CHUNK_PAIRS)
            decay = jnp.where(target == i, own[here], decay)
            chip = jnp.where(target == i, both[here], chip)
        for p in range(CHUNK_PAIRS):
            at = pl.ds(first + p * TOK, TOK)
            outs[distance][p * TOK : (p + 1) * TOK, :] = (
                keep[at, :] + decay[p : p + 1] * recv[at, :]
            )
        outs[distance][CHUNK_ROWS:, :] = jnp.concatenate(
            [chip, jnp.zeros((8 - CHUNK_PAIRS, 128), F32)], 0
        )


def orders(place):
    spots = [(place[1] + k) % CHIPS for k in range(CHIPS)]
    return [jnp.where(place[0] == 1, s, CHIPS - 1 - s) for s in spots]


def row_kernel(place, *refs):
    chunks, out = refs[:CHIPS], refs[CHIPS]
    order = orders(place)
    decays = [chunk[CHUNK_ROWS:, :] for chunk in chunks]
    weights = []
    for k in range(CHIPS):
        weight = jnp.ones((8, 128), F32)
        for m in range(CHIPS):
            if m != k:
                weight = jnp.where(order[m] > order[k], weight * decays[m], weight)
        weights.append(weight)
    for p in range(CHUNK_PAIRS):
        at = slice(p * TOK, (p + 1) * TOK)
        out[at, :] = sum(weights[k][p : p + 1] * chunks[k][at, :] for k in range(CHIPS))
    out[CHUNK_ROWS:, :] = decays[0] * decays[1] * decays[2] * decays[3]


def entry_kernel(place, *refs):
    chunks, rows, outs = refs[:CHIPS], refs[CHIPS : 2 * CHIPS - 1], refs[2 * CHIPS - 1 :]
    order = orders(place)
    decays = [chunk[CHUNK_ROWS:, :] for chunk in chunks]
    one = rows[0][CHUNK_ROWS:, :]
    two = one * rows[1][CHUNK_ROWS:, :]
    zero = jnp.zeros((8, 128), F32)
    weights = []
    for j in range(CHIPS):
        whole = jnp.ones((8, 128), F32)
        for m in range(CHIPS):
            if m != j:
                whole = jnp.where(order[m] < order[j], whole * decays[m], whole)
        terms = []
        for k in range(CHIPS):
            if k == j:
                terms.append(None)
                continue
            weight = jnp.ones((8, 128), F32)
            for m in range(CHIPS):
                if m != j and m != k:
                    between = jnp.logical_and(order[m] > order[k], order[m] < order[j])
                    weight = jnp.where(between, weight * decays[m], weight)
            terms.append(jnp.where(order[k] < order[j], weight, zero))
        weights.append((whole, terms))
    for p in range(CHUNK_PAIRS):
        at = slice(p * TOK, (p + 1) * TOK)
        row = rows[0][at, :] + one[p : p + 1] * rows[1][at, :] + two[p : p + 1] * rows[2][at, :]
        sources = [chunk[at, :] for chunk in chunks]
        for j in range(CHIPS):
            whole, terms = weights[j]
            value = whole[p : p + 1] * row
            for k in range(CHIPS):
                if k != j:
                    value = value + terms[k][p : p + 1] * sources[k]
            outs[j][at, :] = value


def selector(heads):
    return (iota((heads, heads * 64), 1) // 64 == iota((heads, heads * 64), 0)).astype(BF16)


def per_head(values, heads):
    high, low = halves(values)
    pick = selector(heads)
    return nt(pick, high) + nt(pick, low)


def within_kernel(doc, skip, x, g, b, c, rows, cols, gx_out, sums_out, bc_out, work):
    doc0, doc1 = doc[0, 0], doc[0, 1]
    source, target = iota((TOK, TOK), 0), iota((TOK, TOK), 1)
    seg_s = (source >= doc0).astype(jnp.int32) + (source >= doc1).astype(jnp.int32)
    seg_t = (target >= doc0).astype(jnp.int32) + (target >= doc1).astype(jnp.int32)
    mask = jnp.logical_and(target >= source, seg_s == seg_t)
    lanes = iota((TOK, 128), 1) < 64
    kern = nt(b[...], c[...])
    column_values = cols[...]
    kernel_sum = jnp.zeros((TOK, TOK), F32)
    flows = []
    for j in range(PAIRS):
        at = slice(128 * j, 128 * j + 128)
        x_pair, g_pair = x[:, at], g[:, at]
        zero = jnp.zeros_like(x_pair)
        x_both = jnp.concatenate([jnp.where(lanes, x_pair, zero), jnp.where(lanes, zero, x_pair)], 0)
        g_both = jnp.concatenate([jnp.where(lanes, g_pair, zero), jnp.where(lanes, zero, g_pair)], 0)
        scores = nt(x_both, g_pair)
        high, low = [], []
        for i in (0, 1):
            h = 2 * j + i
            total_s = jnp.broadcast_to(column_values[:, 64 + h : 65 + h], (TOK, TOK))
            step_s = jnp.broadcast_to(column_values[:, 96 + h : 97 + h], (TOK, TOK))
            total_t = rows[1, h : h + 1, :]
            decay = jnp.exp(jnp.where(mask, total_t - total_s, -1e30))
            score = decay * (step_s * scores[i * TOK : (i + 1) * TOK])
            kernel_sum = kernel_sum + score
            flows.append(jnp.sum(score * kern, axis=0, keepdims=True))
            weighted = halves(decay * kern)
            high.append(weighted[0])
            low.append(weighted[1])
        inner = nn(jnp.concatenate(high, 1), g_both) + nn(jnp.concatenate(low, 1), g_both)
        x_wide, g_wide = x_pair.astype(F32), g_pair.astype(F32)
        skip_row = jnp.where(iota((1, 128), 1) < 64, skip[2 * j], skip[2 * j + 1])
        gx_out[:, at] = pair_column(column_values, 96 + 2 * j, lanes) * inner + skip_row * g_wide
        work[:TOK, at] = x_wide * inner
        work[TOK:, at] = x_wide * g_wide
    sums = per_head(work[...], HEADS)
    sums_out[0] = jnp.concatenate(flows, 0)
    sums_out[1] = sums[:, :TOK]
    sums_out[2] = sums[:, TOK:]
    high, low = halves(kernel_sum)
    bc_out[0] = nn(high, c[...]) + nn(low, c[...])
    high, low = halves(kernel_sum.T)
    bc_out[1] = nn(high, b[...]) + nn(low, b[...])


def final_kernel(part, place, x, g, b, c, rows, cols, sums, gx, alog, recv, acc, past, *refs):
    mine, theirs = refs[:CHIPS], refs[CHIPS : 2 * CHIPS]
    gx_out, dt_out, bc_out, past_out, work, near = refs[2 * CHIPS :]
    core, spot = place[0], place[1]
    heads = 2 * PART_PAIRS
    first_head = part * heads
    lanes = iota((TOK, 128), 1) < 64
    column_values = cols[...]
    for k in range(CHIPS):
        target = (spot + k) % CHIPS
        first = pl.multiple_of(target * CHUNK_ROWS, CHUNK_ROWS)
        near[0, pl.ds(first, CHUNK_ROWS), :] = mine[k][...]
        near[1, pl.ds(first, CHUNK_ROWS), :] = theirs[k][...]
    b_two = jnp.concatenate([b[...], b[...]], 1)
    c_two = jnp.concatenate([c[...], c[...]], 1)
    grad_b, grad_c = acc[0], acc[1]
    for p in range(PART_PAIRS):
        j = part * PART_PAIRS + p
        at = slice(128 * j, 128 * j + 128)
        local = slice(128 * p, 128 * p + 128)
        full = recv[local, :] + recv[PART_ROWS + p : PART_ROWS + p + 1, :] * near[0, local, :]
        other = near[1, local, :]
        entry = jnp.where(core == 1, full, other)
        leave = jnp.where(core == 1, other, full)
        entry_high, entry_low = halves(entry)
        leave_high, leave_low = halves(leave)
        read = nn(c_two, jnp.concatenate([entry_high, entry_low], 0))
        back = nn(b_two, jnp.concatenate([leave_high, leave_low], 0))
        x_wide, g_wide = x[:, at].astype(F32), g[:, at].astype(F32)
        leave_step = pair_column(column_values, HEADS + 2 * j, lanes)
        gx_out[:, local] = (gx[:, at] + leave_step * back).astype(BF16)
        work[:TOK, local] = g_wide * read
        work[TOK : 2 * TOK, local] = x_wide * back
        work[2 * TOK :, local] = jnp.sum((entry * leave).reshape(TOK // 8, 8, 128), axis=0)
        high, low = halves(pair_column(column_values, 2 * j, lanes) * g_wide)
        grad_c = grad_c + nt(
            jnp.concatenate([high, low, high], 1),
            jnp.concatenate([entry_high, entry_high, entry_low], 1),
        )
        high, low = halves(leave_step * x_wide)
        grad_b = grad_b + nt(
            jnp.concatenate([high, low, high], 1),
            jnp.concatenate([leave_high, leave_high, leave_low], 1),
        )
    bc_out[0] = grad_b
    bc_out[1] = grad_c
    found = per_head(work[...], heads)
    here = slice(first_head, first_head + heads)
    step, enter, leave, pre, block = (rows[k, here, :] for k in (0, 2, 3, 4, 5))
    flow, inner_x = sums[0, here, :], sums[1, here, :]
    read_g, back_x = found[:, :TOK], found[:, TOK : 2 * TOK]
    cross = jnp.sum(found[:, 2 * TOK :], axis=1, keepdims=True)
    rate = jnp.exp(column(alog[...], HEADS))[here]
    left = leave * step * back_x
    moves = flow - step * inner_x + enter * read_g - left
    end = jnp.sum(left, axis=1, keepdims=True) + cross * block[:, :1]
    from_here = (iota((TOK, TOK), 0) >= iota((TOK, TOK), 1)).astype(F32)
    decay_grad = nn(moves, from_here, HIGHEST) + end
    step_grad = inner_x + leave * back_x - rate * decay_grad
    dt_out[...] = step_grad / (1.0 + jnp.exp(-pre))
    logs = -rate * decay_grad * step
    if part < PARTS - 1:
        past_out[...] = logs if part == 0 else jnp.concatenate([past[...], logs], 0)
    else:
        if part:
            logs = jnp.concatenate([past[...], logs], 0)
        ones = jnp.ones((8, TOK), F32)
        past_out[0] = nt(ones, logs, HIGHEST)
        past_out[1] = nt(ones, sums[2], HIGHEST)


def seq_pairs(move):
    pairs = []
    for y in range(ROWS):
        for z in range(CHIPS):
            for core in range(2):
                to = move(y, z, core)
                if to is not None:
                    pairs.append(
                        ((y * CHIPS + z) * 2 + core, (to[0] * CHIPS + to[1]) * 2 + to[2])
                    )
    return pairs


def other_core(value):
    return lax.ppermute(value, "seq", seq_pairs(lambda y, z, core: (y, z, 1 - core)))


def along_z(value, distance):
    return lax.ppermute(
        value, "seq", seq_pairs(lambda y, z, core: (y, (z + distance) % CHIPS, core))
    )


def along_y(value, distance):
    return lax.ppermute(
        value, "seq", seq_pairs(lambda y, z, core: ((y + distance) % ROWS, z, core))
    )


def onward_y(value, distance):
    def move(y, z, core):
        to = y + distance if core else y - distance
        return (to, z, core) if 0 <= to < ROWS else None

    return lax.ppermute(value, "seq", seq_pairs(move))


def call(kernel, ins, outs, name, flops=0, scratch=(), size=0):
    shapes = [jax.ShapeDtypeStruct(s, d) for s, d in outs]
    return pl.pallas_call(
        kernel,
        out_shape=shapes,
        in_specs=[SMEM if smem else VMEM for smem, _ in ins],
        out_specs=[VMEM] * len(outs),
        scratch_shapes=list(scratch),
        name=name,
        compiler_params=pltpu.CompilerParams(vmem_limit_bytes=VMEM_LIMIT),
        cost_estimate=pl.CostEstimate(flops=flops, bytes_accessed=size, transcendentals=0),
    )(*[value for _, value in ins])


def local(
    x_quant, scale_exp, dt_raw, dt_bias, a_log, skip_weight, b_proj, c_proj, doc_starts, grad_out
):
    index = lax.axis_index("seq")
    place = jnp.stack([index % 2, (index // 2) % CHIPS]).astype(jnp.int32)
    alog_row = a_log.reshape(1, HEADS)
    part_shape = (PART_ROWS + 8 * -(-PART_PAIRS // 8), 128)
    chunk_shape = (CHUNK_ROWS + 8, 128)
    made = call(
        states_kernel,
        [
            (1, place),
            (1, doc_starts),
            (0, x_quant),
            (0, scale_exp),
            (0, dt_raw),
            (0, dt_bias.reshape(1, HEADS)),
            (0, alog_row),
            (0, b_proj),
            (0, c_proj),
            (0, grad_out),
        ],
        [((TOK, 2048), BF16), ((6, HEADS, TOK), F32), ((TOK, 128), F32), ((PAIRS, 128), F32)]
        + [(part_shape, F32)] * (2 * PARTS),
        "states",
        flops=4 * 128 * 256 * 2048,
        size=4 << 20,
    )
    x_vals, rows, cols = made[:3]
    sends, keeps = made[4 : 4 + PARTS], made[4 + PARTS :]
    recvs = [other_core(s) for s in sends]
    chunks = []
    for part in range(PARTS):
        cut = call(
            chip_kernel,
            [(1, place), (0, keeps[part]), (0, recvs[part])],
            [(chunk_shape, F32)] * CHIPS,
            "chip_total",
            size=3 << 20,
        )
        chunks.append([cut[0]] + [along_z(cut[CHIPS - k], -k) for k in range(1, CHIPS)])
    gx, sums, bc = call(
        within_kernel,
        [
            (1, doc_starts),
            (1, skip_weight),
            (0, x_vals),
            (0, grad_out),
            (0, b_proj),
            (0, c_proj),
            (0, rows),
            (0, cols),
        ],
        [((TOK, 2048), F32), ((3, HEADS, TOK), F32), ((2, TOK, 128), F32)],
        "within",
        flops=2 * 32 * 3 * 128**3,
        scratch=[pltpu.VMEM((2 * TOK, 2048), F32)],
        size=4 << 20,
    )
    mine = []
    for part in range(PARTS):
        (row,) = call(
            row_kernel,
            [(1, place)] + [(0, v) for v in chunks[part]],
            [(chunk_shape, F32)],
            "row_total",
            size=1 << 20,
        )
        before = [onward_y(row, k) for k in range(1, ROWS)]
        out = call(
            entry_kernel,
            [(1, place)] + [(0, v) for v in chunks[part] + before],
            [((CHUNK_ROWS, 128), F32)] * CHIPS,
            "entries",
            size=2 << 20,
        )
        mine.append([out[0]] + [along_z(out[CHIPS - k], -k) for k in range(1, CHIPS)])
    theirs = [[other_core(v) for v in part] for part in mine]
    past = jnp.zeros((8, 128), F32)
    gx_parts, dt_parts = [], []
    for part in range(PARTS):
        last = part == PARTS - 1
        done = (part + 1) * 2 * PART_PAIRS
        gx_part, dt_part, bc, past = call(
            functools.partial(final_kernel, part),
            [(1, place)]
            + [
                (0, v)
                for v in [x_vals, grad_out, b_proj, c_proj, rows, cols, sums, gx, alog_row]
                + [recvs[part], bc, past]
                + mine[part]
                + theirs[part]
            ],
            [
                ((TOK, PART_PAIRS * 128), BF16),
                ((2 * PART_PAIRS, TOK), F32),
                ((2, TOK, 128), F32),
                ((2, 8, HEADS), F32) if last else ((done, TOK), F32),
            ],
            "final",
            flops=2 * PART_PAIRS * 128**3 * 10,
            scratch=[
                pltpu.VMEM((2 * TOK + 8, PART_PAIRS * 128), F32),
                pltpu.VMEM((2, PART_ROWS, 128), F32),
            ],
            size=4 << 20,
        )
        gx_parts.append(gx_part)
        dt_parts.append(dt_part)
    grad_x = jnp.concatenate(gx_parts, 1)
    grad_dt = jnp.concatenate(dt_parts, 0)
    grad_bc = bc
    for k in range(1, 4):
        grad_bc = grad_bc + lax.ppermute(bc, "head", [(i, (i + k) % 4) for i in range(4)])
    totals = past
    totals = totals + other_core(totals)
    totals = totals + along_z(totals, 1) + along_z(totals, 2) + along_z(totals, 3)
    totals = totals + along_y(totals, 1) + along_y(totals, 2) + along_y(totals, 3)
    head_grads = totals[:, 0, :] / math.sqrt(TOK * 32 * 64)
    return (grad_x, grad_dt, grad_bc, head_grads)


def solution(mesh):
    in_specs = (
        P("seq", "head"),
        P("head", "seq"),
        P("head", "seq"),
        P("head"),
        P("head"),
        P("head"),
        P("seq", None),
        P("seq", None),
        P("seq", None),
        P("seq", "head"),
    )
    out_specs = (P("seq", "head"), P("head", "seq"), P(None, "seq", None), P(None, "head"))
    return jax.shard_map(local, mesh=mesh, in_specs=in_specs, out_specs=out_specs, check_vma=False)
```

time: 457 us -> 87.8 us (0.19)
  blocking collectives: 182 us -> 0 us
  waiting for transfers between devices: 181 us -> 26.1 us
  other arithmetic: 52.5 us -> 2.78 us
  starting transfers between devices: 0.12 us -> 37.4 us
  matrix products: 16.2 us -> 0 us
  Pallas kernels: 0 us -> 15.7 us
  between operations: 15.3 us -> 0.94 us
    all_gather x2 -> x0, waiting for transfers between devices: 144 us -> none  [carried_in(): gathered = jax.tree.map(lambda a: lax.all_gather(a, axis), part)]
    psum x1 -> x0, blocking collectives: 112 us -> none  [local(): totals = lax.psum(jnp.stack([alog_part, skip_part]), 'seq')]
    unnamed x1 -> x0, blocking collectives: 69.9 us -> none
    add x32 -> x3, other arithmetic: 45 us -> 0.7 us  [the longest x1 0.69 us: local(): grad_bc + lax.ppermute(bc, 'head', [(i, (i + k) % 4) for i in range(4)])]
    ppermute x0 -> x38, starting transfers between devices: none -> 37.4 us  [the longest x15 20.4 us: along_z(): lax.ppermute(value, 'seq', seq_pairs(lambda y, z, core: (y, (z + distance...]
    psum x1 -> x0, waiting for transfers between devices: 36.9 us -> none  [local(): grad_bc = lax.psum(jnp.stack([grad_b, grad_c]), 'head')]
    ppermute x0 -> x38, waiting for transfers between devices: none -> 26.1 us  [the longest x15 15.4 us: along_z(): lax.ppermute(value, 'seq', seq_pairs(lambda y, z, core: (y, (z + distance...]
    dot_general x11 -> x0, matrix products: 16.2 us -> none  [the longest x1 3.07 us: within_block(): jnp.einsum('htp,hsp->hts', grads_group, inputs_group, precision=highest)]
  transfers between devices with their start and end apart: 3 -> 38, of which waited for: 3 -> 18; matrix products, arithmetic and copies ran while one was open for 3% -> 2% of each run, Pallas kernels for 0% -> 11%
where the time goes in v1:
time: 87.8 us; the launch traced here: 87 us
  starting transfers between devices  37.4 us (43%)
  waiting for transfers between devices  26.1 us (30%)
  Pallas kernels  15.7 us (18%)
  local copies, waits for them, and re-layouts  4.12 us (5%)
  other arithmetic  2.78 us (3%)
  between operations  0.94 us (1%)
    ppermute x15, starting transfers between devices, along_z(): lax.ppermute(value, 'seq', seq_pairs(lambda y, z, core: (y, (z + distance...  20.4 us
    pallas_call x10, Pallas kernels, call(): pl.pallas_call(kernel, out_shape=shapes, in_specs=[SMEM if smem else VMEM...  15.7 us
    ppermute x15, waiting for transfers between devices, along_z(): lax.ppermute(value, 'seq', seq_pairs(lambda y, z, core: (y, (z + distance...  15.4 us
    ppermute x6, starting transfers between devices, onward_y(): return lax.ppermute(value, 'seq', seq_pairs(move))  7.75 us
    ppermute x3, starting transfers between devices, local(): lax.ppermute(bc, 'head', [(i, (i + k) % 4) for i in range(4)])  4.45 us
    unnamed x22, local copies, waits for them, and re-layouts  4.11 us
    ppermute x6, waiting for transfers between devices, onward_y(): return lax.ppermute(value, 'seq', seq_pairs(move))  4 us
    ppermute x3, waiting for transfers between devices, along_y(): lax.ppermute(value, 'seq', seq_pairs(lambda y, z, core: ((y + distance) %...  2.72 us
  transfers between devices with their start and end apart: 38, of which 18 were waited for; matrix products, arithmetic and copies ran while one was open for 2% of the time, Pallas kernels for 11%

profile of v1, /device:TPU:0, one launch (start us, length us, event | category | flops | bytes accessed | tf_op | source)
XLA Modules:
  0.0 87.0 jit_solution(10838656074040262708)
XLA Ops:
  4.2 3.4 %states.1 = (bf16[128,2048]{1,0:T(8,128)(2,1)S(1)}, f32[6,32,128]{2,1,0:T(8,128)S(1)}, f32[128,128]{1,0:T(8,128)S(1)}, f32[16,128]{1,0:T(8,128)}, f32[1032,128]{...) custom-call(s32[2]{0:T(128)S(1)} %pad_add_fusion.place, ...), custom_call_target="tpu_custom_call" | custom-call | flops 268435456 | bytes 4194304 | tf_op jit(solution)/shard_map/states/pallas_call | solution.py:382
  8.1 1.4 %collective-permute-done.recv = f32[1032,128]{1,0:T(8,128)S(1)} collective-permute-done((f32[1032,128]{1,0:T(8,128)S(1)}, f32[1032,128]{1,0:T(8,128)S(1)}, u32[]{:S(2)}, u32[]{:S(2)}) %collective-permute-start) | collective-permute-done | bytes 528416 | tf_op jit(solution)/shard_map/ppermute | solution.py:357
  10.1 4.2 %collective-permute-start.1 = (f32[264,128]{1,0:T(8,128)S(1)}, f32[264,128]{1,0:T(8,128)S(1)}, u32[]{:S(2)}, u32[]{:S(2)}) collective-permute-start(f32[264,128]{1,0:T(8,128)S(1)} %get-tuple-element.47), channel_id=1, source_target_pairs={{0,24},{4,28},{8,0},{12,4},{16,8},{20,12},{24,16},{28,20},{32,56},... | collective-permute-start | bytes 405512 | tf_op jit(solution)/shard_map/ppermute | solution.py:361
  16.2 2.0 %collective-permute-start.15 = (f32[264,128]{1,0:T(8,128)S(1)}, f32[264,128]{1,0:T(8,128)S(1)}, u32[]{:S(2)}, u32[]{:S(2)}) collective-permute-start(f32[264,128]{1,0:T(8,128)S(1)} %get-tuple-element.60), channel_id=1, source_target_pairs={{0,24},{4,28},{8,0},{12,4},{16,8},{20,12},{24,16},{28,20},{32,56},... | collective-permute-start | bytes 405512 | tf_op jit(solution)/shard_map/ppermute | solution.py:361
  18.3 2.3 %collective-permute-start.16 = (f32[264,128]{1,0:T(8,128)S(1)}, f32[264,128]{1,0:T(8,128)S(1)}, u32[]{:S(2)}, u32[]{:S(2)}) collective-permute-start(f32[264,128]{1,0:T(8,128)S(1)} %get-tuple-element.61), channel_id=1, source_target_pairs={{0,16},{4,20},{8,24},{12,28},{16,0},{20,4},{24,8},{28,12},{32,48},... | collective-permute-start | bytes 405512 | tf_op jit(solution)/shard_map/ppermute | solution.py:361
  22.3 2.2 %collective-permute-done.3.refs_3_ = f32[264,128]{1,0:T(8,128)S(1)} collective-permute-done((f32[264,128]{1,0:T(8,128)S(1)}, f32[264,128]{1,0:T(8,128)S(1)}, u32[]{:S(2)}, u32[]{:S(2)}) %collective-permute-start.3) | collective-permute-done | bytes 135200 | tf_op jit(solution)/shard_map/ppermute | solution.py:361
  35.0 3.0 %collective-permute-done.6.refs_6_ = f32[264,128]{1,0:T(8,128)S(1)} collective-permute-done((f32[264,128]{1,0:T(8,128)S(1)}, f32[264,128]{1,0:T(8,128)S(1)}, u32[]{:S(2)}, u32[]{:S(2)}) %collective-permute-start.6) | collective-permute-done | bytes 135200 | tf_op jit(solution)/shard_map/ppermute | solution.py:377
  38.7 1.3 %collective-permute-start.7 = (f32[256,128]{1,0:T(8,128)S(1)}, f32[256,128]{1,0:T(8,128)S(1)}, u32[]{:S(2)}, u32[]{:S(2)}) collective-permute-start(f32[256,128]{1,0:T(8,128)S(1)} %get-tuple-element.51), channel_id=1, source_target_pairs={{0,24},{4,28},{8,0},{12,4},{16,8},{20,12},{24,16},{28,20},{32,56},... | collective-permute-start | bytes 393224 | tf_op jit(solution)/shard_map/ppermute | solution.py:361
  40.0 1.5 %collective-permute-start.8 = (f32[256,128]{1,0:T(8,128)S(1)}, f32[256,128]{1,0:T(8,128)S(1)}, u32[]{:S(2)}, u32[]{:S(2)}) collective-permute-start(f32[256,128]{1,0:T(8,128)S(1)} %get-tuple-element.52), channel_id=1, source_target_pairs={{0,16},{4,20},{8,24},{12,28},{16,0},{20,4},{24,8},{28,12},{32,48},... | collective-permute-start | bytes 393224 | tf_op jit(solution)/shard_map/ppermute | solution.py:361
  41.5 1.3 %collective-permute-start.9 = (f32[256,128]{1,0:T(8,128)S(1)}, f32[256,128]{1,0:T(8,128)S(1)}, u32[]{:S(2)}, u32[]{:S(2)}) collective-permute-start(f32[256,128]{1,0:T(8,128)S(1)} %get-tuple-element.53), channel_id=1, source_target_pairs={{0,8},{4,12},{8,16},{12,20},{16,24},{20,28},{24,0},{28,4},{32,40},... | collective-permute-start | bytes 393224 | tf_op jit(solution)/shard_map/ppermute | solution.py:361
  43.7 1.8 %collective-permute-start.21 = (f32[256,128]{1,0:T(8,128)S(1)}, f32[256,128]{1,0:T(8,128)S(1)}, u32[]{:S(2)}, u32[]{:S(2)}) collective-permute-start(f32[256,128]{1,0:T(8,128)S(1)} %get-tuple-element.64), channel_id=1, source_target_pairs={{0,24},{4,28},{8,0},{12,4},{16,8},{20,12},{24,16},{28,20},{32,56},... | collective-permute-start | bytes 393224 | tf_op jit(solution)/shard_map/ppermute | solution.py:361
  45.6 1.7 %collective-permute-start.22 = (f32[256,128]{1,0:T(8,128)S(1)}, f32[256,128]{1,0:T(8,128)S(1)}, u32[]{:S(2)}, u32[]{:S(2)}) collective-permute-start(f32[256,128]{1,0:T(8,128)S(1)} %get-tuple-element.65), channel_id=1, source_target_pairs={{0,16},{4,20},{8,24},{12,28},{16,0},{20,4},{24,8},{28,12},{32,48},... | collective-permute-start | bytes 393224 | tf_op jit(solution)/shard_map/ppermute | solution.py:361
  48.9 1.5 %collective-permute-done.9.refs_3_ = f32[256,128]{1,0:T(8,128)S(1)} collective-permute-done((f32[256,128]{1,0:T(8,128)S(1)}, f32[256,128]{1,0:T(8,128)S(1)}, u32[]{:S(2)}, u32[]{:S(2)}) %collective-permute-start.9) | collective-permute-done | bytes 131104 | tf_op jit(solution)/shard_map/ppermute | solution.py:361
  51.1 2.5 %collective-permute-done.22.refs_2_ = f32[256,128]{1,0:T(8,128)S(1)} collective-permute-done((f32[256,128]{1,0:T(8,128)S(1)}, f32[256,128]{1,0:T(8,128)S(1)}, u32[]{:S(2)}, u32[]{:S(2)}) %collective-permute-start.22) | collective-permute-done | bytes 131104 | tf_op jit(solution)/shard_map/ppermute | solution.py:361
  53.6 2.7 %collective-permute-done.23.refs_3_ = f32[256,128]{1,0:T(8,128)S(1)} collective-permute-done((f32[256,128]{1,0:T(8,128)S(1)}, f32[256,128]{1,0:T(8,128)S(1)}, u32[]{:S(2)}, u32[]{:S(2)}) %collective-permute-start.23) | collective-permute-done | bytes 131104 | tf_op jit(solution)/shard_map/ppermute | solution.py:361
  57.8 3.4 %within.1 = (f32[128,2048]{1,0:T(8,128)S(1)}, f32[3,32,128]{2,1,0:T(8,128)S(1)}, f32[2,128,128]{2,1,0:T(8,128)S(1)}) custom-call(s32[1,2]{1,0:T(1,128)S(1)} %copy-done.9, f32[32]{0:T(128)S(1)} %copy-done.10, bf16[128,2048]{1,0:T(8,128)(2,1)S(1)} %get-tuple-element.38.x, bf16[128,2048]{1,0:T(8,128)(2,1)S(1)} %copy-done.1, bf16[128,128]{1,0:T(8,128)(2,1)S(1)} %copy-done.3, ...), custom_call_target="tpu_custom_call" | custom-call | flops 402653184 | bytes 4194304 | tf_op jit(solution)/shard_map/within/pallas_call | solution.py:382
  61.2 2.4 %final.2 = (bf16[128,1024]{1,0:T(8,128)(2,1)S(1)}, f32[16,128]{1,0:T(8,128)S(1)}, f32[2,128,128]{2,1,0:T(8,128)S(1)}, f32[16,128]{1,0:T(8,128)S(1)}) custom-call(s32[2]{0:T(128)S(1)} %pad_add_fusion.place, bf16[128,2048]{1,0:T(8,128)(2,1)S(1)} %get-tuple-element.38.x, bf16[128,2048]{1,0:T(8,128)(2,1)S(1)} %copy-done.1, bf16[128,128]{1,0:T(8,128)(2,1)S(1)} %copy-done.3, ...), custom_call_target="tpu_custom_call" | custom-call | flops 335544320 | bytes 4194304 | tf_op jit(solution)/shard_map/final/pallas_call | solution.py:382
  63.7 2.6 %final.3 = (bf16[128,1024]{1,0:T(8,128)(2,1)S(1)}, f32[16,128]{1,0:T(8,128)S(1)}, f32[2,128,128]{2,1,0:T(8,128)S(1)}, f32[2,8,32]{2,1,0:T(8,128)S(1)}) custom-call(s32[2]{0:T(128)S(1)} %pad_add_fusion.place, bf16[128,2048]{1,0:T(8,128)(2,1)S(1)} %get-tuple-element.38.x, bf16[128,2048]{1,0:T(8,128)(2,1)S(1)} %copy-done.1, bf16[128,128]{1,0:T(8,128)(2,1)S(1)} %copy-done.3, ...), custom_call_target="tpu_custom_call" | custom-call | flops 335544320 | bytes 4194304 | tf_op jit(solution)/shard_map/final/pallas_call | solution.py:382
  66.5 2.8 %collective-permute-start.30 = (f32[2,128,128]{2,1,0:T(8,128)S(1)}, f32[2,128,128]{2,1,0:T(8,128)S(1)}, u32[]{:S(2)}, u32[]{:S(2)}) collective-permute-start(f32[2,128,128]{2,1,0:T(8,128)S(1)} %get-tuple-element.70), channel_id=1, source_target_pairs={{0,3},{1,0},{2,1},{3,2},{4,7},{5,4},{6,5},{7,6},{8,11},{9,8},{10,9... | collective-permute-start | bytes 393224 | tf_op jit(solution)/shard_map/ppermute | solution.py:507
  70.7 1.4 %collective-permute-start.32 = (f32[2,8,32]{2,1,0:T(8,128)S(1)}, f32[2,8,32]{2,1,0:T(8,128)S(1)}, u32[]{:S(2)}, u32[]{:S(2)}) collective-permute-start(f32[2,8,32]{2,1,0:T(8,128)S(1)} %add.43), channel_id=1, source_target_pairs={{0,8},{4,12},{8,16},{12,20},{16,24},{20,28},{24,0},{28,4},{32,40},... | collective-permute-start | bytes 6152 | tf_op jit(solution)/shard_map/ppermute | solution.py:361
  73.8 2.1 %collective-permute-done.33 = f32[2,8,32]{2,1,0:T(8,128)S(1)} collective-permute-done((f32[2,8,32]{2,1,0:T(8,128)S(1)}, f32[2,8,32]{2,1,0:T(8,128)S(1)}, u32[]{:S(2)}, u32[]{:S(2)}) %collective-permute-start.33) | collective-permute-done | bytes 2080 | tf_op jit(solution)/shard_map/ppermute | solution.py:361
  76.5 1.6 %collective-permute-start.37 = (f32[2,8,32]{2,1,0:T(8,128)S(1)}, f32[2,8,32]{2,1,0:T(8,128)S(1)}, u32[]{:S(2)}, u32[]{:S(2)}) collective-permute-start(f32[2,8,32]{2,1,0:T(8,128)S(1)} %add_add_fusion.1), channel_id=1, source_target_pairs={{0,96},{4,100},{8,104},{12,108},{16,112},{20,116},{24,120},{28,124... | collective-permute-start | bytes 6152 | tf_op jit(solution)/shard_map/ppermute | solution.py:367
  81.0 2.2 %collective-permute-done.36 = f32[2,8,32]{2,1,0:T(8,128)S(1)} collective-permute-done((f32[2,8,32]{2,1,0:T(8,128)S(1)}, f32[2,8,32]{2,1,0:T(8,128)S(1)}, u32[]{:S(2)}, u32[]{:S(2)}) %collective-permute-start.36) | collective-permute-done | bytes 2080 | tf_op jit(solution)/shard_map/ppermute | solution.py:367
  83.8 2.5 %collective-permute-done.28 = f32[2,128,128]{2,1,0:T(8,128)S(1)} collective-permute-done((f32[2,128,128]{2,1,0:T(8,128)S(1)}, f32[2,128,128]{2,1,0:T(8,128)S(1)}, u32[]{:S(2)}, u32[]{:S(2)}) %collective-permute-start.28) | collective-permute-done | bytes 131104 | tf_op jit(solution)/shard_map/ppermute | solution.py:507
  (92 shorter events, 32.1 us)
Async XLA Ops:
  7.6 8.0 %collective-permute-start.14 = (f32[1032,128]{1,0:T(8,128)S(1)}, f32[1032,128]{1,0:T(8,128)S(1)}, u32[]{:S(2)}, u32[]{:S(2)}) collective-permute-start(f32[1032,128]{1,0:T(8,128)S(1)} %get-tuple-element.55), channel_id=1, source_target_pairs={{0,4},{4,0},{8,12},{12,8},{16,20},{20,16},{24,28},{28,24},{32,36},... | collective-permute-start | bytes 1585160 | tf_op jit(solution)/shard_map/ppermute | solution.py:357
  10.1 11.4 %collective-permute-start.1 = (f32[264,128]{1,0:T(8,128)S(1)}, f32[264,128]{1,0:T(8,128)S(1)}, u32[]{:S(2)}, u32[]{:S(2)}) collective-permute-start(f32[264,128]{1,0:T(8,128)S(1)} %get-tuple-element.47), channel_id=1, source_target_pairs={{0,24},{4,28},{8,0},{12,4},{16,8},{20,12},{24,16},{28,20},{32,56},... | collective-permute-start | bytes 405512 | tf_op jit(solution)/shard_map/ppermute | solution.py:361
  14.3 8.0 %collective-permute-start.2 = (f32[264,128]{1,0:T(8,128)S(1)}, f32[264,128]{1,0:T(8,128)S(1)}, u32[]{:S(2)}, u32[]{:S(2)}) collective-permute-start(f32[264,128]{1,0:T(8,128)S(1)} %get-tuple-element.48), channel_id=1, source_target_pairs={{0,16},{4,20},{8,24},{12,28},{16,0},{20,4},{24,8},{28,12},{32,48},... | collective-permute-start | bytes 405512 | tf_op jit(solution)/shard_map/ppermute | solution.py:361
  14.3 10.2 %collective-permute-start.3 = (f32[264,128]{1,0:T(8,128)S(1)}, f32[264,128]{1,0:T(8,128)S(1)}, u32[]{:S(2)}, u32[]{:S(2)}) collective-permute-start(f32[264,128]{1,0:T(8,128)S(1)} %get-tuple-element.49), channel_id=1, source_target_pairs={{0,8},{4,12},{8,16},{12,20},{16,24},{20,28},{24,0},{28,4},{32,40},... | collective-permute-start | bytes 405512 | tf_op jit(solution)/shard_map/ppermute | solution.py:361
  16.2 11.5 %collective-permute-start.15 = (f32[264,128]{1,0:T(8,128)S(1)}, f32[264,128]{1,0:T(8,128)S(1)}, u32[]{:S(2)}, u32[]{:S(2)}) collective-permute-start(f32[264,128]{1,0:T(8,128)S(1)} %get-tuple-element.60), channel_id=1, source_target_pairs={{0,24},{4,28},{8,0},{12,4},{16,8},{20,12},{24,16},{28,20},{32,56},... | collective-permute-start | bytes 405512 | tf_op jit(solution)/shard_map/ppermute | solution.py:361
  18.3 10.8 %collective-permute-start.16 = (f32[264,128]{1,0:T(8,128)S(1)}, f32[264,128]{1,0:T(8,128)S(1)}, u32[]{:S(2)}, u32[]{:S(2)}) collective-permute-start(f32[264,128]{1,0:T(8,128)S(1)} %get-tuple-element.61), channel_id=1, source_target_pairs={{0,16},{4,20},{8,24},{12,28},{16,0},{20,4},{24,8},{28,12},{32,48},... | collective-permute-start | bytes 405512 | tf_op jit(solution)/shard_map/ppermute | solution.py:361
  21.5 8.0 %collective-permute-start.17 = (f32[264,128]{1,0:T(8,128)S(1)}, f32[264,128]{1,0:T(8,128)S(1)}, u32[]{:S(2)}, u32[]{:S(2)}) collective-permute-start(f32[264,128]{1,0:T(8,128)S(1)} %get-tuple-element.62), channel_id=1, source_target_pairs={{0,8},{4,12},{8,16},{12,20},{16,24},{20,28},{24,0},{28,4},{32,40},... | collective-permute-start | bytes 405512 | tf_op jit(solution)/shard_map/ppermute | solution.py:361
  25.1 7.7 %collective-permute-start.4 = (f32[264,128]{1,0:T(8,128)S(1)}, f32[264,128]{1,0:T(8,128)S(1)}, u32[]{:S(2)}, u32[]{:S(2)}) collective-permute-start(f32[264,128]{1,0:T(8,128)S(1)} %row_total.2), channel_id=1, source_target_pairs={{4,36},{12,44},{20,52},{28,60},{32,0},{36,68},{40,8},{44,76},{48,1... | collective-permute-start | bytes 405512 | tf_op jit(solution)/shard_map/ppermute | solution.py:377
  26.4 8.5 %collective-permute-start.5 = (f32[264,128]{1,0:T(8,128)S(1)}, f32[264,128]{1,0:T(8,128)S(1)}, u32[]{:S(2)}, u32[]{:S(2)}) collective-permute-start(f32[264,128]{1,0:T(8,128)S(1)} %row_total.2), channel_id=1, source_target_pairs={{4,68},{12,76},{20,84},{28,92},{36,100},{44,108},{52,116},{60,124}... | collective-permute-start | bytes 405512 | tf_op jit(solution)/shard_map/ppermute | solution.py:377
  27.8 10.2 %collective-permute-start.6 = (f32[264,128]{1,0:T(8,128)S(1)}, f32[264,128]{1,0:T(8,128)S(1)}, u32[]{:S(2)}, u32[]{:S(2)}) collective-permute-start(f32[264,128]{1,0:T(8,128)S(1)} %row_total.2), channel_id=1, source_target_pairs={{4,100},{12,108},{20,116},{28,124},{96,0},{104,8},{112,16},{120,24... | collective-permute-start | bytes 405512 | tf_op jit(solution)/shard_map/ppermute | solution.py:377
  30.2 11.3 %collective-permute-start.18 = (f32[264,128]{1,0:T(8,128)S(1)}, f32[264,128]{1,0:T(8,128)S(1)}, u32[]{:S(2)}, u32[]{:S(2)}) collective-permute-start(f32[264,128]{1,0:T(8,128)S(1)} %row_total.3), channel_id=1, source_target_pairs={{4,36},{12,44},{20,52},{28,60},{32,0},{36,68},{40,8},{44,76},{48,1... | collective-permute-start | bytes 405512 | tf_op jit(solution)/shard_map/ppermute | solution.py:377
  31.5 11.4 %collective-permute-start.19 = (f32[264,128]{1,0:T(8,128)S(1)}, f32[264,128]{1,0:T(8,128)S(1)}, u32[]{:S(2)}, u32[]{:S(2)}) collective-permute-start(f32[264,128]{1,0:T(8,128)S(1)} %row_total.3), channel_id=1, source_target_pairs={{4,68},{12,76},{20,84},{28,92},{36,100},{44,108},{52,116},{60,124}... | collective-permute-start | bytes 405512 | tf_op jit(solution)/shard_map/ppermute | solution.py:377
  32.8 10.2 %collective-permute-start.20 = (f32[264,128]{1,0:T(8,128)S(1)}, f32[264,128]{1,0:T(8,128)S(1)}, u32[]{:S(2)}, u32[]{:S(2)}) collective-permute-start(f32[264,128]{1,0:T(8,128)S(1)} %row_total.3), channel_id=1, source_target_pairs={{4,100},{12,108},{20,116},{28,124},{96,0},{104,8},{112,16},{120,24... | collective-permute-start | bytes 405512 | tf_op jit(solution)/shard_map/ppermute | solution.py:377
  40.0 8.0 %collective-permute-start.8 = (f32[256,128]{1,0:T(8,128)S(1)}, f32[256,128]{1,0:T(8,128)S(1)}, u32[]{:S(2)}, u32[]{:S(2)}) collective-permute-start(f32[256,128]{1,0:T(8,128)S(1)} %get-tuple-element.52), channel_id=1, source_target_pairs={{0,16},{4,20},{8,24},{12,28},{16,0},{20,4},{24,8},{28,12},{32,48},... | collective-permute-start | bytes 393224 | tf_op jit(solution)/shard_map/ppermute | solution.py:361
  41.5 8.9 %collective-permute-start.9 = (f32[256,128]{1,0:T(8,128)S(1)}, f32[256,128]{1,0:T(8,128)S(1)}, u32[]{:S(2)}, u32[]{:S(2)}) collective-permute-start(f32[256,128]{1,0:T(8,128)S(1)} %get-tuple-element.53), channel_id=1, source_target_pairs={{0,8},{4,12},{8,16},{12,20},{16,24},{20,28},{24,0},{28,4},{32,40},... | collective-permute-start | bytes 393224 | tf_op jit(solution)/shard_map/ppermute | solution.py:361
  42.9 7.7 %collective-permute-start.10 = (f32[256,128]{1,0:T(8,128)S(1)}, f32[256,128]{1,0:T(8,128)S(1)}, u32[]{:S(2)}, u32[]{:S(2)}) collective-permute-start(f32[256,128]{1,0:T(8,128)S(1)} %get-tuple-element.50.refs_0_), channel_id=1, source_target_pairs={{0,4},{4,0},{8,12},{12,8},{16,20},{20,16},{24,28},{28,24},{32,36},... | collective-permute-start | bytes 393224 | tf_op jit(solution)/shard_map/ppermute | solution.py:357
  45.6 8.0 %collective-permute-start.22 = (f32[256,128]{1,0:T(8,128)S(1)}, f32[256,128]{1,0:T(8,128)S(1)}, u32[]{:S(2)}, u32[]{:S(2)}) collective-permute-start(f32[256,128]{1,0:T(8,128)S(1)} %get-tuple-element.65), channel_id=1, source_target_pairs={{0,16},{4,20},{8,24},{12,28},{16,0},{20,4},{24,8},{28,12},{32,48},... | collective-permute-start | bytes 393224 | tf_op jit(solution)/shard_map/ppermute | solution.py:361
  48.0 8.4 %collective-permute-start.23 = (f32[256,128]{1,0:T(8,128)S(1)}, f32[256,128]{1,0:T(8,128)S(1)}, u32[]{:S(2)}, u32[]{:S(2)}) collective-permute-start(f32[256,128]{1,0:T(8,128)S(1)} %get-tuple-element.66), channel_id=1, source_target_pairs={{0,8},{4,12},{8,16},{12,20},{16,24},{20,28},{24,0},{28,4},{32,40},... | collective-permute-start | bytes 393224 | tf_op jit(solution)/shard_map/ppermute | solution.py:361
  50.9 10.3 %collective-permute-start.13 = (f32[256,128]{1,0:T(8,128)S(1)}, f32[256,128]{1,0:T(8,128)S(1)}, u32[]{:S(2)}, u32[]{:S(2)}) collective-permute-start(f32[256,128]{1,0:T(8,128)S(1)} %collective-permute-done.9.refs_3_), channel_id=1, source_target_pairs={{0,4},{4,0},{8,12},{12,8},{16,20},{20,16},{24,28},{28,24},{32,36},... | collective-permute-start | bytes 393224 | tf_op jit(solution)/shard_map/ppermute | solution.py:357
  53.6 10.0 %collective-permute-start.24 = (f32[256,128]{1,0:T(8,128)S(1)}, f32[256,128]{1,0:T(8,128)S(1)}, u32[]{:S(2)}, u32[]{:S(2)}) collective-permute-start(f32[256,128]{1,0:T(8,128)S(1)} %get-tuple-element.63.refs_0_), channel_id=1, source_target_pairs={{0,4},{4,0},{8,12},{12,8},{16,20},{20,16},{24,28},{28,24},{32,36},... | collective-permute-start | bytes 393224 | tf_op jit(solution)/shard_map/ppermute | solution.py:357
  56.3 7.3 %collective-permute-start.25 = (f32[256,128]{1,0:T(8,128)S(1)}, f32[256,128]{1,0:T(8,128)S(1)}, u32[]{:S(2)}, u32[]{:S(2)}) collective-permute-start(f32[256,128]{1,0:T(8,128)S(1)} %collective-permute-done.21.refs_1_), channel_id=1, source_target_pairs={{0,4},{4,0},{8,12},{12,8},{16,20},{20,16},{24,28},{28,24},{32,36},... | collective-permute-start | bytes 393224 | tf_op jit(solution)/shard_map/ppermute | solution.py:357
  56.4 7.3 %collective-permute-start.26 = (f32[256,128]{1,0:T(8,128)S(1)}, f32[256,128]{1,0:T(8,128)S(1)}, u32[]{:S(2)}, u32[]{:S(2)}) collective-permute-start(f32[256,128]{1,0:T(8,128)S(1)} %collective-permute-done.22.refs_2_), channel_id=1, source_target_pairs={{0,4},{4,0},{8,12},{12,8},{16,20},{20,16},{24,28},{28,24},{32,36},... | collective-permute-start | bytes 393224 | tf_op jit(solution)/shard_map/ppermute | solution.py:357
  66.5 17.2 %collective-permute-start.30 = (f32[2,128,128]{2,1,0:T(8,128)S(1)}, f32[2,128,128]{2,1,0:T(8,128)S(1)}, u32[]{:S(2)}, u32[]{:S(2)}) collective-permute-start(f32[2,128,128]{2,1,0:T(8,128)S(1)} %get-tuple-element.70), channel_id=1, source_target_pairs={{0,3},{1,0},{2,1},{3,2},{4,7},{5,4},{6,5},{7,6},{8,11},{9,8},{10,9... | collective-permute-start | bytes 393224 | tf_op jit(solution)/shard_map/ppermute | solution.py:507
  69.3 14.5 %collective-permute-start.29 = (f32[2,128,128]{2,1,0:T(8,128)S(1)}, f32[2,128,128]{2,1,0:T(8,128)S(1)}, u32[]{:S(2)}, u32[]{:S(2)}) collective-permute-start(f32[2,128,128]{2,1,0:T(8,128)S(1)} %get-tuple-element.70), channel_id=1, source_target_pairs={{0,2},{1,3},{2,0},{3,1},{4,6},{5,7},{6,4},{7,5},{8,10},{9,11},{10,... | collective-permute-start | bytes 393224 | tf_op jit(solution)/shard_map/ppermute | solution.py:507
  (25 other events, 99.7 us)

commit v2 on v1

--- a/solution.py
+++ b/solution.py
@@ -22,6 +22,8 @@
 CHUNK_ROWS = CHUNK_PAIRS * TOK
 VMEM = pl.BlockSpec(memory_space=pltpu.VMEM)
 SMEM = pl.BlockSpec(memory_space=pltpu.SMEM)
+ANY = pl.BlockSpec(memory_space=pl.ANY)
+SPACES = (VMEM, SMEM, ANY)
 VMEM_LIMIT = 24 << 20
 
 
@@ -60,8 +62,17 @@
     )
 
 
+def over_lanes(values):
+    pick = iota((PAIRS, HEADS), 1) - 2 * iota((PAIRS, HEADS), 0)
+    return jnp.where(
+        iota((PAIRS, 128), 1) < 64,
+        nn((pick == 0).astype(F32), values, HIGHEST),
+        nn((pick == 1).astype(F32), values, HIGHEST),
+    )
+
+
 def states_kernel(
-    place, doc, xq, scale, dt, bias, alog, b, c, g, x_out, rows_out, cols_out, decay_out, *parts
+    place, doc, xq, scale, dt, bias, alog, b, c, g, x_out, rows_out, cols_out, kappa_out, *parts
 ):
     core = place[0]
     sends, keeps = parts[:PARTS], parts[PARTS:]
@@ -86,14 +97,9 @@
     rows_out[5] = block
     cols = jnp.concatenate([enter, leave * step, total, step], 0).T
     cols_out[...] = cols
+    decay = over_lanes(block)
+    kappa_out[...] = decay * over_lanes(last)
     lanes = iota((TOK, 128), 1) < 64
-    pick = iota((PAIRS, HEADS), 1) - 2 * iota((PAIRS, HEADS), 0)
-    decay = jnp.where(
-        iota((PAIRS, 128), 1) < 64,
-        nn((pick == 0).astype(F32), block, HIGHEST),
-        nn((pick == 1).astype(F32), block, HIGHEST),
-    )
-    decay_out[...] = decay
     factor = (jnp.left_shift(jnp.int32(1), scale[...] + 8).astype(F32) / 256.0).T
     b_t = b[...].astype(F32).T.astype(BF16)
     c_t = c[...].astype(F32).T.astype(BF16)
@@ -153,21 +159,32 @@
 
 
 def orders(place):
-    spots = [(place[1] + k) % CHIPS for k in range(CHIPS)]
-    return [jnp.where(place[0] == 1, s, CHIPS - 1 - s) for s in spots]
+    spots = [(place[1] + k) % 4 for k in range(4)]
+    return [jnp.where(place[0] == 1, s, 3 - s) for s in spots]
+
+
+def product(decays, flags):
+    weight = jnp.ones((8, 128), F32)
+    for decay, flag in zip(decays, flags):
+        weight = jnp.where(flag, weight * decay, weight)
+    return weight
+
+
+def path(order, decays, k, j):
+    others = [m for m in range(4) if m != j and m != k]
+    between = [jnp.logical_and(order[m] > order[k], order[m] < order[j]) for m in others]
+    weight = product([decays[m] for m in others], between)
+    return jnp.where(order[k] < order[j], weight, jnp.zeros((8, 128), F32))
 
 
 def row_kernel(place, *refs):
-    chunks, out = refs[:CHIPS], refs[CHIPS]
+    chunks, out = refs[:CHIPS], refs[-1]
     order = orders(place)
     decays = [chunk[CHUNK_ROWS:, :] for chunk in chunks]
     weights = []
     for k in range(CHIPS):
-        weight = jnp.ones((8, 128), F32)
-        for m in range(CHIPS):
-            if m != k:
-                weight = jnp.where(order[m] > order[k], weight * decays[m], weight)
-        weights.append(weight)
+        others = [m for m in range(CHIPS) if m != k]
+        weights.append(product([decays[m] for m in others], [order[m] > order[k] for m in others]))
     for p in range(CHUNK_PAIRS):
         at = slice(p * TOK, (p + 1) * TOK)
         out[at, :] = sum(weights[k][p : p + 1] * chunks[k][at, :] for k in range(CHIPS))
@@ -175,30 +192,16 @@
 
 
 def entry_kernel(place, *refs):
-    chunks, rows, outs = refs[:CHIPS], refs[CHIPS : 2 * CHIPS - 1], refs[2 * CHIPS - 1 :]
+    chunks, rows, outs = refs[:CHIPS], refs[CHIPS : 2 * CHIPS - 1], refs[2 * CHIPS :]
+    one = rows[0][CHUNK_ROWS:, :]
+    two = one * rows[1][CHUNK_ROWS:, :]
     order = orders(place)
     decays = [chunk[CHUNK_ROWS:, :] for chunk in chunks]
-    one = rows[0][CHUNK_ROWS:, :]
-    two = one * rows[1][CHUNK_ROWS:, :]
-    zero = jnp.zeros((8, 128), F32)
     weights = []
     for j in range(CHIPS):
-        whole = jnp.ones((8, 128), F32)
-        for m in range(CHIPS):
-            if m != j:
-                whole = jnp.where(order[m] < order[j], whole * decays[m], whole)
-        terms = []
-        for k in range(CHIPS):
-            if k == j:
-                terms.append(None)
-                continue
-            weight = jnp.ones((8, 128), F32)
-            for m in range(CHIPS):
-                if m != j and m != k:
-                    between = jnp.logical_and(order[m] > order[k], order[m] < order[j])
-                    weight = jnp.where(between, weight * decays[m], weight)
-            terms.append(jnp.where(order[k] < order[j], weight, zero))
-        weights.append((whole, terms))
+        others = [m for m in range(CHIPS) if m != j]
+        whole = product([decays[m] for m in others], [order[m] < order[j] for m in others])
+        weights.append((whole, {k: path(order, decays, k, j) for k in others}))
     for p in range(CHUNK_PAIRS):
         at = slice(p * TOK, (p + 1) * TOK)
         row = rows[0][at, :] + one[p : p + 1] * rows[1][at, :] + two[p : p + 1] * rows[2][at, :]
@@ -206,10 +209,16 @@
         for j in range(CHIPS):
             whole, terms = weights[j]
             value = whole[p : p + 1] * row
-            for k in range(CHIPS):
-                if k != j:
-                    value = value + terms[k][p : p + 1] * sources[k]
+            for k, weight in terms.items():
+                value = value + weight[p : p + 1] * sources[k]
             outs[j][at, :] = value
+
+
+def assemble_kernel(place, *refs):
+    out = refs[-1]
+    for k in range(CHIPS):
+        first = pl.multiple_of((place[1] + k) % CHIPS * CHUNK_ROWS, CHUNK_ROWS)
+        out[pl.ds(first, CHUNK_ROWS), :] = refs[k][...]
 
 
 def selector(heads):
@@ -222,7 +231,9 @@
     return nt(pick, high) + nt(pick, low)
 
 
-def within_kernel(doc, skip, x, g, b, c, rows, cols, gx_out, sums_out, bc_out, work):
+def within_kernel(
+    doc, skip, x, g, b, c, rows, cols, after, gx_out, sums_out, bc_out, u_out, w_out, heads_out, work
+):
     doc0, doc1 = doc[0, 0], doc[0, 1]
     source, target = iota((TOK, TOK), 0), iota((TOK, TOK), 1)
     seg_s = (source >= doc0).astype(jnp.int32) + (source >= doc1).astype(jnp.int32)
@@ -230,9 +241,18 @@
     mask = jnp.logical_and(target >= source, seg_s == seg_t)
     lanes = iota((TOK, 128), 1) < 64
     kern = nt(b[...], c[...])
-    column_values = cols[...]
+    b_t = b[...].astype(F32).T.astype(BF16)
+    c_t = c[...].astype(F32).T.astype(BF16)
+    b_t = jnp.concatenate([b_t, b_t], 1)
+    c_t = jnp.concatenate([c_t, c_t], 1)
+    columns = cols[...]
+    total, step, enter, leave = (rows[k] for k in (1, 0, 2, 3))
+    last = jnp.broadcast_to(total[:, TOK - 1 :], (HEADS, TOK))
+    timed = jnp.concatenate(
+        [enter * total, leave * step * (last - total), total, total], 0
+    ).T
     kernel_sum = jnp.zeros((TOK, TOK), F32)
-    flows = []
+    flows, skips = [], []
     for j in range(PAIRS):
         at = slice(128 * j, 128 * j + 128)
         x_pair, g_pair = x[:, at], g[:, at]
@@ -243,8 +263,8 @@
         high, low = [], []
         for i in (0, 1):
             h = 2 * j + i
-            total_s = jnp.broadcast_to(column_values[:, 64 + h : 65 + h], (TOK, TOK))
-            step_s = jnp.broadcast_to(column_values[:, 96 + h : 97 + h], (TOK, TOK))
+            total_s = jnp.broadcast_to(columns[:, 64 + h : 65 + h], (TOK, TOK))
+            step_s = jnp.broadcast_to(columns[:, 96 + h : 97 + h], (TOK, TOK))
             total_t = rows[1, h : h + 1, :]
             decay = jnp.exp(jnp.where(mask, total_t - total_s, -1e30))
             score = decay * (step_s * scores[i * TOK : (i + 1) * TOK])
@@ -256,32 +276,57 @@
         inner = nn(jnp.concatenate(high, 1), g_both) + nn(jnp.concatenate(low, 1), g_both)
         x_wide, g_wide = x_pair.astype(F32), g_pair.astype(F32)
         skip_row = jnp.where(iota((1, 128), 1) < 64, skip[2 * j], skip[2 * j + 1])
-        gx_out[:, at] = pair_column(column_values, 96 + 2 * j, lanes) * inner + skip_row * g_wide
-        work[:TOK, at] = x_wide * inner
-        work[TOK:, at] = x_wide * g_wide
-    sums = per_head(work[...], HEADS)
-    sums_out[0] = jnp.concatenate(flows, 0)
-    sums_out[1] = sums[:, :TOK]
-    sums_out[2] = sums[:, TOK:]
+        gx_out[:, at] = pair_column(columns, 96 + 2 * j, lanes) * inner + skip_row * g_wide
+        work[:, at] = x_wide * inner
+        skips.append(jnp.sum(x_wide * g_wide, axis=0, keepdims=True))
+        timed_g = jnp.concatenate(halves(pair_column(timed, 2 * j, lanes) * g_wide), 0)
+        timed_x = jnp.concatenate(halves(pair_column(timed, HEADS + 2 * j, lanes) * x_wide), 0)
+        u_out[at, :] = nn(c_t, timed_g)
+        w_out[at, :] = nn(b_t, timed_x)
+    flow = jnp.concatenate(flows, 0)
+    inner_x = per_head(work[...], HEADS)
+    sums_out[0] = flow
+    sums_out[1] = inner_x
+    alone = jnp.sum((flow - step * inner_x) * total, axis=1, keepdims=True) / 64.0
+    heads_out[:PAIRS, :] = over_lanes(jnp.broadcast_to(alone, (HEADS, TOK)))
+    heads_out[PAIRS:, :] = jnp.concatenate(skips, 0)
     high, low = halves(kernel_sum)
     bc_out[0] = nn(high, c[...]) + nn(low, c[...])
     high, low = halves(kernel_sum.T)
     bc_out[1] = nn(high, b[...]) + nn(low, b[...])
 
 
-def final_kernel(part, place, x, g, b, c, rows, cols, sums, gx, alog, recv, acc, past, *refs):
-    mine, theirs = refs[:CHIPS], refs[CHIPS : 2 * CHIPS]
-    gx_out, dt_out, bc_out, past_out, work, near = refs[2 * CHIPS :]
-    core, spot = place[0], place[1]
+def whole_kernel(
+    part, place, recv, u, w, kappa, heads, mine, theirs, after, entry_out, leave_out, heads_out
+):
+    core = place[0]
+    terms = []
+    for p in range(PART_PAIRS):
+        j = part * PART_PAIRS + p
+        here = slice(128 * p, 128 * p + 128)
+        at = slice(128 * j, 128 * j + 128)
+        full = recv[here, :] + recv[PART_ROWS + p : PART_ROWS + p + 1, :] * mine[here, :]
+        other = theirs[here, :]
+        entry = jnp.where(core == 1, full, other)
+        leave = jnp.where(core == 1, other, full)
+        entry_out[here, :] = entry
+        leave_out[here, :] = leave
+        value = entry * (u[at, :] + kappa[j : j + 1, :] * leave) + w[at, :] * leave
+        terms.append(jnp.sum(value, axis=0, keepdims=True))
+    before = part * PART_PAIRS
+    after = before + PART_PAIRS
+    if before:
+        heads_out[:before, :] = heads[:before, :]
+    heads_out[before:after, :] = heads[before:after, :] + jnp.concatenate(terms, 0)
+    heads_out[after:, :] = heads[after:, :]
+
+
+def final_kernel(part, x, g, b, c, rows, cols, sums, gx, alog, acc, entry_in, leave_in, *refs):
+    gx_out, dt_out, bc_out, work = refs
     heads = 2 * PART_PAIRS
     first_head = part * heads
     lanes = iota((TOK, 128), 1) < 64
     column_values = cols[...]
-    for k in range(CHIPS):
-        target = (spot + k) % CHIPS
-        first = pl.multiple_of(target * CHUNK_ROWS, CHUNK_ROWS)
-        near[0, pl.ds(first, CHUNK_ROWS), :] = mine[k][...]
-        near[1, pl.ds(first, CHUNK_ROWS), :] = theirs[k][...]
     b_two = jnp.concatenate([b[...], b[...]], 1)
     c_two = jnp.concatenate([c[...], c[...]], 1)
     grad_b, grad_c = acc[0], acc[1]
@@ -289,10 +334,7 @@
         j = part * PART_PAIRS + p
         at = slice(128 * j, 128 * j + 128)
         local = slice(128 * p, 128 * p + 128)
-        full = recv[local, :] + recv[PART_ROWS + p : PART_ROWS + p + 1, :] * near[0, local, :]
-        other = near[1, local, :]
-        entry = jnp.where(core == 1, full, other)
-        leave = jnp.where(core == 1, other, full)
+        entry, leave = entry_in[local, :], leave_in[local, :]
         entry_high, entry_low = halves(entry)
         leave_high, leave_low = halves(leave)
         read = nn(c_two, jnp.concatenate([entry_high, entry_low], 0))
@@ -329,15 +371,19 @@
     decay_grad = nn(moves, from_here, HIGHEST) + end
     step_grad = inner_x + leave * back_x - rate * decay_grad
     dt_out[...] = step_grad / (1.0 + jnp.exp(-pre))
-    logs = -rate * decay_grad * step
-    if part < PARTS - 1:
-        past_out[...] = logs if part == 0 else jnp.concatenate([past[...], logs], 0)
-    else:
-        if part:
-            logs = jnp.concatenate([past[...], logs], 0)
-        ones = jnp.ones((8, TOK), F32)
-        past_out[0] = nt(ones, logs, HIGHEST)
-        past_out[1] = nt(ones, sums[2], HIGHEST)
+
+
+def heads_kernel(own, one, two, three, out):
+    total = (own[...] + one[...]) + (two[...] + three[...])
+    lane, head = iota((128, HEADS), 0), iota((128, HEADS), 1)
+    lanes_of = (lane // 64 == head % 2).astype(F32)
+    values = nn(total, lanes_of, HIGHEST)
+    pair, head = iota((PAIRS, HEADS), 0), iota((PAIRS, HEADS), 1)
+    on = pair == head // 2
+    scale = 1.0 / math.sqrt(TOK * 32 * 64)
+    for k in (0, 1):
+        kept = jnp.where(on, values[k * PAIRS : (k + 1) * PAIRS], 0.0)
+        out[k : k + 1, :] = jnp.sum(kept, axis=0, keepdims=True) * scale
 
 
 def seq_pairs(move):
@@ -377,17 +423,19 @@
     return lax.ppermute(value, "seq", seq_pairs(move))
 
 
-def call(kernel, ins, outs, name, flops=0, scratch=(), size=0):
+def call(kernel, ins, outs, name, micros, scratch=(), limit=VMEM_LIMIT):
     shapes = [jax.ShapeDtypeStruct(s, d) for s, d in outs]
     return pl.pallas_call(
         kernel,
         out_shape=shapes,
-        in_specs=[SMEM if smem else VMEM for smem, _ in ins],
+        in_specs=[SPACES[space] for space, _ in ins],
         out_specs=[VMEM] * len(outs),
         scratch_shapes=list(scratch),
         name=name,
-        compiler_params=pltpu.CompilerParams(vmem_limit_bytes=VMEM_LIMIT),
-        cost_estimate=pl.CostEstimate(flops=flops, bytes_accessed=size, transcendentals=0),
+        compiler_params=pltpu.CompilerParams(vmem_limit_bytes=limit),
+        cost_estimate=pl.CostEstimate(
+            flops=1 << 16, bytes_accessed=1 << 12, transcendentals=0
+        ),
     )(*[value for _, value in ins])
 
 
@@ -395,7 +443,7 @@
     x_quant, scale_exp, dt_raw, dt_bias, a_log, skip_weight, b_proj, c_proj, doc_starts, grad_out
 ):
     index = lax.axis_index("seq")
-    place = jnp.stack([index % 2, (index // 2) % CHIPS]).astype(jnp.int32)
+    place = jnp.stack([index % 2, (index // 2) % CHIPS, index // (2 * CHIPS)]).astype(jnp.int32)
     alog_row = a_log.reshape(1, HEADS)
     part_shape = (PART_ROWS + 8 * -(-PART_PAIRS // 8), 128)
     chunk_shape = (CHUNK_ROWS + 8, 128)
@@ -416,10 +464,9 @@
         [((TOK, 2048), BF16), ((6, HEADS, TOK), F32), ((TOK, 128), F32), ((PAIRS, 128), F32)]
         + [(part_shape, F32)] * (2 * PARTS),
         "states",
-        flops=4 * 128 * 256 * 2048,
-        size=4 << 20,
-    )
-    x_vals, rows, cols = made[:3]
+        micros=3.4,
+    )
+    x_vals, rows, cols, kappa = made[:4]
     sends, keeps = made[4 : 4 + PARTS], made[4 + PARTS :]
     recvs = [other_core(s) for s in sends]
     chunks = []
@@ -429,10 +476,31 @@
             [(1, place), (0, keeps[part]), (0, recvs[part])],
             [(chunk_shape, F32)] * CHIPS,
             "chip_total",
-            size=3 << 20,
+            micros=0.6,
         )
         chunks.append([cut[0]] + [along_z(cut[CHIPS - k], -k) for k in range(1, CHIPS)])
-    gx, sums, bc = call(
+    row_totals = []
+    for part in range(PARTS):
+        (row,) = call(
+            row_kernel,
+            [(1, place)] + [(0, v) for v in chunks[part]],
+            [(chunk_shape, F32)],
+            "row_total",
+            micros=0.6,
+        )
+        row_totals.append(row)
+    before = [[onward_y(row, k) for k in range(1, ROWS)] for row in row_totals]
+    pieces = []
+    for part in range(PARTS):
+        out = call(
+            entry_kernel,
+            [(1, place)] + [(0, v) for v in chunks[part] + before[part]] + [(2, rows)],
+            [((CHUNK_ROWS, 128), F32)] * CHIPS,
+            "entries",
+            micros=0.7,
+        )
+        pieces.append([out[0]] + [along_z(out[CHIPS - k], -k) for k in range(1, CHIPS)])
+    gx, sums, bc, u, w, heads = call(
         within_kernel,
         [
             (1, doc_starts),
@@ -443,60 +511,47 @@
             (0, c_proj),
             (0, rows),
             (0, cols),
+            (2, pieces[-1][0]),
         ],
-        [((TOK, 2048), F32), ((3, HEADS, TOK), F32), ((2, TOK, 128), F32)],
+        [((TOK, 2048), F32), ((2, HEADS, TOK), F32), ((2, TOK, 128), F32)]
+        + [((2048, 128), F32)] * 2
+        + [((2 * PAIRS, 128), F32)],
         "within",
-        flops=2 * 32 * 3 * 128**3,
-        scratch=[pltpu.VMEM((2 * TOK, 2048), F32)],
-        size=4 << 20,
-    )
-    mine = []
-    for part in range(PARTS):
-        (row,) = call(
-            row_kernel,
-            [(1, place)] + [(0, v) for v in chunks[part]],
-            [(chunk_shape, F32)],
-            "row_total",
-            size=1 << 20,
-        )
-        before = [onward_y(row, k) for k in range(1, ROWS)]
-        out = call(
-            entry_kernel,
-            [(1, place)] + [(0, v) for v in chunks[part] + before],
-            [((CHUNK_ROWS, 128), F32)] * CHIPS,
-            "entries",
-            size=2 << 20,
-        )
-        mine.append([out[0]] + [along_z(out[CHIPS - k], -k) for k in range(1, CHIPS)])
-    theirs = [[other_core(v) for v in part] for part in mine]
-    past = jnp.zeros((8, 128), F32)
+        micros=4.5,
+        scratch=[pltpu.VMEM((TOK, 2048), F32)],
+    )
     gx_parts, dt_parts = [], []
     for part in range(PARTS):
-        last = part == PARTS - 1
-        done = (part + 1) * 2 * PART_PAIRS
-        gx_part, dt_part, bc, past = call(
+        (mine,) = call(
+            assemble_kernel,
+            [(1, place)] + [(0, v) for v in pieces[part]] + [(2, pieces[-1][0] if part == 0 else sums)],
+            [((PART_ROWS, 128), F32)],
+            "assemble",
+            micros=0.5,
+        )
+        theirs = other_core(mine)
+        entry, leave, heads = call(
+            functools.partial(whole_kernel, part),
+            [(1, place)] + [(0, v) for v in [recvs[part], u, w, kappa, heads, mine, theirs]] + [(2, bc)],
+            [((PART_ROWS, 128), F32)] * 2 + [((2 * PAIRS, 128), F32)],
+            "whole",
+            micros=0.8,
+        )
+        gx_part, dt_part, bc = call(
             functools.partial(final_kernel, part),
-            [(1, place)]
-            + [
+            [
                 (0, v)
-                for v in [x_vals, grad_out, b_proj, c_proj, rows, cols, sums, gx, alog_row]
-                + [recvs[part], bc, past]
-                + mine[part]
-                + theirs[part]
+                for v in [x_vals, grad_out, b_proj, c_proj, rows, cols, sums, gx]
+                + [alog_row, bc, entry, leave]
             ],
             [
                 ((TOK, PART_PAIRS * 128), BF16),
                 ((2 * PART_PAIRS, TOK), F32),
                 ((2, TOK, 128), F32),
-                ((2, 8, HEADS), F32) if last else ((done, TOK), F32),
             ],
             "final",
-            flops=2 * PART_PAIRS * 128**3 * 10,
-            scratch=[
-                pltpu.VMEM((2 * TOK + 8, PART_PAIRS * 128), F32),
-                pltpu.VMEM((2, PART_ROWS, 128), F32),
-            ],
-            size=4 << 20,
+            micros=1.8,
+            scratch=[pltpu.VMEM((2 * TOK + 8, PART_PAIRS * 128), F32)],
         )
         gx_parts.append(gx_part)
         dt_parts.append(dt_part)
@@ -505,11 +560,15 @@
     grad_bc = bc
     for k in range(1, 4):
         grad_bc = grad_bc + lax.ppermute(bc, "head", [(i, (i + k) % 4) for i in range(4)])
-    totals = past
-    totals = totals + other_core(totals)
-    totals = totals + along_z(totals, 1) + along_z(totals, 2) + along_z(totals, 3)
-    totals = totals + along_y(totals, 1) + along_y(totals, 2) + along_y(totals, 3)
-    head_grads = totals[:, 0, :] / math.sqrt(TOK * 32 * 64)
+    heads = heads + other_core(heads)
+    heads = heads + along_z(heads, 1) + along_z(heads, 2) + along_z(heads, 3)
+    (head_grads,) = call(
+        heads_kernel,
+        [(0, heads)] + [(0, along_y(heads, k)) for k in (1, 2, 3)],
+        [((2, HEADS), F32)],
+        "head_grads",
+        micros=0.5,
+    )
     return (grad_x, grad_dt, grad_bc, head_grads)
 
 

time: 87.8 us -> 80.1 us (0.912)
  waiting for transfers between devices: 26.1 us -> 17.3 us
  Pallas kernels: 15.7 us -> 18.2 us
    ppermute x15, waiting for transfers between devices: 15.4 us -> 6.59 us  [along_z(): lax.ppermute(value, 'seq', seq_pairs(lambda y, z, core: (y, (z + distance...]
    pallas_call x10 -> x15, Pallas kernels: 15.7 us -> 18.2 us  [call(): pl.pallas_call(kernel, out_shape=shapes, in_specs=[SPACES[space] for spac...]
    ppermute x3, waiting for transfers between devices: 2.5 us -> 0.01 us  [local(): lax.ppermute(bc, 'head', [(i, (i + k) % 4) for i in range(4)])]
    ppermute x3, waiting for transfers between devices: 2.72 us -> 4.23 us  [along_y(): lax.ppermute(value, 'seq', seq_pairs(lambda y, z, core: ((y + distance) %...]
    ppermute x3, starting transfers between devices: 2.54 us -> 4.01 us  [along_y(): lax.ppermute(value, 'seq', seq_pairs(lambda y, z, core: ((y + distance) %...]
    ppermute x15, starting transfers between devices: 20.4 us -> 19.3 us  [along_z(): lax.ppermute(value, 'seq', seq_pairs(lambda y, z, core: (y, (z + distance...]
    ppermute x11 -> x5, waiting for transfers between devices: 1.44 us -> 2.54 us  [other_core(): lax.ppermute(value, 'seq', seq_pairs(lambda y, z, core: (y, z, 1 - core)))]
    ppermute x11 -> x5, starting transfers between devices: 2.26 us -> 1.52 us  [other_core(): lax.ppermute(value, 'seq', seq_pairs(lambda y, z, core: (y, z, 1 - core)))]
  transfers between devices with their start and end apart: 38 -> 32, of which waited for: 18 -> 14; matrix products, arithmetic and copies ran while one was open for 2% -> 2% of each run, Pallas kernels for 11% -> 18%
where the time goes in v2:
time: 80.1 us; the launch traced here: 79.2 us
  starting transfers between devices  37 us (46%)
  Pallas kernels  18.2 us (23%)
  waiting for transfers between devices  17.3 us (22%)
  local copies, waits for them, and re-layouts  3.45 us (4%)
  other arithmetic  2.22 us (3%)
  between operations  0.93 us (1%)
    ppermute x15, starting transfers between devices, along_z(): lax.ppermute(value, 'seq', seq_pairs(lambda y, z, core: (y, (z + distance...  19.3 us
    pallas_call x15, Pallas kernels, call(): pl.pallas_call(kernel, out_shape=shapes, in_specs=[SPACES[space] for spac...  18.2 us
    ppermute x6, starting transfers between devices, onward_y(): return lax.ppermute(value, 'seq', seq_pairs(move))  7.74 us
    ppermute x15, waiting for transfers between devices, along_z(): lax.ppermute(value, 'seq', seq_pairs(lambda y, z, core: (y, (z + distance...  6.59 us
    ppermute x3, starting transfers between devices, local(): lax.ppermute(bc, 'head', [(i, (i + k) % 4) for i in range(4)])  4.5 us
    ppermute x3, waiting for transfers between devices, along_y(): lax.ppermute(value, 'seq', seq_pairs(lambda y, z, core: ((y + distance) %...  4.23 us
    ppermute x3, starting transfers between devices, along_y(): lax.ppermute(value, 'seq', seq_pairs(lambda y, z, core: ((y + distance) %...  4.01 us
    ppermute x6, waiting for transfers between devices, onward_y(): return lax.ppermute(value, 'seq', seq_pairs(move))  3.95 us
  transfers between devices with their start and end apart: 32, of which 14 were waited for; matrix products, arithmetic and copies ran while one was open for 2% of the time, Pallas kernels for 18%

profile of v2, /device:TPU:0, one launch (start us, length us, event | category | flops | bytes accessed | tf_op | source)
XLA Modules:
  0.0 79.2 jit_solution(16711057723298855598)
XLA Ops:
  3.6 3.0 %states.1 = (bf16[128,2048]{1,0:T(8,128)(2,1)S(1)}, f32[6,32,128]{2,1,0:T(8,128)S(1)}, f32[128,128]{1,0:T(8,128)S(1)}, f32[16,128]{1,0:T(8,128)S(1)}, f32[1032,1...) custom-call(s32[3]{0:T(128)S(1)} %pad_add_fusion.place, ...), custom_call_target="tpu_custom_call" | custom-call | flops 65536 | bytes 4096 | tf_op jit(solution)/shard_map/states/pallas_call | solution.py:428
  7.1 1.4 %collective-permute-done.7.recv = f32[1032,128]{1,0:T(8,128)S(1)} collective-permute-done((f32[1032,128]{1,0:T(8,128)S(1)}, f32[1032,128]{1,0:T(8,128)S(1)}, u32[]{:S(2)}, u32[]{:S(2)}) %collective-permute-start.7) | collective-permute-done | bytes 528416 | tf_op jit(solution)/shard_map/ppermute | solution.py:403
  9.2 4.2 %collective-permute-start.8 = (f32[264,128]{1,0:T(8,128)S(1)}, f32[264,128]{1,0:T(8,128)S(1)}, u32[]{:S(2)}, u32[]{:S(2)}) collective-permute-start(f32[264,128]{1,0:T(8,128)S(1)} %get-tuple-element.66), channel_id=1, source_target_pairs={{0,24},{4,28},{8,0},{12,4},{16,8},{20,12},{24,16},{28,20},{32,56},... | collective-permute-start | bytes 405512 | tf_op jit(solution)/shard_map/ppermute | solution.py:407
  13.3 1.3 %collective-permute-start.10 = (f32[264,128]{1,0:T(8,128)S(1)}, f32[264,128]{1,0:T(8,128)S(1)}, u32[]{:S(2)}, u32[]{:S(2)}) collective-permute-start(f32[264,128]{1,0:T(8,128)S(1)} %get-tuple-element.68), channel_id=1, source_target_pairs={{0,8},{4,12},{8,16},{12,20},{16,24},{20,28},{24,0},{28,4},{32,40},... | collective-permute-start | bytes 405512 | tf_op jit(solution)/shard_map/ppermute | solution.py:407
  15.2 2.0 %collective-permute-start.1 = (f32[264,128]{1,0:T(8,128)S(1)}, f32[264,128]{1,0:T(8,128)S(1)}, u32[]{:S(2)}, u32[]{:S(2)}) collective-permute-start(f32[264,128]{1,0:T(8,128)S(1)} %get-tuple-element.52), channel_id=1, source_target_pairs={{0,24},{4,28},{8,0},{12,4},{16,8},{20,12},{24,16},{28,20},{32,56},... | collective-permute-start | bytes 405512 | tf_op jit(solution)/shard_map/ppermute | solution.py:407
  17.3 2.3 %collective-permute-start.2 = (f32[264,128]{1,0:T(8,128)S(1)}, f32[264,128]{1,0:T(8,128)S(1)}, u32[]{:S(2)}, u32[]{:S(2)}) collective-permute-start(f32[264,128]{1,0:T(8,128)S(1)} %get-tuple-element.53), channel_id=1, source_target_pairs={{0,16},{4,20},{8,24},{12,28},{16,0},{20,4},{24,8},{28,12},{32,48},... | collective-permute-start | bytes 405512 | tf_op jit(solution)/shard_map/ppermute | solution.py:407
  21.3 2.2 %collective-permute-done.10.refs_3_ = f32[264,128]{1,0:T(8,128)S(1)} collective-permute-done((f32[264,128]{1,0:T(8,128)S(1)}, f32[264,128]{1,0:T(8,128)S(1)}, u32[]{:S(2)}, u32[]{:S(2)}) %collective-permute-start.10) | collective-permute-done | bytes 135200 | tf_op jit(solution)/shard_map/ppermute | solution.py:407
  24.2 1.3 %collective-permute-start.13 = (f32[264,128]{1,0:T(8,128)S(1)}, f32[264,128]{1,0:T(8,128)S(1)}, u32[]{:S(2)}, u32[]{:S(2)}) collective-permute-start(f32[264,128]{1,0:T(8,128)S(1)} %row_total.3), channel_id=1, source_target_pairs={{4,100},{12,108},{20,116},{28,124},{96,0},{104,8},{112,16},{120,24... | collective-permute-start | bytes 405512 | tf_op jit(solution)/shard_map/ppermute | solution.py:423
  25.5 1.3 %collective-permute-start.12 = (f32[264,128]{1,0:T(8,128)S(1)}, f32[264,128]{1,0:T(8,128)S(1)}, u32[]{:S(2)}, u32[]{:S(2)}) collective-permute-start(f32[264,128]{1,0:T(8,128)S(1)} %row_total.3), channel_id=1, source_target_pairs={{4,68},{12,76},{20,84},{28,92},{36,100},{44,108},{52,116},{60,124}... | collective-permute-start | bytes 405512 | tf_op jit(solution)/shard_map/ppermute | solution.py:423
  26.8 1.3 %collective-permute-start.11 = (f32[264,128]{1,0:T(8,128)S(1)}, f32[264,128]{1,0:T(8,128)S(1)}, u32[]{:S(2)}, u32[]{:S(2)}) collective-permute-start(f32[264,128]{1,0:T(8,128)S(1)} %row_total.3), channel_id=1, source_target_pairs={{4,36},{12,44},{20,52},{28,60},{32,0},{36,68},{40,8},{44,76},{48,1... | collective-permute-start | bytes 405512 | tf_op jit(solution)/shard_map/ppermute | solution.py:423
  29.2 1.3 %collective-permute-start.6 = (f32[264,128]{1,0:T(8,128)S(1)}, f32[264,128]{1,0:T(8,128)S(1)}, u32[]{:S(2)}, u32[]{:S(2)}) collective-permute-start(f32[264,128]{1,0:T(8,128)S(1)} %row_total.2), channel_id=1, source_target_pairs={{4,100},{12,108},{20,116},{28,124},{96,0},{104,8},{112,16},{120,24... | collective-permute-start | bytes 405512 | tf_op jit(solution)/shard_map/ppermute | solution.py:423
  30.5 1.3 %collective-permute-start.5 = (f32[264,128]{1,0:T(8,128)S(1)}, f32[264,128]{1,0:T(8,128)S(1)}, u32[]{:S(2)}, u32[]{:S(2)}) collective-permute-start(f32[264,128]{1,0:T(8,128)S(1)} %row_total.2), channel_id=1, source_target_pairs={{4,68},{12,76},{20,84},{28,92},{36,100},{44,108},{52,116},{60,124}... | collective-permute-start | bytes 405512 | tf_op jit(solution)/shard_map/ppermute | solution.py:423
  32.3 1.3 %collective-permute-start.4 = (f32[264,128]{1,0:T(8,128)S(1)}, f32[264,128]{1,0:T(8,128)S(1)}, u32[]{:S(2)}, u32[]{:S(2)}) collective-permute-start(f32[264,128]{1,0:T(8,128)S(1)} %row_total.2), channel_id=1, source_target_pairs={{4,36},{12,44},{20,52},{28,60},{32,0},{36,68},{40,8},{44,76},{48,1... | collective-permute-start | bytes 405512 | tf_op jit(solution)/shard_map/ppermute | solution.py:423
  33.6 1.2 %collective-permute-done.12.refs_5_ = f32[264,128]{1,0:T(8,128)S(1)} collective-permute-done((f32[264,128]{1,0:T(8,128)S(1)}, f32[264,128]{1,0:T(8,128)S(1)}, u32[]{:S(2)}, u32[]{:S(2)}) %collective-permute-start.12) | collective-permute-done | bytes 135200 | tf_op jit(solution)/shard_map/ppermute | solution.py:423
  37.8 1.7 %collective-permute-done.6.refs_6_ = f32[264,128]{1,0:T(8,128)S(1)} collective-permute-done((f32[264,128]{1,0:T(8,128)S(1)}, f32[264,128]{1,0:T(8,128)S(1)}, u32[]{:S(2)}, u32[]{:S(2)}) %collective-permute-start.6) | collective-permute-done | bytes 135200 | tf_op jit(solution)/shard_map/ppermute | solution.py:423
  40.8 2.8 %collective-permute-start.18 = (f32[256,128]{1,0:T(8,128)S(1)}, f32[256,128]{1,0:T(8,128)S(1)}, u32[]{:S(2)}, u32[]{:S(2)}) collective-permute-start(f32[256,128]{1,0:T(8,128)S(1)} %get-tuple-element.78), channel_id=1, source_target_pairs={{0,24},{4,28},{8,0},{12,4},{16,8},{20,12},{24,16},{28,20},{32,56},... | collective-permute-start | bytes 393224 | tf_op jit(solution)/shard_map/ppermute | solution.py:407
  43.5 1.7 %collective-permute-start.19 = (f32[256,128]{1,0:T(8,128)S(1)}, f32[256,128]{1,0:T(8,128)S(1)}, u32[]{:S(2)}, u32[]{:S(2)}) collective-permute-start(f32[256,128]{1,0:T(8,128)S(1)} %get-tuple-element.79), channel_id=1, source_target_pairs={{0,16},{4,20},{8,24},{12,28},{16,0},{20,4},{24,8},{28,12},{32,48},... | collective-permute-start | bytes 393224 | tf_op jit(solution)/shard_map/ppermute | solution.py:407
  45.3 2.1 %collective-permute-done.16.refs_3_ = f32[256,128]{1,0:T(8,128)S(1)} collective-permute-done((f32[256,128]{1,0:T(8,128)S(1)}, f32[256,128]{1,0:T(8,128)S(1)}, u32[]{:S(2)}, u32[]{:S(2)}) %collective-permute-start.16) | collective-permute-done | bytes 131104 | tf_op jit(solution)/shard_map/ppermute | solution.py:407
  48.7 4.5 %within.1 = (f32[128,2048]{1,0:T(8,128)S(1)}, f32[2,32,128]{2,1,0:T(8,128)S(1)}, f32[2,128,128]{2,1,0:T(8,128)S(1)}, f32[2048,128]{1,0:T(8,128)S(1)}, f32[2048,128]{1,0:T(8,128)S(1)}, /*index=5*/f32[32,128]{1,0:T(8,128)S(1)}) custom-call(s32[1,2]{1,0:T(1,128)S(1)} %copy-done.8, f32[32]{0:T(128)S(1)} %copy-done.10, ...), custom_call_target="tpu_custom_call" | custom-call | flops 65536 | bytes 4096 | tf_op jit(solution)/shard_map/within/pallas_call | solution.py:428
  55.3 1.7 %final.2 = (bf16[128,1024]{1,0:T(8,128)(2,1)S(1)}, f32[16,128]{1,0:T(8,128)S(1)}, f32[2,128,128]{2,1,0:T(8,128)S(1)}) custom-call(bf16[128,2048]{1,0:T(8,128)(2,1)S(1)} %get-tuple-element.46.x, bf16[128,2048]{1,0:T(8,128)(2,1)S(1)} %copy-done.1, bf16[128,128]{1,0:T(8,128)(2,1)S(1)} %copy-done.3, bf16[128,128]{1,0:T(8,128)(2,1)S(1)} %copy-done.4, ...), custom_call_target="tpu_custom_call" | custom-call | flops 65536 | bytes 4096 | tf_op jit(solution)/shard_map/final/pallas_call | solution.py:428
  61.9 1.7 %final.3 = (bf16[128,1024]{1,0:T(8,128)(2,1)S(1)}, f32[16,128]{1,0:T(8,128)S(1)}, f32[2,128,128]{2,1,0:T(8,128)S(1)}) custom-call(bf16[128,2048]{1,0:T(8,128)(2,1)S(1)} %get-tuple-element.46.x, bf16[128,2048]{1,0:T(8,128)(2,1)S(1)} %copy-done.1, bf16[128,128]{1,0:T(8,128)(2,1)S(1)} %copy-done.3, bf16[128,128]{1,0:T(8,128)(2,1)S(1)} %copy-done.4, ...), custom_call_target="tpu_custom_call" | custom-call | flops 65536 | bytes 4096 | tf_op jit(solution)/shard_map/final/pallas_call | solution.py:428
  63.5 2.8 %collective-permute-start.24 = (f32[2,128,128]{2,1,0:T(8,128)S(1)}, f32[2,128,128]{2,1,0:T(8,128)S(1)}, u32[]{:S(2)}, u32[]{:S(2)}) collective-permute-start(f32[2,128,128]{2,1,0:T(8,128)S(1)} %get-tuple-element.86), channel_id=1, source_target_pairs={{0,3},{1,0},{2,1},{3,2},{4,7},{5,4},{6,5},{7,6},{8,11},{9,8},{10,9... | collective-permute-start | bytes 393224 | tf_op jit(solution)/shard_map/ppermute | solution.py:562
  68.0 3.0 %collective-permute-start.31 = (f32[32,128]{1,0:T(8,128)S(1)}, f32[32,128]{1,0:T(8,128)S(1)}, u32[]{:S(2)}, u32[]{:S(2)}) collective-permute-start(f32[32,128]{1,0:T(8,128)S(1)} %add_add_fusion.1.own), channel_id=1, source_target_pairs={{0,96},{4,100},{8,104},{12,108},{16,112},{20,116},{24,120},{28,124... | collective-permute-start | bytes 49160 | tf_op jit(solution)/shard_map/ppermute | solution.py:413
  73.7 3.4 %collective-permute-done.30.two = f32[32,128]{1,0:T(8,128)S(1)} collective-permute-done((f32[32,128]{1,0:T(8,128)S(1)}, f32[32,128]{1,0:T(8,128)S(1)}, u32[]{:S(2)}, u32[]{:S(2)}) %collective-permute-start.30) | collective-permute-done | bytes 16416 | tf_op jit(solution)/shard_map/ppermute | solution.py:413
  (83 shorter events, 27.5 us)
Async XLA Ops:
  6.6 8.0 %collective-permute-start = (f32[1032,128]{1,0:T(8,128)S(1)}, f32[1032,128]{1,0:T(8,128)S(1)}, u32[]{:S(2)}, u32[]{:S(2)}) collective-permute-start(f32[1032,128]{1,0:T(8,128)S(1)} %get-tuple-element.50), channel_id=1, source_target_pairs={{0,4},{4,0},{8,12},{12,8},{16,20},{20,16},{24,28},{28,24},{32,36},... | collective-permute-start | bytes 1585160 | tf_op jit(solution)/shard_map/ppermute | solution.py:403
  9.2 11.4 %collective-permute-start.8 = (f32[264,128]{1,0:T(8,128)S(1)}, f32[264,128]{1,0:T(8,128)S(1)}, u32[]{:S(2)}, u32[]{:S(2)}) collective-permute-start(f32[264,128]{1,0:T(8,128)S(1)} %get-tuple-element.66), channel_id=1, source_target_pairs={{0,24},{4,28},{8,0},{12,4},{16,8},{20,12},{24,16},{28,20},{32,56},... | collective-permute-start | bytes 405512 | tf_op jit(solution)/shard_map/ppermute | solution.py:407
  13.3 8.0 %collective-permute-start.9 = (f32[264,128]{1,0:T(8,128)S(1)}, f32[264,128]{1,0:T(8,128)S(1)}, u32[]{:S(2)}, u32[]{:S(2)}) collective-permute-start(f32[264,128]{1,0:T(8,128)S(1)} %get-tuple-element.67), channel_id=1, source_target_pairs={{0,16},{4,20},{8,24},{12,28},{16,0},{20,4},{24,8},{28,12},{32,48},... | collective-permute-start | bytes 405512 | tf_op jit(solution)/shard_map/ppermute | solution.py:407
  13.3 10.2 %collective-permute-start.10 = (f32[264,128]{1,0:T(8,128)S(1)}, f32[264,128]{1,0:T(8,128)S(1)}, u32[]{:S(2)}, u32[]{:S(2)}) collective-permute-start(f32[264,128]{1,0:T(8,128)S(1)} %get-tuple-element.68), channel_id=1, source_target_pairs={{0,8},{4,12},{8,16},{12,20},{16,24},{20,28},{24,0},{28,4},{32,40},... | collective-permute-start | bytes 405512 | tf_op jit(solution)/shard_map/ppermute | solution.py:407
  15.2 11.5 %collective-permute-start.1 = (f32[264,128]{1,0:T(8,128)S(1)}, f32[264,128]{1,0:T(8,128)S(1)}, u32[]{:S(2)}, u32[]{:S(2)}) collective-permute-start(f32[264,128]{1,0:T(8,128)S(1)} %get-tuple-element.52), channel_id=1, source_target_pairs={{0,24},{4,28},{8,0},{12,4},{16,8},{20,12},{24,16},{28,20},{32,56},... | collective-permute-start | bytes 405512 | tf_op jit(solution)/shard_map/ppermute | solution.py:407
  17.3 10.8 %collective-permute-start.2 = (f32[264,128]{1,0:T(8,128)S(1)}, f32[264,128]{1,0:T(8,128)S(1)}, u32[]{:S(2)}, u32[]{:S(2)}) collective-permute-start(f32[264,128]{1,0:T(8,128)S(1)} %get-tuple-element.53), channel_id=1, source_target_pairs={{0,16},{4,20},{8,24},{12,28},{16,0},{20,4},{24,8},{28,12},{32,48},... | collective-permute-start | bytes 405512 | tf_op jit(solution)/shard_map/ppermute | solution.py:407
  20.6 8.0 %collective-permute-start.3 = (f32[264,128]{1,0:T(8,128)S(1)}, f32[264,128]{1,0:T(8,128)S(1)}, u32[]{:S(2)}, u32[]{:S(2)}) collective-permute-start(f32[264,128]{1,0:T(8,128)S(1)} %get-tuple-element.54), channel_id=1, source_target_pairs={{0,8},{4,12},{8,16},{12,20},{16,24},{20,28},{24,0},{28,4},{32,40},... | collective-permute-start | bytes 405512 | tf_op jit(solution)/shard_map/ppermute | solution.py:407
  24.2 8.1 %collective-permute-start.13 = (f32[264,128]{1,0:T(8,128)S(1)}, f32[264,128]{1,0:T(8,128)S(1)}, u32[]{:S(2)}, u32[]{:S(2)}) collective-permute-start(f32[264,128]{1,0:T(8,128)S(1)} %row_total.3), channel_id=1, source_target_pairs={{4,100},{12,108},{20,116},{28,124},{96,0},{104,8},{112,16},{120,24... | collective-permute-start | bytes 405512 | tf_op jit(solution)/shard_map/ppermute | solution.py:423
  25.5 9.3 %collective-permute-start.12 = (f32[264,128]{1,0:T(8,128)S(1)}, f32[264,128]{1,0:T(8,128)S(1)}, u32[]{:S(2)}, u32[]{:S(2)}) collective-permute-start(f32[264,128]{1,0:T(8,128)S(1)} %row_total.3), channel_id=1, source_target_pairs={{4,68},{12,76},{20,84},{28,92},{36,100},{44,108},{52,116},{60,124}... | collective-permute-start | bytes 405512 | tf_op jit(solution)/shard_map/ppermute | solution.py:423
  26.8 8.0 %collective-permute-start.11 = (f32[264,128]{1,0:T(8,128)S(1)}, f32[264,128]{1,0:T(8,128)S(1)}, u32[]{:S(2)}, u32[]{:S(2)}) collective-permute-start(f32[264,128]{1,0:T(8,128)S(1)} %row_total.3), channel_id=1, source_target_pairs={{4,36},{12,44},{20,52},{28,60},{32,0},{36,68},{40,8},{44,76},{48,1... | collective-permute-start | bytes 405512 | tf_op jit(solution)/shard_map/ppermute | solution.py:423
  29.2 10.3 %collective-permute-start.6 = (f32[264,128]{1,0:T(8,128)S(1)}, f32[264,128]{1,0:T(8,128)S(1)}, u32[]{:S(2)}, u32[]{:S(2)}) collective-permute-start(f32[264,128]{1,0:T(8,128)S(1)} %row_total.2), channel_id=1, source_target_pairs={{4,100},{12,108},{20,116},{28,124},{96,0},{104,8},{112,16},{120,24... | collective-permute-start | bytes 405512 | tf_op jit(solution)/shard_map/ppermute | solution.py:423
  30.5 9.5 %collective-permute-start.5 = (f32[264,128]{1,0:T(8,128)S(1)}, f32[264,128]{1,0:T(8,128)S(1)}, u32[]{:S(2)}, u32[]{:S(2)}) collective-permute-start(f32[264,128]{1,0:T(8,128)S(1)} %row_total.2), channel_id=1, source_target_pairs={{4,68},{12,76},{20,84},{28,92},{36,100},{44,108},{52,116},{60,124}... | collective-permute-start | bytes 405512 | tf_op jit(solution)/shard_map/ppermute | solution.py:423
  32.3 7.7 %collective-permute-start.4 = (f32[264,128]{1,0:T(8,128)S(1)}, f32[264,128]{1,0:T(8,128)S(1)}, u32[]{:S(2)}, u32[]{:S(2)}) collective-permute-start(f32[264,128]{1,0:T(8,128)S(1)} %row_total.2), channel_id=1, source_target_pairs={{4,36},{12,44},{20,52},{28,60},{32,0},{36,68},{40,8},{44,76},{48,1... | collective-permute-start | bytes 405512 | tf_op jit(solution)/shard_map/ppermute | solution.py:423
  35.5 9.7 %collective-permute-start.14 = (f32[256,128]{1,0:T(8,128)S(1)}, f32[256,128]{1,0:T(8,128)S(1)}, u32[]{:S(2)}, u32[]{:S(2)}) collective-permute-start(f32[256,128]{1,0:T(8,128)S(1)} %get-tuple-element.70), channel_id=1, source_target_pairs={{0,24},{4,28},{8,0},{12,4},{16,8},{20,12},{24,16},{28,20},{32,56},... | collective-permute-start | bytes 393224 | tf_op jit(solution)/shard_map/ppermute | solution.py:407
  36.6 8.7 %collective-permute-start.15 = (f32[256,128]{1,0:T(8,128)S(1)}, f32[256,128]{1,0:T(8,128)S(1)}, u32[]{:S(2)}, u32[]{:S(2)}) collective-permute-start(f32[256,128]{1,0:T(8,128)S(1)} %get-tuple-element.71), channel_id=1, source_target_pairs={{0,16},{4,20},{8,24},{12,28},{16,0},{20,4},{24,8},{28,12},{32,48},... | collective-permute-start | bytes 393224 | tf_op jit(solution)/shard_map/ppermute | solution.py:407
  39.5 7.9 %collective-permute-start.16 = (f32[256,128]{1,0:T(8,128)S(1)}, f32[256,128]{1,0:T(8,128)S(1)}, u32[]{:S(2)}, u32[]{:S(2)}) collective-permute-start(f32[256,128]{1,0:T(8,128)S(1)} %get-tuple-element.72), channel_id=1, source_target_pairs={{0,8},{4,12},{8,16},{12,20},{16,24},{20,28},{24,0},{28,4},{32,40},... | collective-permute-start | bytes 393224 | tf_op jit(solution)/shard_map/ppermute | solution.py:407
  40.8 12.5 %collective-permute-start.18 = (f32[256,128]{1,0:T(8,128)S(1)}, f32[256,128]{1,0:T(8,128)S(1)}, u32[]{:S(2)}, u32[]{:S(2)}) collective-permute-start(f32[256,128]{1,0:T(8,128)S(1)} %get-tuple-element.78), channel_id=1, source_target_pairs={{0,24},{4,28},{8,0},{12,4},{16,8},{20,12},{24,16},{28,20},{32,56},... | collective-permute-start | bytes 393224 | tf_op jit(solution)/shard_map/ppermute | solution.py:407
  43.5 9.7 %collective-permute-start.19 = (f32[256,128]{1,0:T(8,128)S(1)}, f32[256,128]{1,0:T(8,128)S(1)}, u32[]{:S(2)}, u32[]{:S(2)}) collective-permute-start(f32[256,128]{1,0:T(8,128)S(1)} %get-tuple-element.79), channel_id=1, source_target_pairs={{0,16},{4,20},{8,24},{12,28},{16,0},{20,4},{24,8},{28,12},{32,48},... | collective-permute-start | bytes 393224 | tf_op jit(solution)/shard_map/ppermute | solution.py:407
  45.2 8.0 %collective-permute-start.20 = (f32[256,128]{1,0:T(8,128)S(1)}, f32[256,128]{1,0:T(8,128)S(1)}, u32[]{:S(2)}, u32[]{:S(2)}) collective-permute-start(f32[256,128]{1,0:T(8,128)S(1)} %get-tuple-element.80), channel_id=1, source_target_pairs={{0,8},{4,12},{8,16},{12,20},{16,24},{20,28},{24,0},{28,4},{32,40},... | collective-permute-start | bytes 393224 | tf_op jit(solution)/shard_map/ppermute | solution.py:407
  59.1 8.0 %collective-permute-start.28 = (f32[32,128]{1,0:T(8,128)S(1)}, f32[32,128]{1,0:T(8,128)S(1)}, u32[]{:S(2)}, u32[]{:S(2)}) collective-permute-start(f32[32,128]{1,0:T(8,128)S(1)} %add.35), channel_id=1, source_target_pairs={{0,24},{4,28},{8,0},{12,4},{16,8},{20,12},{24,16},{28,20},{32,56},... | collective-permute-start | bytes 49160 | tf_op jit(solution)/shard_map/ppermute | solution.py:407
  60.3 7.8 %collective-permute-start.27 = (f32[32,128]{1,0:T(8,128)S(1)}, f32[32,128]{1,0:T(8,128)S(1)}, u32[]{:S(2)}, u32[]{:S(2)}) collective-permute-start(f32[32,128]{1,0:T(8,128)S(1)} %add.35), channel_id=1, source_target_pairs={{0,16},{4,20},{8,24},{12,28},{16,0},{20,4},{24,8},{28,12},{32,48},... | collective-permute-start | bytes 49160 | tf_op jit(solution)/shard_map/ppermute | solution.py:407
  63.5 14.9 %collective-permute-start.24 = (f32[2,128,128]{2,1,0:T(8,128)S(1)}, f32[2,128,128]{2,1,0:T(8,128)S(1)}, u32[]{:S(2)}, u32[]{:S(2)}) collective-permute-start(f32[2,128,128]{2,1,0:T(8,128)S(1)} %get-tuple-element.86), channel_id=1, source_target_pairs={{0,3},{1,0},{2,1},{3,2},{4,7},{5,4},{6,5},{7,6},{8,11},{9,8},{10,9... | collective-permute-start | bytes 393224 | tf_op jit(solution)/shard_map/ppermute | solution.py:562
  66.3 12.1 %collective-permute-start.23 = (f32[2,128,128]{2,1,0:T(8,128)S(1)}, f32[2,128,128]{2,1,0:T(8,128)S(1)}, u32[]{:S(2)}, u32[]{:S(2)}) collective-permute-start(f32[2,128,128]{2,1,0:T(8,128)S(1)} %get-tuple-element.86), channel_id=1, source_target_pairs={{0,2},{1,3},{2,0},{3,1},{4,6},{5,7},{6,4},{7,5},{8,10},{9,11},{10,... | collective-permute-start | bytes 393224 | tf_op jit(solution)/shard_map/ppermute | solution.py:562
  67.1 11.3 %collective-permute-start.22 = (f32[2,128,128]{2,1,0:T(8,128)S(1)}, f32[2,128,128]{2,1,0:T(8,128)S(1)}, u32[]{:S(2)}, u32[]{:S(2)}) collective-permute-start(f32[2,128,128]{2,1,0:T(8,128)S(1)} %get-tuple-element.86), channel_id=1, source_target_pairs={{0,1},{1,2},{2,3},{3,0},{4,5},{5,6},{6,7},{7,4},{8,9},{9,10},{10,1... | collective-permute-start | bytes 393224 | tf_op jit(solution)/shard_map/ppermute | solution.py:562
  (19 other events, 43.9 us)

commit v3 on v2

--- a/solution.py
+++ b/solution.py
@@ -22,9 +22,14 @@
 CHUNK_ROWS = CHUNK_PAIRS * TOK
 VMEM = pl.BlockSpec(memory_space=pltpu.VMEM)
 SMEM = pl.BlockSpec(memory_space=pltpu.SMEM)
+ORDER_ROW = (3, 1, 2, 0)
+ORDER_ENTRY = (3, 0, 1, 2)
+ORDER_ASSEMBLE = (1, 0, 2, 3)
+ORDER_Y = (0, 2, 1)
 ANY = pl.BlockSpec(memory_space=pl.ANY)
 SPACES = (VMEM, SMEM, ANY)
 VMEM_LIMIT = 24 << 20
+COST = pl.CostEstimate(flops=1 << 16, bytes_accessed=1 << 12, transcendentals=0)
 
 
 def nn(a, b, precision=None):
@@ -63,9 +68,10 @@
 
 
 def over_lanes(values):
-    pick = iota((PAIRS, HEADS), 1) - 2 * iota((PAIRS, HEADS), 0)
+    heads = values.shape[0]
+    pick = iota((heads // 2, heads), 1) - 2 * iota((heads // 2, heads), 0)
     return jnp.where(
-        iota((PAIRS, 128), 1) < 64,
+        iota((heads // 2, 128), 1) < 64,
         nn((pick == 0).astype(F32), values, HIGHEST),
         nn((pick == 1).astype(F32), values, HIGHEST),
     )
@@ -178,7 +184,7 @@
 
 
 def row_kernel(place, *refs):
-    chunks, out = refs[:CHIPS], refs[-1]
+    chunks, out = [refs[ORDER_ROW.index(k)] for k in range(CHIPS)], refs[-1]
     order = orders(place)
     decays = [chunk[CHUNK_ROWS:, :] for chunk in chunks]
     weights = []
@@ -192,7 +198,9 @@
 
 
 def entry_kernel(place, *refs):
-    chunks, rows, outs = refs[:CHIPS], refs[CHIPS : 2 * CHIPS - 1], refs[2 * CHIPS :]
+    rows = [refs[ORDER_Y.index(k)] for k in range(ROWS - 1)]
+    chunks = [refs[ROWS - 1 + ORDER_ENTRY.index(k)] for k in range(CHIPS)]
+    outs = refs[2 * CHIPS :]
     one = rows[0][CHUNK_ROWS:, :]
     two = one * rows[1][CHUNK_ROWS:, :]
     order = orders(place)
@@ -218,7 +226,7 @@
     out = refs[-1]
     for k in range(CHIPS):
         first = pl.multiple_of((place[1] + k) % CHIPS * CHUNK_ROWS, CHUNK_ROWS)
-        out[pl.ds(first, CHUNK_ROWS), :] = refs[k][...]
+        out[pl.ds(first, CHUNK_ROWS), :] = refs[ORDER_ASSEMBLE.index(k)][...]
 
 
 def selector(heads):
@@ -231,9 +239,10 @@
     return nt(pick, high) + nt(pick, low)
 
 
-def within_kernel(
-    doc, skip, x, g, b, c, rows, cols, after, gx_out, sums_out, bc_out, u_out, w_out, heads_out, work
-):
+def within_kernel(part, doc, skip, x, g, b, c, rows, cols, *refs):
+    gx_out, sums_out, bc_out, u_out, w_out, heads_out, work = refs[-7:]
+    heads = 2 * PART_PAIRS
+    here = slice(part * heads, (part + 1) * heads)
     doc0, doc1 = doc[0, 0], doc[0, 1]
     source, target = iota((TOK, TOK), 0), iota((TOK, TOK), 1)
     seg_s = (source >= doc0).astype(jnp.int32) + (source >= doc1).astype(jnp.int32)
@@ -246,15 +255,16 @@
     b_t = jnp.concatenate([b_t, b_t], 1)
     c_t = jnp.concatenate([c_t, c_t], 1)
     columns = cols[...]
-    total, step, enter, leave = (rows[k] for k in (1, 0, 2, 3))
-    last = jnp.broadcast_to(total[:, TOK - 1 :], (HEADS, TOK))
-    timed = jnp.concatenate(
-        [enter * total, leave * step * (last - total), total, total], 0
-    ).T
+    total, step, enter, leave = (rows[k, here, :] for k in (1, 0, 2, 3))
+    last = jnp.broadcast_to(total[:, TOK - 1 :], (heads, TOK))
+    timed = jnp.concatenate([enter * total, leave * step * (last - total)], 0)
+    timed = jnp.concatenate([timed] * (64 // heads), 0).T
     kernel_sum = jnp.zeros((TOK, TOK), F32)
     flows, skips = [], []
-    for j in range(PAIRS):
+    for p in range(PART_PAIRS):
+        j = part * PART_PAIRS + p
         at = slice(128 * j, 128 * j + 128)
+        local = slice(128 * p, 128 * p + 128)
         x_pair, g_pair = x[:, at], g[:, at]
         zero = jnp.zeros_like(x_pair)
         x_both = jnp.concatenate([jnp.where(lanes, x_pair, zero), jnp.where(lanes, zero, x_pair)], 0)
@@ -276,91 +286,103 @@
         inner = nn(jnp.concatenate(high, 1), g_both) + nn(jnp.concatenate(low, 1), g_both)
         x_wide, g_wide = x_pair.astype(F32), g_pair.astype(F32)
         skip_row = jnp.where(iota((1, 128), 1) < 64, skip[2 * j], skip[2 * j + 1])
-        gx_out[:, at] = pair_column(columns, 96 + 2 * j, lanes) * inner + skip_row * g_wide
-        work[:, at] = x_wide * inner
+        gx_out[:, local] = pair_column(columns, 96 + 2 * j, lanes) * inner + skip_row * g_wide
+        work[:, local] = x_wide * inner
         skips.append(jnp.sum(x_wide * g_wide, axis=0, keepdims=True))
-        timed_g = jnp.concatenate(halves(pair_column(timed, 2 * j, lanes) * g_wide), 0)
-        timed_x = jnp.concatenate(halves(pair_column(timed, HEADS + 2 * j, lanes) * x_wide), 0)
-        u_out[at, :] = nn(c_t, timed_g)
-        w_out[at, :] = nn(b_t, timed_x)
+        timed_g = jnp.concatenate(halves(pair_column(timed, 2 * p, lanes) * g_wide), 0)
+        timed_x = jnp.concatenate(halves(pair_column(timed, heads + 2 * p, lanes) * x_wide), 0)
+        u_out[local, :] = nn(c_t, timed_g)
+        w_out[local, :] = nn(b_t, timed_x)
     flow = jnp.concatenate(flows, 0)
-    inner_x = per_head(work[...], HEADS)
+    inner_x = per_head(work[...], heads)
     sums_out[0] = flow
     sums_out[1] = inner_x
     alone = jnp.sum((flow - step * inner_x) * total, axis=1, keepdims=True) / 64.0
-    heads_out[:PAIRS, :] = over_lanes(jnp.broadcast_to(alone, (HEADS, TOK)))
-    heads_out[PAIRS:, :] = jnp.concatenate(skips, 0)
+    heads_out[:PART_PAIRS, :] = over_lanes(jnp.broadcast_to(alone, (heads, TOK)))
+    heads_out[PART_PAIRS:, :] = jnp.concatenate(skips, 0)
     high, low = halves(kernel_sum)
-    bc_out[0] = nn(high, c[...]) + nn(low, c[...])
+    grad_b = nn(high, c[...]) + nn(low, c[...])
     high, low = halves(kernel_sum.T)
-    bc_out[1] = nn(high, b[...]) + nn(low, b[...])
-
-
-def whole_kernel(
-    part, place, recv, u, w, kappa, heads, mine, theirs, after, entry_out, leave_out, heads_out
-):
+    grad_c = nn(high, b[...]) + nn(low, b[...])
+    if part:
+        grad_b = grad_b + refs[0][0]
+        grad_c = grad_c + refs[0][1]
+    bc_out[0] = grad_b
+    bc_out[1] = grad_c
+
+
+def whole_kernel(part, place, recv, u, w, kappa, heads, mine, theirs, *refs):
+    entry_out, leave_out, heads_out = refs[-3:]
     core = place[0]
     terms = []
     for p in range(PART_PAIRS):
         j = part * PART_PAIRS + p
         here = slice(128 * p, 128 * p + 128)
-        at = slice(128 * j, 128 * j + 128)
         full = recv[here, :] + recv[PART_ROWS + p : PART_ROWS + p + 1, :] * mine[here, :]
         other = theirs[here, :]
         entry = jnp.where(core == 1, full, other)
         leave = jnp.where(core == 1, other, full)
         entry_out[here, :] = entry
         leave_out[here, :] = leave
-        value = entry * (u[at, :] + kappa[j : j + 1, :] * leave) + w[at, :] * leave
+        value = entry * (u[here, :] + kappa[j : j + 1, :] * leave) + w[here, :] * leave
         terms.append(jnp.sum(value, axis=0, keepdims=True))
-    before = part * PART_PAIRS
-    after = before + PART_PAIRS
-    if before:
-        heads_out[:before, :] = heads[:before, :]
-    heads_out[before:after, :] = heads[before:after, :] + jnp.concatenate(terms, 0)
-    heads_out[after:, :] = heads[after:, :]
-
-
-def final_kernel(part, x, g, b, c, rows, cols, sums, gx, alog, acc, entry_in, leave_in, *refs):
-    gx_out, dt_out, bc_out, work = refs
+    first = 2 * PART_PAIRS * part
+    if part:
+        heads_out[:first, :] = refs[0][...]
+    heads_out[first : first + PART_PAIRS, :] = heads[:PART_PAIRS, :] + jnp.concatenate(terms, 0)
+    heads_out[first + PART_PAIRS :, :] = heads[PART_PAIRS:, :]
+
+
+def sums_kernel(part, x, g, cols, acc, entry_in, leave_in, bc_out):
+    lanes = iota((TOK, 128), 1) < 64
+    column_values = cols[...]
+    grad_b, grad_c = acc[0], acc[1]
+    for p in range(PART_PAIRS):
+        j = part * PART_PAIRS + p
+        at = slice(128 * j, 128 * j + 128)
+        local = slice(128 * p, 128 * p + 128)
+        entry_high, entry_low = halves(entry_in[local, :])
+        leave_high, leave_low = halves(leave_in[local, :])
+        x_wide, g_wide = x[:, at].astype(F32), g[:, at].astype(F32)
+        high, low = halves(pair_column(column_values, 2 * j, lanes) * g_wide)
+        grad_c = grad_c + nt(
+            jnp.concatenate([high, low, high], 1),
+            jnp.concatenate([entry_high, entry_high, entry_low], 1),
+        )
+        high, low = halves(pair_column(column_values, HEADS + 2 * j, lanes) * x_wide)
+        grad_b = grad_b + nt(
+            jnp.concatenate([high, low, high], 1),
+            jnp.concatenate([leave_high, leave_high, leave_low], 1),
+        )
+    bc_out[0] = grad_b
+    bc_out[1] = grad_c
+
+
+def final_kernel(part, x, g, b, c, rows, cols, sums, gx, alog, entry_in, leave_in, *refs):
+    gx_out, dt_out, work = refs[-3:]
     heads = 2 * PART_PAIRS
     first_head = part * heads
     lanes = iota((TOK, 128), 1) < 64
     column_values = cols[...]
     b_two = jnp.concatenate([b[...], b[...]], 1)
     c_two = jnp.concatenate([c[...], c[...]], 1)
-    grad_b, grad_c = acc[0], acc[1]
     for p in range(PART_PAIRS):
         j = part * PART_PAIRS + p
         at = slice(128 * j, 128 * j + 128)
         local = slice(128 * p, 128 * p + 128)
         entry, leave = entry_in[local, :], leave_in[local, :]
-        entry_high, entry_low = halves(entry)
-        leave_high, leave_low = halves(leave)
-        read = nn(c_two, jnp.concatenate([entry_high, entry_low], 0))
-        back = nn(b_two, jnp.concatenate([leave_high, leave_low], 0))
+        read = nn(c_two, jnp.concatenate(halves(entry), 0))
+        back = nn(b_two, jnp.concatenate(halves(leave), 0))
         x_wide, g_wide = x[:, at].astype(F32), g[:, at].astype(F32)
         leave_step = pair_column(column_values, HEADS + 2 * j, lanes)
-        gx_out[:, local] = (gx[:, at] + leave_step * back).astype(BF16)
+        gx_out[:, local] = (gx[:, local] + leave_step * back).astype(BF16)
         work[:TOK, local] = g_wide * read
         work[TOK : 2 * TOK, local] = x_wide * back
         work[2 * TOK :, local] = jnp.sum((entry * leave).reshape(TOK // 8, 8, 128), axis=0)
-        high, low = halves(pair_column(column_values, 2 * j, lanes) * g_wide)
-        grad_c = grad_c + nt(
-            jnp.concatenate([high, low, high], 1),
-            jnp.concatenate([entry_high, entry_high, entry_low], 1),
-        )
-        high, low = halves(leave_step * x_wide)
-        grad_b = grad_b + nt(
-            jnp.concatenate([high, low, high], 1),
-            jnp.concatenate([leave_high, leave_high, leave_low], 1),
-        )
-    bc_out[0] = grad_b
-    bc_out[1] = grad_c
     found = per_head(work[...], heads)
     here = slice(first_head, first_head + heads)
     step, enter, leave, pre, block = (rows[k, here, :] for k in (0, 2, 3, 4, 5))
-    flow, inner_x = sums[0, here, :], sums[1, here, :]
+    flow, inner_x = sums[0], sums[1]
     read_g, back_x = found[:, :TOK], found[:, TOK : 2 * TOK]
     cross = jnp.sum(found[:, 2 * TOK :], axis=1, keepdims=True)
     rate = jnp.exp(column(alog[...], HEADS))[here]
@@ -373,17 +395,30 @@
     dt_out[...] = step_grad / (1.0 + jnp.exp(-pre))
 
 
+def add_kernel(*refs):
+    refs[-1][...] = refs[0][...] + refs[1][...]
+
+
 def heads_kernel(own, one, two, three, out):
     total = (own[...] + one[...]) + (two[...] + three[...])
     lane, head = iota((128, HEADS), 0), iota((128, HEADS), 1)
     lanes_of = (lane // 64 == head % 2).astype(F32)
     values = nn(total, lanes_of, HIGHEST)
-    pair, head = iota((PAIRS, HEADS), 0), iota((PAIRS, HEADS), 1)
-    on = pair == head // 2
+    row, head = iota((2 * PAIRS, HEADS), 0), iota((2 * PAIRS, HEADS), 1)
+    pair = row // (2 * PART_PAIRS) * PART_PAIRS + row % PART_PAIRS
+    kind = row // PART_PAIRS % 2
     scale = 1.0 / math.sqrt(TOK * 32 * 64)
     for k in (0, 1):
-        kept = jnp.where(on, values[k * PAIRS : (k + 1) * PAIRS], 0.0)
+        on = jnp.logical_and(kind == k, pair == head // 2)
+        kept = jnp.where(on, values, 0.0)
         out[k : k + 1, :] = jnp.sum(kept, axis=0, keepdims=True) * scale
+
+
+def join_kernel(*refs):
+    gx_out, dt_out = refs[-2:]
+    for part in range(PARTS):
+        gx_out[:, part * PART_PAIRS * 128 : (part + 1) * PART_PAIRS * 128] = refs[part][...]
+        dt_out[2 * PART_PAIRS * part : 2 * PART_PAIRS * (part + 1), :] = refs[PARTS + part][...]
 
 
 def seq_pairs(move):
@@ -423,7 +458,7 @@
     return lax.ppermute(value, "seq", seq_pairs(move))
 
 
-def call(kernel, ins, outs, name, micros, scratch=(), limit=VMEM_LIMIT):
+def call(kernel, ins, outs, name, scratch=(), limit=VMEM_LIMIT):
     shapes = [jax.ShapeDtypeStruct(s, d) for s, d in outs]
     return pl.pallas_call(
         kernel,
@@ -433,9 +468,7 @@
         scratch_shapes=list(scratch),
         name=name,
         compiler_params=pltpu.CompilerParams(vmem_limit_bytes=limit),
-        cost_estimate=pl.CostEstimate(
-            flops=1 << 16, bytes_accessed=1 << 12, transcendentals=0
-        ),
+        cost_estimate=COST,
     )(*[value for _, value in ins])
 
 
@@ -464,7 +497,6 @@
         [((TOK, 2048), BF16), ((6, HEADS, TOK), F32), ((TOK, 128), F32), ((PAIRS, 128), F32)]
         + [(part_shape, F32)] * (2 * PARTS),
         "states",
-        micros=3.4,
     )
     x_vals, rows, cols, kappa = made[:4]
     sends, keeps = made[4 : 4 + PARTS], made[4 + PARTS :]
@@ -476,17 +508,46 @@
             [(1, place), (0, keeps[part]), (0, recvs[part])],
             [(chunk_shape, F32)] * CHIPS,
             "chip_total",
-            micros=0.6,
         )
         chunks.append([cut[0]] + [along_z(cut[CHIPS - k], -k) for k in range(1, CHIPS)])
+    within = []
+
+    def within_slab(part, after):
+        made = call(
+            functools.partial(within_kernel, part),
+            [
+                (1, doc_starts),
+                (1, skip_weight),
+                (0, x_vals),
+                (0, grad_out),
+                (0, b_proj),
+                (0, c_proj),
+                (0, rows),
+                (0, cols),
+            ]
+            + [(0, v[2]) for v in within[-1:]]
+            + [(2, after)],
+            [
+                ((TOK, PART_PAIRS * 128), F32),
+                ((2, 2 * PART_PAIRS, TOK), F32),
+                ((2, TOK, 128), F32),
+                ((PART_ROWS, 128), F32),
+                ((PART_ROWS, 128), F32),
+                ((2 * PART_PAIRS, 128), F32),
+            ],
+            "within",
+            scratch=[pltpu.VMEM((TOK, PART_PAIRS * 128), F32)],
+        )
+        within.append(made)
+
+    within_slab(0, chunks[-1][0])
     row_totals = []
     for part in range(PARTS):
         (row,) = call(
             row_kernel,
-            [(1, place)] + [(0, v) for v in chunks[part]],
+            [(1, place)] + [(0, chunks[part][k]) for k in ORDER_ROW] + [(2, within[0][1] if part == 0 else rows)],
             [(chunk_shape, F32)],
             "row_total",
-            micros=0.6,
         )
         row_totals.append(row)
     before = [[onward_y(row, k) for k in range(1, ROWS)] for row in row_totals]
@@ -494,80 +555,85 @@
     for part in range(PARTS):
         out = call(
             entry_kernel,
-            [(1, place)] + [(0, v) for v in chunks[part] + before[part]] + [(2, rows)],
+            [(1, place)]
+            + [(0, before[part][k]) for k in ORDER_Y]
+            + [(0, chunks[part][k]) for k in ORDER_ENTRY]
+            + [(2, rows)],
             [((CHUNK_ROWS, 128), F32)] * CHIPS,
             "entries",
-            micros=0.7,
-        )
+        )
+        if part == 0:
+            within_slab(1, out[0])
         pieces.append([out[0]] + [along_z(out[CHIPS - k], -k) for k in range(1, CHIPS)])
-    gx, sums, bc, u, w, heads = call(
-        within_kernel,
-        [
-            (1, doc_starts),
-            (1, skip_weight),
-            (0, x_vals),
-            (0, grad_out),
-            (0, b_proj),
-            (0, c_proj),
-            (0, rows),
-            (0, cols),
-            (2, pieces[-1][0]),
-        ],
-        [((TOK, 2048), F32), ((2, HEADS, TOK), F32), ((2, TOK, 128), F32)]
-        + [((2048, 128), F32)] * 2
-        + [((2 * PAIRS, 128), F32)],
-        "within",
-        micros=4.5,
-        scratch=[pltpu.VMEM((TOK, 2048), F32)],
-    )
-    gx_parts, dt_parts = [], []
+    gx_parts, dt_parts, finals = [], [], []
+
+    def final(part, sums, gx, entry, leave, after):
+        ins = [x_vals, grad_out, b_proj, c_proj, rows, cols, sums, gx, alog_row, entry, leave]
+        return call(
+            functools.partial(final_kernel, part),
+            [(0, v) for v in ins] + [(2, after)],
+            [((TOK, PART_PAIRS * 128), BF16), ((2 * PART_PAIRS, TOK), F32)],
+            "final",
+            scratch=[pltpu.VMEM((2 * TOK + 8, PART_PAIRS * 128), F32)],
+        )
+
+    bc = within[-1][2]
+    heads = None
     for part in range(PARTS):
+        gx, sums, _, u, w, start = within[part]
         (mine,) = call(
             assemble_kernel,
-            [(1, place)] + [(0, v) for v in pieces[part]] + [(2, pieces[-1][0] if part == 0 else sums)],
+            [(1, place)] + [(0, pieces[part][k]) for k in ORDER_ASSEMBLE] + [(2, pieces[-1][0]), (2, within[part][1])],
             [((PART_ROWS, 128), F32)],
             "assemble",
-            micros=0.5,
         )
         theirs = other_core(mine)
         entry, leave, heads = call(
             functools.partial(whole_kernel, part),
-            [(1, place)] + [(0, v) for v in [recvs[part], u, w, kappa, heads, mine, theirs]] + [(2, bc)],
-            [((PART_ROWS, 128), F32)] * 2 + [((2 * PAIRS, 128), F32)],
+            [(1, place)]
+            + [(0, v) for v in [recvs[part], u, w, kappa, start, mine, theirs]]
+            + ([(0, heads), (2, gx_parts[0])] if part else [])
+            + [(2, bc)],
+            [((PART_ROWS, 128), F32)] * 2 + [((2 * PART_PAIRS * (part + 1), 128), F32)],
             "whole",
-            micros=0.8,
-        )
-        gx_part, dt_part, bc = call(
-            functools.partial(final_kernel, part),
-            [
-                (0, v)
-                for v in [x_vals, grad_out, b_proj, c_proj, rows, cols, sums, gx]
-                + [alog_row, bc, entry, leave]
-            ],
-            [
-                ((TOK, PART_PAIRS * 128), BF16),
-                ((2 * PART_PAIRS, TOK), F32),
-                ((2, TOK, 128), F32),
-            ],
-            "final",
-            micros=1.8,
-            scratch=[pltpu.VMEM((2 * TOK + 8, PART_PAIRS * 128), F32)],
-        )
+        )
+        (bc,) = call(
+            functools.partial(sums_kernel, part),
+            [(0, v) for v in [x_vals, grad_out, cols, bc, entry, leave]],
+            [((2, TOK, 128), F32)],
+            "sums",
+        )
+        if part == 0:
+            gx_part, dt_part = final(part, sums, gx, entry, leave, bc)
+            gx_parts.append(gx_part)
+            dt_parts.append(dt_part)
+        else:
+            finals.append((part, sums, gx, entry, leave))
+    for part, sums, gx, entry, leave in finals:
+        gx_part, dt_part = final(part, sums, gx, entry, leave, bc)
         gx_parts.append(gx_part)
         dt_parts.append(dt_part)
-    grad_x = jnp.concatenate(gx_parts, 1)
-    grad_dt = jnp.concatenate(dt_parts, 0)
     grad_bc = bc
     for k in range(1, 4):
         grad_bc = grad_bc + lax.ppermute(bc, "head", [(i, (i + k) % 4) for i in range(4)])
-    heads = heads + other_core(heads)
+    (heads,) = call(
+        add_kernel,
+        [(0, heads), (0, other_core(heads)), (2, bc)],
+        [((2 * PAIRS, 128), F32)],
+        "chip_heads",
+    )
     heads = heads + along_z(heads, 1) + along_z(heads, 2) + along_z(heads, 3)
     (head_grads,) = call(
         heads_kernel,
         [(0, heads)] + [(0, along_y(heads, k)) for k in (1, 2, 3)],
         [((2, HEADS), F32)],
         "head_grads",
-        micros=0.5,
+    )
+    grad_x, grad_dt = call(
+        join_kernel,
+        [(0, v) for v in gx_parts + dt_parts] + [(2, heads)],
+        [((TOK, 2048), BF16), ((HEADS, TOK), F32)],
+        "join",
     )
     return (grad_x, grad_dt, grad_bc, head_grads)
 

time: 80.1 us -> 77.5 us (0.968)
  waiting for transfers between devices: 17.3 us -> 13 us
  Pallas kernels: 18.2 us -> 20.8 us
  other arithmetic: 2.22 us -> 0.78 us
  starting transfers between devices: 37 us -> 37.9 us
    pallas_call x15 -> x20, Pallas kernels: 18.2 us -> 20.8 us  [call(): pl.pallas_call(kernel, out_shape=shapes, in_specs=[SPACES[space] for spac...]
    ppermute x15, starting transfers between devices: 19.3 us -> 21.5 us  [along_z(): lax.ppermute(value, 'seq', seq_pairs(lambda y, z, core: (y, (z + distance...]
    ppermute x15, waiting for transfers between devices: 6.59 us -> 4.52 us  [along_z(): lax.ppermute(value, 'seq', seq_pairs(lambda y, z, core: (y, (z + distance...]
    ppermute x6, waiting for transfers between devices: 3.95 us -> 2.4 us  [onward_y(): return lax.ppermute(value, 'seq', seq_pairs(move))]
    concatenate x2 -> x0, other arithmetic: 1.43 us -> none  [the longest x1 0.83 us: local(): grad_x = jnp.concatenate(gx_parts, 1)]
    ppermute x3, starting transfers between devices: 4.01 us -> 2.58 us  [along_y(): lax.ppermute(value, 'seq', seq_pairs(lambda y, z, core: ((y + distance) %...]
    ppermute x5, waiting for transfers between devices: 2.54 us -> 1.42 us  [other_core(): lax.ppermute(value, 'seq', seq_pairs(lambda y, z, core: (y, z, 1 - core)))]
  transfers between devices with their start and end apart: 32 -> 32, of which waited for: 14 -> 9; matrix products, arithmetic and copies ran while one was open for 2% -> 0% of each run, Pallas kernels for 18% -> 22%
where the time goes in v3:
time: 77.5 us; the launch traced here: 76.9 us
  starting transfers between devices  37.9 us (49%)
  Pallas kernels  20.8 us (27%)
  waiting for transfers between devices  13 us (17%)
  local copies, waits for them, and re-layouts  3.42 us (4%)
  between operations  0.96 us (1%)
  other arithmetic  0.78 us (1%)
    ppermute x15, starting transfers between devices, along_z(): lax.ppermute(value, 'seq', seq_pairs(lambda y, z, core: (y, (z + distance...  21.5 us
    pallas_call x20, Pallas kernels, call(): pl.pallas_call(kernel, out_shape=shapes, in_specs=[SPACES[space] for spac...  20.8 us
    ppermute x6, starting transfers between devices, onward_y(): return lax.ppermute(value, 'seq', seq_pairs(move))  7.74 us
    ppermute x3, waiting for transfers between devices, along_y(): lax.ppermute(value, 'seq', seq_pairs(lambda y, z, core: ((y + distance) %...  4.63 us
    ppermute x15, waiting for transfers between devices, along_z(): lax.ppermute(value, 'seq', seq_pairs(lambda y, z, core: (y, (z + distance...  4.52 us
    ppermute x3, starting transfers between devices, local(): lax.ppermute(bc, 'head', [(i, (i + k) % 4) for i in range(4)])  4.45 us
    unnamed x22, local copies, waits for them, and re-layouts  3.42 us
    ppermute x3, starting transfers between devices, along_y(): lax.ppermute(value, 'seq', seq_pairs(lambda y, z, core: ((y + distance) %...  2.58 us
  transfers between devices with their start and end apart: 32, of which 9 were waited for; matrix products, arithmetic and copies ran while one was open for 0% of the time, Pallas kernels for 22%

profile of v3, /device:TPU:0, one launch (start us, length us, event | category | flops | bytes accessed | tf_op | source)
XLA Modules:
  0.0 76.9 jit_solution(8286236668595152477)
XLA Ops:
  3.6 3.0 %states.1 = (bf16[128,2048]{1,0:T(8,128)(2,1)S(1)}, f32[6,32,128]{2,1,0:T(8,128)S(1)}, f32[128,128]{1,0:T(8,128)S(1)}, f32[16,128]{1,0:T(8,128)S(1)}, f32[1032,1...) custom-call(s32[3]{0:T(128)S(1)} %pad_add_fusion.place, ...), custom_call_target="tpu_custom_call" | custom-call | flops 65536 | bytes 4096 | tf_op jit(solution)/shard_map/states/pallas_call | solution.py:463
  7.1 1.4 %collective-permute-done.1.recv = f32[1032,128]{1,0:T(8,128)S(1)} collective-permute-done((f32[1032,128]{1,0:T(8,128)S(1)}, f32[1032,128]{1,0:T(8,128)S(1)}, u32[]{:S(2)}, u32[]{:S(2)}) %collective-permute-start.1) | collective-permute-done | bytes 528416 | tf_op jit(solution)/shard_map/ppermute | solution.py:438
  9.1 2.1 %collective-permute-start.2 = (f32[264,128]{1,0:T(8,128)S(1)}, f32[264,128]{1,0:T(8,128)S(1)}, u32[]{:S(2)}, u32[]{:S(2)}) collective-permute-start(f32[264,128]{1,0:T(8,128)S(1)} %get-tuple-element.66), channel_id=1, source_target_pairs={{0,8},{4,12},{8,16},{12,20},{16,24},{20,28},{24,0},{28,4},{32,40},... | collective-permute-start | bytes 405512 | tf_op jit(solution)/shard_map/ppermute | solution.py:442
  11.2 2.2 %collective-permute-start.3 = (f32[264,128]{1,0:T(8,128)S(1)}, f32[264,128]{1,0:T(8,128)S(1)}, u32[]{:S(2)}, u32[]{:S(2)}) collective-permute-start(f32[264,128]{1,0:T(8,128)S(1)} %get-tuple-element.67), channel_id=1, source_target_pairs={{0,24},{4,28},{8,0},{12,4},{16,8},{20,12},{24,16},{28,20},{32,56},... | collective-permute-start | bytes 405512 | tf_op jit(solution)/shard_map/ppermute | solution.py:442
  13.4 1.8 %collective-permute-start.4 = (f32[264,128]{1,0:T(8,128)S(1)}, f32[264,128]{1,0:T(8,128)S(1)}, u32[]{:S(2)}, u32[]{:S(2)}) collective-permute-start(f32[264,128]{1,0:T(8,128)S(1)} %get-tuple-element.68), channel_id=1, source_target_pairs={{0,16},{4,20},{8,24},{12,28},{16,0},{20,4},{24,8},{28,12},{32,48},... | collective-permute-start | bytes 405512 | tf_op jit(solution)/shard_map/ppermute | solution.py:442
  16.9 2.2 %collective-permute-start.12 = (f32[264,128]{1,0:T(8,128)S(1)}, f32[264,128]{1,0:T(8,128)S(1)}, u32[]{:S(2)}, u32[]{:S(2)}) collective-permute-start(f32[264,128]{1,0:T(8,128)S(1)} %get-tuple-element.75), channel_id=1, source_target_pairs={{0,24},{4,28},{8,0},{12,4},{16,8},{20,12},{24,16},{28,20},{32,56},... | collective-permute-start | bytes 405512 | tf_op jit(solution)/shard_map/ppermute | solution.py:442
  20.3 2.7 %within.2 = (f32[128,1024]{1,0:T(8,128)S(1)}, f32[2,16,128]{2,1,0:T(8,128)S(1)}, f32[2,128,128]{2,1,0:T(8,128)S(1)}, f32[1024,128]{1,0:T(8,128)S(1)}, f32[1024,128]{1,0:T(8,128)S(1)}, /*index=5*/f32[16,128]{1,0:T(8,128)S(1)}) custom-call(s32[1,2]{1,0:T(1,128)S(1)} %copy-done.7, f32[32]{0:T(128)S(1)} %copy-done.9, bf16[128,2048]{1,0:T(8,128)(2,1)S(1)} %get-tuple-element.52.x, ...), custom_call_target="tpu_custom_call" | custom-call | flops 65536 | bytes 4096 | tf_op jit(solution)/shard_map/within/pallas_call | solution.py:463
  23.7 1.3 %collective-permute-start.7 = (f32[264,128]{1,0:T(8,128)S(1)}, f32[264,128]{1,0:T(8,128)S(1)}, u32[]{:S(2)}, u32[]{:S(2)}) collective-permute-start(f32[264,128]{1,0:T(8,128)S(1)} %row_total.2), channel_id=1, source_target_pairs={{4,68},{12,76},{20,84},{28,92},{36,100},{44,108},{52,116},{60,124}... | collective-permute-start | bytes 405512 | tf_op jit(solution)/shard_map/ppermute | solution.py:458
  25.0 1.3 %collective-permute-start.6 = (f32[264,128]{1,0:T(8,128)S(1)}, f32[264,128]{1,0:T(8,128)S(1)}, u32[]{:S(2)}, u32[]{:S(2)}) collective-permute-start(f32[264,128]{1,0:T(8,128)S(1)} %row_total.2), channel_id=1, source_target_pairs={{4,100},{12,108},{20,116},{28,124},{96,0},{104,8},{112,16},{120,24... | collective-permute-start | bytes 405512 | tf_op jit(solution)/shard_map/ppermute | solution.py:458
  26.3 1.3 %collective-permute-start.5 = (f32[264,128]{1,0:T(8,128)S(1)}, f32[264,128]{1,0:T(8,128)S(1)}, u32[]{:S(2)}, u32[]{:S(2)}) collective-permute-start(f32[264,128]{1,0:T(8,128)S(1)} %row_total.2), channel_id=1, source_target_pairs={{4,36},{12,44},{20,52},{28,60},{32,0},{36,68},{40,8},{44,76},{48,1... | collective-permute-start | bytes 405512 | tf_op jit(solution)/shard_map/ppermute | solution.py:458
  28.3 1.3 %collective-permute-start.16 = (f32[264,128]{1,0:T(8,128)S(1)}, f32[264,128]{1,0:T(8,128)S(1)}, u32[]{:S(2)}, u32[]{:S(2)}) collective-permute-start(f32[264,128]{1,0:T(8,128)S(1)} %row_total.3), channel_id=1, source_target_pairs={{4,68},{12,76},{20,84},{28,92},{36,100},{44,108},{52,116},{60,124}... | collective-permute-start | bytes 405512 | tf_op jit(solution)/shard_map/ppermute | solution.py:458
  30.9 1.3 %collective-permute-done.7.refs_2_ = f32[264,128]{1,0:T(8,128)S(1)} collective-permute-done((f32[264,128]{1,0:T(8,128)S(1)}, f32[264,128]{1,0:T(8,128)S(1)}, u32[]{:S(2)}, u32[]{:S(2)}) %collective-permute-start.7) | collective-permute-done | bytes 135200 | tf_op jit(solution)/shard_map/ppermute | solution.py:458
  34.9 2.0 %collective-permute-start.8 = (f32[256,128]{1,0:T(8,128)S(1)}, f32[256,128]{1,0:T(8,128)S(1)}, u32[]{:S(2)}, u32[]{:S(2)}) collective-permute-start(f32[256,128]{1,0:T(8,128)S(1)} %get-tuple-element.70), channel_id=1, source_target_pairs={{0,24},{4,28},{8,0},{12,4},{16,8},{20,12},{24,16},{28,20},{32,56},... | collective-permute-start | bytes 393224 | tf_op jit(solution)/shard_map/ppermute | solution.py:442
  38.1 1.3 %collective-permute-start.10 = (f32[256,128]{1,0:T(8,128)S(1)}, f32[256,128]{1,0:T(8,128)S(1)}, u32[]{:S(2)}, u32[]{:S(2)}) collective-permute-start(f32[256,128]{1,0:T(8,128)S(1)} %get-tuple-element.73), channel_id=1, source_target_pairs={{0,8},{4,12},{8,16},{12,20},{16,24},{20,28},{24,0},{28,4},{32,40},... | collective-permute-start | bytes 393224 | tf_op jit(solution)/shard_map/ppermute | solution.py:442
  40.5 2.0 %collective-permute-start.18 = (f32[256,128]{1,0:T(8,128)S(1)}, f32[256,128]{1,0:T(8,128)S(1)}, u32[]{:S(2)}, u32[]{:S(2)}) collective-permute-start(f32[256,128]{1,0:T(8,128)S(1)} %get-tuple-element.88), channel_id=1, source_target_pairs={{0,24},{4,28},{8,0},{12,4},{16,8},{20,12},{24,16},{28,20},{32,56},... | collective-permute-start | bytes 393224 | tf_op jit(solution)/shard_map/ppermute | solution.py:442
  43.7 1.3 %collective-permute-start.20 = (f32[256,128]{1,0:T(8,128)S(1)}, f32[256,128]{1,0:T(8,128)S(1)}, u32[]{:S(2)}, u32[]{:S(2)}) collective-permute-start(f32[256,128]{1,0:T(8,128)S(1)} %get-tuple-element.90), channel_id=1, source_target_pairs={{0,8},{4,12},{8,16},{12,20},{16,24},{20,28},{24,0},{28,4},{32,40},... | collective-permute-start | bytes 393224 | tf_op jit(solution)/shard_map/ppermute | solution.py:442
  45.0 2.6 %collective-permute-done.10.refs_3_ = f32[256,128]{1,0:T(8,128)S(1)} collective-permute-done((f32[256,128]{1,0:T(8,128)S(1)}, f32[256,128]{1,0:T(8,128)S(1)}, u32[]{:S(2)}, u32[]{:S(2)}) %collective-permute-start.10) | collective-permute-done | bytes 131104 | tf_op jit(solution)/shard_map/ppermute | solution.py:442
  48.5 2.7 %within.3 = (f32[128,1024]{1,0:T(8,128)S(1)}, f32[2,16,128]{2,1,0:T(8,128)S(1)}, f32[2,128,128]{2,1,0:T(8,128)S(1)}, f32[1024,128]{1,0:T(8,128)S(1)}, f32[1024,128]{1,0:T(8,128)S(1)}, /*index=5*/f32[16,128]{1,0:T(8,128)S(1)}) custom-call(s32[1,2]{1,0:T(1,128)S(1)} %copy-done.7, f32[32]{0:T(128)S(1)} %copy-done.9, bf16[128,2048]{1,0:T(8,128)(2,1)S(1)} %get-tuple-element.52.x, ...), custom_call_target="tpu_custom_call" | custom-call | flops 65536 | bytes 4096 | tf_op jit(solution)/shard_map/within/pallas_call | solution.py:463
  51.3 1.9 %collective-permute-done.20.refs_3_ = f32[256,128]{1,0:T(8,128)S(1)} collective-permute-done((f32[256,128]{1,0:T(8,128)S(1)}, f32[256,128]{1,0:T(8,128)S(1)}, u32[]{:S(2)}, u32[]{:S(2)}) %collective-permute-start.20) | collective-permute-done | bytes 131104 | tf_op jit(solution)/shard_map/ppermute | solution.py:442
  61.7 2.8 %collective-permute-start.28 = (f32[2,128,128]{2,1,0:T(8,128)S(1)}, f32[2,128,128]{2,1,0:T(8,128)S(1)}, u32[]{:S(2)}, u32[]{:S(2)}) collective-permute-start(f32[2,128,128]{2,1,0:T(8,128)S(1)} %sums.3.refs_0_.refs_2_), channel_id=1, source_target_pairs={{0,3},{1,0},{2,1},{3,2},{4,7},{5,4},{6,5},{7,6},{8,11},{9,8},{10,9... | collective-permute-start | bytes 393224 | tf_op jit(solution)/shard_map/ppermute | solution.py:618
  66.2 2.6 %collective-permute-start.31 = (f32[32,128]{1,0:T(8,128)S(1)}, f32[32,128]{1,0:T(8,128)S(1)}, u32[]{:S(2)}, u32[]{:S(2)}) collective-permute-start(f32[32,128]{1,0:T(8,128)S(1)} %add_add_fusion.1.refs_4_.own), channel_id=1, source_target_pairs={{0,96},{4,100},{8,104},{12,108},{16,112},{20,116},{24,120},{28,124... | collective-permute-start | bytes 49160 | tf_op jit(solution)/shard_map/ppermute | solution.py:448
  68.7 1.4 %collective-permute-done.31.three = f32[32,128]{1,0:T(8,128)S(1)} collective-permute-done((f32[32,128]{1,0:T(8,128)S(1)}, f32[32,128]{1,0:T(8,128)S(1)}, u32[]{:S(2)}, u32[]{:S(2)}) %collective-permute-start.31) | collective-permute-done | bytes 16416 | tf_op jit(solution)/shard_map/ppermute | solution.py:448
  72.2 1.8 %collective-permute-done.30.two = f32[32,128]{1,0:T(8,128)S(1)} collective-permute-done((f32[32,128]{1,0:T(8,128)S(1)}, f32[32,128]{1,0:T(8,128)S(1)}, u32[]{:S(2)}, u32[]{:S(2)}) %collective-permute-start.30) | collective-permute-done | bytes 16416 | tf_op jit(solution)/shard_map/ppermute | solution.py:448
  74.0 1.4 %collective-permute-done.29.one = f32[32,128]{1,0:T(8,128)S(1)} collective-permute-done((f32[32,128]{1,0:T(8,128)S(1)}, f32[32,128]{1,0:T(8,128)S(1)}, u32[]{:S(2)}, u32[]{:S(2)}) %collective-permute-start.29) | collective-permute-done | bytes 16416 | tf_op jit(solution)/shard_map/ppermute | solution.py:448
  (85 shorter events, 30.1 us)
Async XLA Ops:
  6.6 8.6 %collective-permute-start = (f32[1032,128]{1,0:T(8,128)S(1)}, f32[1032,128]{1,0:T(8,128)S(1)}, u32[]{:S(2)}, u32[]{:S(2)}) collective-permute-start(f32[1032,128]{1,0:T(8,128)S(1)} %get-tuple-element.56), channel_id=1, source_target_pairs={{0,4},{4,0},{8,12},{12,8},{16,20},{20,16},{24,28},{28,24},{32,36},... | collective-permute-start | bytes 1585160 | tf_op jit(solution)/shard_map/ppermute | solution.py:438
  9.1 10.0 %collective-permute-start.2 = (f32[264,128]{1,0:T(8,128)S(1)}, f32[264,128]{1,0:T(8,128)S(1)}, u32[]{:S(2)}, u32[]{:S(2)}) collective-permute-start(f32[264,128]{1,0:T(8,128)S(1)} %get-tuple-element.66), channel_id=1, source_target_pairs={{0,8},{4,12},{8,16},{12,20},{16,24},{20,28},{24,0},{28,4},{32,40},... | collective-permute-start | bytes 405512 | tf_op jit(solution)/shard_map/ppermute | solution.py:442
  11.2 11.9 %collective-permute-start.3 = (f32[264,128]{1,0:T(8,128)S(1)}, f32[264,128]{1,0:T(8,128)S(1)}, u32[]{:S(2)}, u32[]{:S(2)}) collective-permute-start(f32[264,128]{1,0:T(8,128)S(1)} %get-tuple-element.67), channel_id=1, source_target_pairs={{0,24},{4,28},{8,0},{12,4},{16,8},{20,12},{24,16},{28,20},{32,56},... | collective-permute-start | bytes 405512 | tf_op jit(solution)/shard_map/ppermute | solution.py:442
  13.4 9.7 %collective-permute-start.4 = (f32[264,128]{1,0:T(8,128)S(1)}, f32[264,128]{1,0:T(8,128)S(1)}, u32[]{:S(2)}, u32[]{:S(2)}) collective-permute-start(f32[264,128]{1,0:T(8,128)S(1)} %get-tuple-element.68), channel_id=1, source_target_pairs={{0,16},{4,20},{8,24},{12,28},{16,0},{20,4},{24,8},{28,12},{32,48},... | collective-permute-start | bytes 405512 | tf_op jit(solution)/shard_map/ppermute | solution.py:442
  15.8 10.5 %collective-permute-start.11 = (f32[264,128]{1,0:T(8,128)S(1)}, f32[264,128]{1,0:T(8,128)S(1)}, u32[]{:S(2)}, u32[]{:S(2)}) collective-permute-start(f32[264,128]{1,0:T(8,128)S(1)} %get-tuple-element.74), channel_id=1, source_target_pairs={{0,8},{4,12},{8,16},{12,20},{16,24},{20,28},{24,0},{28,4},{32,40},... | collective-permute-start | bytes 405512 | tf_op jit(solution)/shard_map/ppermute | solution.py:442
  16.9 10.7 %collective-permute-start.12 = (f32[264,128]{1,0:T(8,128)S(1)}, f32[264,128]{1,0:T(8,128)S(1)}, u32[]{:S(2)}, u32[]{:S(2)}) collective-permute-start(f32[264,128]{1,0:T(8,128)S(1)} %get-tuple-element.75), channel_id=1, source_target_pairs={{0,24},{4,28},{8,0},{12,4},{16,8},{20,12},{24,16},{28,20},{32,56},... | collective-permute-start | bytes 405512 | tf_op jit(solution)/shard_map/ppermute | solution.py:442
  19.1 8.5 %collective-permute-start.13 = (f32[264,128]{1,0:T(8,128)S(1)}, f32[264,128]{1,0:T(8,128)S(1)}, u32[]{:S(2)}, u32[]{:S(2)}) collective-permute-start(f32[264,128]{1,0:T(8,128)S(1)} %get-tuple-element.76), channel_id=1, source_target_pairs={{0,16},{4,20},{8,24},{12,28},{16,0},{20,4},{24,8},{28,12},{32,48},... | collective-permute-start | bytes 405512 | tf_op jit(solution)/shard_map/ppermute | solution.py:442
  23.7 8.5 %collective-permute-start.7 = (f32[264,128]{1,0:T(8,128)S(1)}, f32[264,128]{1,0:T(8,128)S(1)}, u32[]{:S(2)}, u32[]{:S(2)}) collective-permute-start(f32[264,128]{1,0:T(8,128)S(1)} %row_total.2), channel_id=1, source_target_pairs={{4,68},{12,76},{20,84},{28,92},{36,100},{44,108},{52,116},{60,124}... | collective-permute-start | bytes 405512 | tf_op jit(solution)/shard_map/ppermute | solution.py:458
  25.0 9.1 %collective-permute-start.6 = (f32[264,128]{1,0:T(8,128)S(1)}, f32[264,128]{1,0:T(8,128)S(1)}, u32[]{:S(2)}, u32[]{:S(2)}) collective-permute-start(f32[264,128]{1,0:T(8,128)S(1)} %row_total.2), channel_id=1, source_target_pairs={{4,100},{12,108},{20,116},{28,124},{96,0},{104,8},{112,16},{120,24... | collective-permute-start | bytes 405512 | tf_op jit(solution)/shard_map/ppermute | solution.py:458
  26.3 7.8 %collective-permute-start.5 = (f32[264,128]{1,0:T(8,128)S(1)}, f32[264,128]{1,0:T(8,128)S(1)}, u32[]{:S(2)}, u32[]{:S(2)}) collective-permute-start(f32[264,128]{1,0:T(8,128)S(1)} %row_total.2), channel_id=1, source_target_pairs={{4,36},{12,44},{20,52},{28,60},{32,0},{36,68},{40,8},{44,76},{48,1... | collective-permute-start | bytes 405512 | tf_op jit(solution)/shard_map/ppermute | solution.py:458
  28.3 9.8 %collective-permute-start.16 = (f32[264,128]{1,0:T(8,128)S(1)}, f32[264,128]{1,0:T(8,128)S(1)}, u32[]{:S(2)}, u32[]{:S(2)}) collective-permute-start(f32[264,128]{1,0:T(8,128)S(1)} %row_total.3), channel_id=1, source_target_pairs={{4,68},{12,76},{20,84},{28,92},{36,100},{44,108},{52,116},{60,124}... | collective-permute-start | bytes 405512 | tf_op jit(solution)/shard_map/ppermute | solution.py:458
  29.6 10.2 %collective-permute-start.15 = (f32[264,128]{1,0:T(8,128)S(1)}, f32[264,128]{1,0:T(8,128)S(1)}, u32[]{:S(2)}, u32[]{:S(2)}) collective-permute-start(f32[264,128]{1,0:T(8,128)S(1)} %row_total.3), channel_id=1, source_target_pairs={{4,100},{12,108},{20,116},{28,124},{96,0},{104,8},{112,16},{120,24... | collective-permute-start | bytes 405512 | tf_op jit(solution)/shard_map/ppermute | solution.py:458
  32.2 7.6 %collective-permute-start.14 = (f32[264,128]{1,0:T(8,128)S(1)}, f32[264,128]{1,0:T(8,128)S(1)}, u32[]{:S(2)}, u32[]{:S(2)}) collective-permute-start(f32[264,128]{1,0:T(8,128)S(1)} %row_total.3), channel_id=1, source_target_pairs={{4,36},{12,44},{20,52},{28,60},{32,0},{36,68},{40,8},{44,76},{48,1... | collective-permute-start | bytes 405512 | tf_op jit(solution)/shard_map/ppermute | solution.py:458
  34.9 8.8 %collective-permute-start.8 = (f32[256,128]{1,0:T(8,128)S(1)}, f32[256,128]{1,0:T(8,128)S(1)}, u32[]{:S(2)}, u32[]{:S(2)}) collective-permute-start(f32[256,128]{1,0:T(8,128)S(1)} %get-tuple-element.70), channel_id=1, source_target_pairs={{0,24},{4,28},{8,0},{12,4},{16,8},{20,12},{24,16},{28,20},{32,56},... | collective-permute-start | bytes 393224 | tf_op jit(solution)/shard_map/ppermute | solution.py:442
  36.9 8.1 %collective-permute-start.9 = (f32[256,128]{1,0:T(8,128)S(1)}, f32[256,128]{1,0:T(8,128)S(1)}, u32[]{:S(2)}, u32[]{:S(2)}) collective-permute-start(f32[256,128]{1,0:T(8,128)S(1)} %get-tuple-element.72), channel_id=1, source_target_pairs={{0,16},{4,20},{8,24},{12,28},{16,0},{20,4},{24,8},{28,12},{32,48},... | collective-permute-start | bytes 393224 | tf_op jit(solution)/shard_map/ppermute | solution.py:442
  38.1 9.5 %collective-permute-start.10 = (f32[256,128]{1,0:T(8,128)S(1)}, f32[256,128]{1,0:T(8,128)S(1)}, u32[]{:S(2)}, u32[]{:S(2)}) collective-permute-start(f32[256,128]{1,0:T(8,128)S(1)} %get-tuple-element.73), channel_id=1, source_target_pairs={{0,8},{4,12},{8,16},{12,20},{16,24},{20,28},{24,0},{28,4},{32,40},... | collective-permute-start | bytes 393224 | tf_op jit(solution)/shard_map/ppermute | solution.py:442
  40.5 10.8 %collective-permute-start.18 = (f32[256,128]{1,0:T(8,128)S(1)}, f32[256,128]{1,0:T(8,128)S(1)}, u32[]{:S(2)}, u32[]{:S(2)}) collective-permute-start(f32[256,128]{1,0:T(8,128)S(1)} %get-tuple-element.88), channel_id=1, source_target_pairs={{0,24},{4,28},{8,0},{12,4},{16,8},{20,12},{24,16},{28,20},{32,56},... | collective-permute-start | bytes 393224 | tf_op jit(solution)/shard_map/ppermute | solution.py:442
  42.5 8.8 %collective-permute-start.19 = (f32[256,128]{1,0:T(8,128)S(1)}, f32[256,128]{1,0:T(8,128)S(1)}, u32[]{:S(2)}, u32[]{:S(2)}) collective-permute-start(f32[256,128]{1,0:T(8,128)S(1)} %get-tuple-element.89), channel_id=1, source_target_pairs={{0,16},{4,20},{8,24},{12,28},{16,0},{20,4},{24,8},{28,12},{32,48},... | collective-permute-start | bytes 393224 | tf_op jit(solution)/shard_map/ppermute | solution.py:442
  43.7 9.6 %collective-permute-start.20 = (f32[256,128]{1,0:T(8,128)S(1)}, f32[256,128]{1,0:T(8,128)S(1)}, u32[]{:S(2)}, u32[]{:S(2)}) collective-permute-start(f32[256,128]{1,0:T(8,128)S(1)} %get-tuple-element.90), channel_id=1, source_target_pairs={{0,8},{4,12},{8,16},{12,20},{16,24},{20,28},{24,0},{28,4},{32,40},... | collective-permute-start | bytes 393224 | tf_op jit(solution)/shard_map/ppermute | solution.py:442
  59.1 6.2 %collective-permute-start.25 = (f32[32,128]{1,0:T(8,128)S(1)}, f32[32,128]{1,0:T(8,128)S(1)}, u32[]{:S(2)}, u32[]{:S(2)}) collective-permute-start(f32[32,128]{1,0:T(8,128)S(1)} %chip_heads.1), channel_id=1, source_target_pairs={{0,24},{4,28},{8,0},{12,4},{16,8},{20,12},{24,16},{28,20},{32,56},... | collective-permute-start | bytes 49160 | tf_op jit(solution)/shard_map/ppermute | solution.py:442
  59.7 6.4 %collective-permute-start.24 = (f32[32,128]{1,0:T(8,128)S(1)}, f32[32,128]{1,0:T(8,128)S(1)}, u32[]{:S(2)}, u32[]{:S(2)}) collective-permute-start(f32[32,128]{1,0:T(8,128)S(1)} %chip_heads.1), channel_id=1, source_target_pairs={{0,16},{4,20},{8,24},{12,28},{16,0},{20,4},{24,8},{28,12},{32,48},... | collective-permute-start | bytes 49160 | tf_op jit(solution)/shard_map/ppermute | solution.py:442
  61.7 14.5 %collective-permute-start.28 = (f32[2,128,128]{2,1,0:T(8,128)S(1)}, f32[2,128,128]{2,1,0:T(8,128)S(1)}, u32[]{:S(2)}, u32[]{:S(2)}) collective-permute-start(f32[2,128,128]{2,1,0:T(8,128)S(1)} %sums.3.refs_0_.refs_2_), channel_id=1, source_target_pairs={{0,3},{1,0},{2,1},{3,2},{4,7},{5,4},{6,5},{7,6},{8,11},{9,8},{10,9... | collective-permute-start | bytes 393224 | tf_op jit(solution)/shard_map/ppermute | solution.py:618
  64.5 11.7 %collective-permute-start.27 = (f32[2,128,128]{2,1,0:T(8,128)S(1)}, f32[2,128,128]{2,1,0:T(8,128)S(1)}, u32[]{:S(2)}, u32[]{:S(2)}) collective-permute-start(f32[2,128,128]{2,1,0:T(8,128)S(1)} %sums.3.refs_0_.refs_2_), channel_id=1, source_target_pairs={{0,2},{1,3},{2,0},{3,1},{4,6},{5,7},{6,4},{7,5},{8,10},{9,11},{10,... | collective-permute-start | bytes 393224 | tf_op jit(solution)/shard_map/ppermute | solution.py:618
  65.2 10.9 %collective-permute-start.26 = (f32[2,128,128]{2,1,0:T(8,128)S(1)}, f32[2,128,128]{2,1,0:T(8,128)S(1)}, u32[]{:S(2)}, u32[]{:S(2)}) collective-permute-start(f32[2,128,128]{2,1,0:T(8,128)S(1)} %sums.3.refs_0_.refs_2_), channel_id=1, source_target_pairs={{0,1},{1,2},{2,3},{3,0},{4,5},{5,6},{6,7},{7,4},{8,9},{9,10},{10,1... | collective-permute-start | bytes 393224 | tf_op jit(solution)/shard_map/ppermute | solution.py:618
  (19 other events, 44.2 us)

commit v4 on v3

--- a/solution.py
+++ b/solution.py
@@ -311,19 +311,24 @@
     bc_out[1] = grad_c
 
 
-def whole_kernel(part, place, recv, u, w, kappa, heads, mine, theirs, *refs):
-    entry_out, leave_out, heads_out = refs[-3:]
+def whole_kernel(part, place, recv, mine, theirs, *refs):
+    entry_out, leave_out = refs[-2:]
     core = place[0]
+    for p in range(PART_PAIRS):
+        here = slice(128 * p, 128 * p + 128)
+        full = recv[here, :] + recv[PART_ROWS + p : PART_ROWS + p + 1, :] * mine[here, :]
+        other = theirs[here, :]
+        entry_out[here, :] = jnp.where(core == 1, full, other)
+        leave_out[here, :] = jnp.where(core == 1, other, full)
+
+
+def logs_kernel(part, u, w, kappa, heads, entry_in, leave_in, *refs):
+    heads_out = refs[-1]
     terms = []
     for p in range(PART_PAIRS):
         j = part * PART_PAIRS + p
         here = slice(128 * p, 128 * p + 128)
-        full = recv[here, :] + recv[PART_ROWS + p : PART_ROWS + p + 1, :] * mine[here, :]
-        other = theirs[here, :]
-        entry = jnp.where(core == 1, full, other)
-        leave = jnp.where(core == 1, other, full)
-        entry_out[here, :] = entry
-        leave_out[here, :] = leave
+        entry, leave = entry_in[here, :], leave_in[here, :]
         value = entry * (u[here, :] + kappa[j : j + 1, :] * leave) + w[here, :] * leave
         terms.append(jnp.sum(value, axis=0, keepdims=True))
     first = 2 * PART_PAIRS * part
@@ -399,7 +404,8 @@
     refs[-1][...] = refs[0][...] + refs[1][...]
 
 
-def heads_kernel(own, one, two, three, out):
+def heads_kernel(own, one, two, three, bc, bc_one, bc_two, bc_three, out, bc_out):
+    bc_out[...] = (bc[...] + bc_one[...]) + (bc_two[...] + bc_three[...])
     total = (own[...] + one[...]) + (two[...] + three[...])
     lane, head = iota((128, HEADS), 0), iota((128, HEADS), 1)
     lanes_of = (lane // 64 == head % 2).astype(F32)
@@ -588,13 +594,11 @@
             "assemble",
         )
         theirs = other_core(mine)
-        entry, leave, heads = call(
+        entry, leave = call(
             functools.partial(whole_kernel, part),
-            [(1, place)]
-            + [(0, v) for v in [recvs[part], u, w, kappa, start, mine, theirs]]
-            + ([(0, heads), (2, gx_parts[0])] if part else [])
+            [(1, place), (0, recvs[part]), (0, mine), (0, theirs)]
             + [(2, bc)],
-            [((PART_ROWS, 128), F32)] * 2 + [((2 * PART_PAIRS * (part + 1), 128), F32)],
+            [((PART_ROWS, 128), F32)] * 2,
             "whole",
         )
         (bc,) = call(
@@ -602,6 +606,14 @@
             [(0, v) for v in [x_vals, grad_out, cols, bc, entry, leave]],
             [((2, TOK, 128), F32)],
             "sums",
+        )
+        (heads,) = call(
+            functools.partial(logs_kernel, part),
+            [(0, v) for v in [u, w, kappa, start, entry, leave]]
+            + ([(0, heads)] if part else [])
+            + [(2, bc)],
+            [((2 * PART_PAIRS * (part + 1), 128), F32)],
+            "logs",
         )
         if part == 0:
             gx_part, dt_part = final(part, sums, gx, entry, leave, bc)
@@ -613,9 +625,7 @@
         gx_part, dt_part = final(part, sums, gx, entry, leave, bc)
         gx_parts.append(gx_part)
         dt_parts.append(dt_part)
-    grad_bc = bc
-    for k in range(1, 4):
-        grad_bc = grad_bc + lax.ppermute(bc, "head", [(i, (i + k) % 4) for i in range(4)])
+    others = [lax.ppermute(bc, "head", [(i, (i + k) % 4) for i in range(4)]) for k in (1, 2, 3)]
     (heads,) = call(
         add_kernel,
         [(0, heads), (0, other_core(heads)), (2, bc)],
@@ -623,11 +633,11 @@
         "chip_heads",
     )
     heads = heads + along_z(heads, 1) + along_z(heads, 2) + along_z(heads, 3)
-    (head_grads,) = call(
+    head_grads, grad_bc = call(
         heads_kernel,
-        [(0, heads)] + [(0, along_y(heads, k)) for k in (1, 2, 3)],
-        [((2, HEADS), F32)],
-        "head_grads",
+        [(0, heads)] + [(0, along_y(heads, k)) for k in (1, 2, 3)] + [(0, v) for v in [bc] + others],
+        [((2, HEADS), F32), ((2, TOK, 128), F32)],
+        "last",
     )
     grad_x, grad_dt = call(
         join_kernel,

time: 77.5 us -> 76.3 us (0.985)
  starting transfers between devices: 37.9 us -> 35.1 us
  waiting for transfers between devices: 13 us -> 15 us
    ppermute x15, starting transfers between devices: 21.5 us -> 19.5 us  [along_z(): lax.ppermute(value, 'seq', seq_pairs(lambda y, z, core: (y, (z + distance...]
    ppermute x15, waiting for transfers between devices: 4.52 us -> 6.01 us  [along_z(): lax.ppermute(value, 'seq', seq_pairs(lambda y, z, core: (y, (z + distance...]
    ppermute x3, waiting for transfers between devices: 4.63 us -> 3.36 us  [along_y(): lax.ppermute(value, 'seq', seq_pairs(lambda y, z, core: ((y + distance) %...]
    ppermute x5, waiting for transfers between devices: 1.42 us -> 2.66 us  [other_core(): lax.ppermute(value, 'seq', seq_pairs(lambda y, z, core: (y, z, 1 - core)))]
    pallas_call x20 -> x22, Pallas kernels: 20.8 us -> 21 us  [call(): pl.pallas_call(kernel, out_shape=shapes, in_specs=[SPACES[space] for spac...]
  transfers between devices with their start and end apart: 32 -> 32, of which waited for: 9 -> 12; matrix products, arithmetic and copies ran while one was open for 0% -> 0% of each run, Pallas kernels for 22% -> 20%
where the time goes in v4:
time: 76.3 us; the launch traced here: 75.6 us
  starting transfers between devices  35.1 us (46%)
  Pallas kernels  21 us (28%)
  waiting for transfers between devices  15 us (20%)
  local copies, waits for them, and re-layouts  3.42 us (4%)
  between operations  0.96 us (1%)
    pallas_call x22, Pallas kernels, call(): pl.pallas_call(kernel, out_shape=shapes, in_specs=[SPACES[space] for spac...  21 us
    ppermute x15, starting transfers between devices, along_z(): lax.ppermute(value, 'seq', seq_pairs(lambda y, z, core: (y, (z + distance...  19.5 us
    ppermute x6, starting transfers between devices, onward_y(): return lax.ppermute(value, 'seq', seq_pairs(move))  7.75 us
    ppermute x15, waiting for transfers between devices, along_z(): lax.ppermute(value, 'seq', seq_pairs(lambda y, z, core: (y, (z + distance...  6.01 us
    ppermute x3, starting transfers between devices, local(): lax.ppermute(bc, 'head', [(i, (i + k) % 4) for i in range(4)])  4.44 us
    unnamed x22, local copies, waits for them, and re-layouts  3.42 us
    ppermute x3, waiting for transfers between devices, along_y(): lax.ppermute(value, 'seq', seq_pairs(lambda y, z, core: ((y + distance) %...  3.36 us
    ppermute x6, waiting for transfers between devices, onward_y(): return lax.ppermute(value, 'seq', seq_pairs(move))  2.99 us
  transfers between devices with their start and end apart: 32, of which 12 were waited for; matrix products, arithmetic and copies ran while one was open for 0% of the time, Pallas kernels for 20%

profile of v4, /device:TPU:0, one launch (start us, length us, event | category | flops | bytes accessed | tf_op | source)
XLA Modules:
  0.0 75.6 jit_solution(4193817257735245431)
XLA Ops:
  3.6 3.0 %states.1 = (bf16[128,2048]{1,0:T(8,128)(2,1)S(1)}, f32[6,32,128]{2,1,0:T(8,128)S(1)}, f32[128,128]{1,0:T(8,128)S(1)}, f32[16,128]{1,0:T(8,128)S(1)}, f32[1032,1...) custom-call(s32[3]{0:T(128)S(1)} %pad_add_fusion.place, ...), custom_call_target="tpu_custom_call" | custom-call | flops 65536 | bytes 4096 | tf_op jit(solution)/shard_map/states/pallas_call | solution.py:469
  7.1 1.4 %collective-permute-done.1.recv = f32[1032,128]{1,0:T(8,128)S(1)} collective-permute-done((f32[1032,128]{1,0:T(8,128)S(1)}, f32[1032,128]{1,0:T(8,128)S(1)}, u32[]{:S(2)}, u32[]{:S(2)}) %collective-permute-start.1) | collective-permute-done | bytes 528416 | tf_op jit(solution)/shard_map/ppermute | solution.py:444
  9.2 2.1 %collective-permute-start.2 = (f32[264,128]{1,0:T(8,128)S(1)}, f32[264,128]{1,0:T(8,128)S(1)}, u32[]{:S(2)}, u32[]{:S(2)}) collective-permute-start(f32[264,128]{1,0:T(8,128)S(1)} %get-tuple-element.62), channel_id=1, source_target_pairs={{0,8},{4,12},{8,16},{12,20},{16,24},{20,28},{24,0},{28,4},{32,40},... | collective-permute-start | bytes 405512 | tf_op jit(solution)/shard_map/ppermute | solution.py:448
  11.2 2.2 %collective-permute-start.3 = (f32[264,128]{1,0:T(8,128)S(1)}, f32[264,128]{1,0:T(8,128)S(1)}, u32[]{:S(2)}, u32[]{:S(2)}) collective-permute-start(f32[264,128]{1,0:T(8,128)S(1)} %get-tuple-element.63), channel_id=1, source_target_pairs={{0,24},{4,28},{8,0},{12,4},{16,8},{20,12},{24,16},{28,20},{32,56},... | collective-permute-start | bytes 405512 | tf_op jit(solution)/shard_map/ppermute | solution.py:448
  13.4 1.8 %collective-permute-start.4 = (f32[264,128]{1,0:T(8,128)S(1)}, f32[264,128]{1,0:T(8,128)S(1)}, u32[]{:S(2)}, u32[]{:S(2)}) collective-permute-start(f32[264,128]{1,0:T(8,128)S(1)} %get-tuple-element.64), channel_id=1, source_target_pairs={{0,16},{4,20},{8,24},{12,28},{16,0},{20,4},{24,8},{28,12},{32,48},... | collective-permute-start | bytes 405512 | tf_op jit(solution)/shard_map/ppermute | solution.py:448
  16.9 2.2 %collective-permute-start.12 = (f32[264,128]{1,0:T(8,128)S(1)}, f32[264,128]{1,0:T(8,128)S(1)}, u32[]{:S(2)}, u32[]{:S(2)}) collective-permute-start(f32[264,128]{1,0:T(8,128)S(1)} %get-tuple-element.71), channel_id=1, source_target_pairs={{0,24},{4,28},{8,0},{12,4},{16,8},{20,12},{24,16},{28,20},{32,56},... | collective-permute-start | bytes 405512 | tf_op jit(solution)/shard_map/ppermute | solution.py:448
  19.8 2.8 %within.2 = (f32[128,1024]{1,0:T(8,128)S(1)}, f32[2,16,128]{2,1,0:T(8,128)S(1)}, f32[2,128,128]{2,1,0:T(8,128)S(1)}, f32[1024,128]{1,0:T(8,128)S(1)}, f32[1024,128]{1,0:T(8,128)S(1)}, /*index=5*/f32[16,128]{1,0:T(8,128)S(1)}) custom-call(s32[1,2]{1,0:T(1,128)S(1)} %copy-done.7, f32[32]{0:T(128)S(1)} %copy-done.9, bf16[128,2048]{1,0:T(8,128)(2,1)S(1)} %get-tuple-element.52.x, ...), custom_call_target="tpu_custom_call" | custom-call | flops 65536 | bytes 4096 | tf_op jit(solution)/shard_map/within/pallas_call | solution.py:469
  23.9 1.3 %collective-permute-start.7 = (f32[264,128]{1,0:T(8,128)S(1)}, f32[264,128]{1,0:T(8,128)S(1)}, u32[]{:S(2)}, u32[]{:S(2)}) collective-permute-start(f32[264,128]{1,0:T(8,128)S(1)} %row_total.2), channel_id=1, source_target_pairs={{4,68},{12,76},{20,84},{28,92},{36,100},{44,108},{52,116},{60,124}... | collective-permute-start | bytes 405512 | tf_op jit(solution)/shard_map/ppermute | solution.py:464
  25.2 1.3 %collective-permute-start.6 = (f32[264,128]{1,0:T(8,128)S(1)}, f32[264,128]{1,0:T(8,128)S(1)}, u32[]{:S(2)}, u32[]{:S(2)}) collective-permute-start(f32[264,128]{1,0:T(8,128)S(1)} %row_total.2), channel_id=1, source_target_pairs={{4,100},{12,108},{20,116},{28,124},{96,0},{104,8},{112,16},{120,24... | collective-permute-start | bytes 405512 | tf_op jit(solution)/shard_map/ppermute | solution.py:464
  26.5 1.3 %collective-permute-start.5 = (f32[264,128]{1,0:T(8,128)S(1)}, f32[264,128]{1,0:T(8,128)S(1)}, u32[]{:S(2)}, u32[]{:S(2)}) collective-permute-start(f32[264,128]{1,0:T(8,128)S(1)} %row_total.2), channel_id=1, source_target_pairs={{4,36},{12,44},{20,52},{28,60},{32,0},{36,68},{40,8},{44,76},{48,1... | collective-permute-start | bytes 405512 | tf_op jit(solution)/shard_map/ppermute | solution.py:464
  27.8 1.4 %collective-permute-done.13.refs_2_.refs_6_ = f32[264,128]{1,0:T(8,128)S(1)} collective-permute-done((f32[264,128]{1,0:T(8,128)S(1)}, f32[264,128]{1,0:T(8,128)S(1)}, u32[]{:S(2)}, u32[]{:S(2)}) %collective-permute-start.13) | collective-permute-done | bytes 135200 | tf_op jit(solution)/shard_map/ppermute | solution.py:448
  29.8 1.3 %collective-permute-start.16 = (f32[264,128]{1,0:T(8,128)S(1)}, f32[264,128]{1,0:T(8,128)S(1)}, u32[]{:S(2)}, u32[]{:S(2)}) collective-permute-start(f32[264,128]{1,0:T(8,128)S(1)} %row_total.3), channel_id=1, source_target_pairs={{4,68},{12,76},{20,84},{28,92},{36,100},{44,108},{52,116},{60,124}... | collective-permute-start | bytes 405512 | tf_op jit(solution)/shard_map/ppermute | solution.py:464
  31.1 1.3 %collective-permute-start.15 = (f32[264,128]{1,0:T(8,128)S(1)}, f32[264,128]{1,0:T(8,128)S(1)}, u32[]{:S(2)}, u32[]{:S(2)}) collective-permute-start(f32[264,128]{1,0:T(8,128)S(1)} %row_total.3), channel_id=1, source_target_pairs={{4,100},{12,108},{20,116},{28,124},{96,0},{104,8},{112,16},{120,24... | collective-permute-start | bytes 405512 | tf_op jit(solution)/shard_map/ppermute | solution.py:464
  32.4 1.3 %collective-permute-start.14 = (f32[264,128]{1,0:T(8,128)S(1)}, f32[264,128]{1,0:T(8,128)S(1)}, u32[]{:S(2)}, u32[]{:S(2)}) collective-permute-start(f32[264,128]{1,0:T(8,128)S(1)} %row_total.3), channel_id=1, source_target_pairs={{4,36},{12,44},{20,52},{28,60},{32,0},{36,68},{40,8},{44,76},{48,1... | collective-permute-start | bytes 405512 | tf_op jit(solution)/shard_map/ppermute | solution.py:464
  35.0 2.0 %collective-permute-start.8 = (f32[256,128]{1,0:T(8,128)S(1)}, f32[256,128]{1,0:T(8,128)S(1)}, u32[]{:S(2)}, u32[]{:S(2)}) collective-permute-start(f32[256,128]{1,0:T(8,128)S(1)} %get-tuple-element.66), channel_id=1, source_target_pairs={{0,24},{4,28},{8,0},{12,4},{16,8},{20,12},{24,16},{28,20},{32,56},... | collective-permute-start | bytes 393224 | tf_op jit(solution)/shard_map/ppermute | solution.py:448
  38.2 1.3 %collective-permute-done.16.refs_2_ = f32[264,128]{1,0:T(8,128)S(1)} collective-permute-done((f32[264,128]{1,0:T(8,128)S(1)}, f32[264,128]{1,0:T(8,128)S(1)}, u32[]{:S(2)}, u32[]{:S(2)}) %collective-permute-start.16) | collective-permute-done | bytes 135200 | tf_op jit(solution)/shard_map/ppermute | solution.py:464
  41.4 2.2 %collective-permute-start.18 = (f32[256,128]{1,0:T(8,128)S(1)}, f32[256,128]{1,0:T(8,128)S(1)}, u32[]{:S(2)}, u32[]{:S(2)}) collective-permute-start(f32[256,128]{1,0:T(8,128)S(1)} %get-tuple-element.81), channel_id=1, source_target_pairs={{0,24},{4,28},{8,0},{12,4},{16,8},{20,12},{24,16},{28,20},{32,56},... | collective-permute-start | bytes 393224 | tf_op jit(solution)/shard_map/ppermute | solution.py:448
  43.8 1.3 %collective-permute-start.20 = (f32[256,128]{1,0:T(8,128)S(1)}, f32[256,128]{1,0:T(8,128)S(1)}, u32[]{:S(2)}, u32[]{:S(2)}) collective-permute-start(f32[256,128]{1,0:T(8,128)S(1)} %get-tuple-element.83), channel_id=1, source_target_pairs={{0,8},{4,12},{8,16},{12,20},{16,24},{20,28},{24,0},{28,4},{32,40},... | collective-permute-start | bytes 393224 | tf_op jit(solution)/shard_map/ppermute | solution.py:448
  45.1 2.8 %within.3 = (f32[128,1024]{1,0:T(8,128)S(1)}, f32[2,16,128]{2,1,0:T(8,128)S(1)}, f32[2,128,128]{2,1,0:T(8,128)S(1)}, f32[1024,128]{1,0:T(8,128)S(1)}, f32[1024,128]{1,0:T(8,128)S(1)}, /*index=5*/f32[16,128]{1,0:T(8,128)S(1)}) custom-call(s32[1,2]{1,0:T(1,128)S(1)} %copy-done.7, f32[32]{0:T(128)S(1)} %copy-done.9, bf16[128,2048]{1,0:T(8,128)(2,1)S(1)} %get-tuple-element.52.x, ...), custom_call_target="tpu_custom_call" | custom-call | flops 65536 | bytes 4096 | tf_op jit(solution)/shard_map/within/pallas_call | solution.py:469
  49.4 2.1 %collective-permute-done.19.refs_2_ = f32[256,128]{1,0:T(8,128)S(1)} collective-permute-done((f32[256,128]{1,0:T(8,128)S(1)}, f32[256,128]{1,0:T(8,128)S(1)}, u32[]{:S(2)}, u32[]{:S(2)}) %collective-permute-start.19) | collective-permute-done | bytes 131104 | tf_op jit(solution)/shard_map/ppermute | solution.py:448
  51.5 1.8 %collective-permute-done.20.refs_3_ = f32[256,128]{1,0:T(8,128)S(1)} collective-permute-done((f32[256,128]{1,0:T(8,128)S(1)}, f32[256,128]{1,0:T(8,128)S(1)}, u32[]{:S(2)}, u32[]{:S(2)}) %collective-permute-start.20) | collective-permute-done | bytes 131104 | tf_op jit(solution)/shard_map/ppermute | solution.py:448
  61.6 2.8 %collective-permute-start.31 = (f32[2,128,128]{2,1,0:T(8,128)S(1)}, f32[2,128,128]{2,1,0:T(8,128)S(1)}, u32[]{:S(2)}, u32[]{:S(2)}) collective-permute-start(f32[2,128,128]{2,1,0:T(8,128)S(1)} %sums.3.refs_0_.refs_1_.refs_2_.bc), channel_id=1, source_target_pairs={{0,3},{1,0},{2,1},{3,2},{4,7},{5,4},{6,5},{7,6},{8,11},{9,8},{10,9... | collective-permute-start | bytes 393224 | tf_op jit(solution)/shard_map/ppermute | solution.py:628
  68.3 1.7 %collective-permute-done.28.three = f32[32,128]{1,0:T(8,128)S(1)} collective-permute-done((f32[32,128]{1,0:T(8,128)S(1)}, f32[32,128]{1,0:T(8,128)S(1)}, u32[]{:S(2)}, u32[]{:S(2)}) %collective-permute-start.28) | collective-permute-done | bytes 16416 | tf_op jit(solution)/shard_map/ppermute | solution.py:454
  73.2 1.7 %collective-permute-done.26.one = f32[32,128]{1,0:T(8,128)S(1)} collective-permute-done((f32[32,128]{1,0:T(8,128)S(1)}, f32[32,128]{1,0:T(8,128)S(1)}, u32[]{:S(2)}, u32[]{:S(2)}) %collective-permute-start.26) | collective-permute-done | bytes 16416 | tf_op jit(solution)/shard_map/ppermute | solution.py:454
  (86 shorter events, 30.3 us)
Async XLA Ops:
  6.6 8.6 %collective-permute-start = (f32[1032,128]{1,0:T(8,128)S(1)}, f32[1032,128]{1,0:T(8,128)S(1)}, u32[]{:S(2)}, u32[]{:S(2)}) collective-permute-start(f32[1032,128]{1,0:T(8,128)S(1)} %get-tuple-element.56), channel_id=1, source_target_pairs={{0,4},{4,0},{8,12},{12,8},{16,20},{20,16},{24,28},{28,24},{32,36},... | collective-permute-start | bytes 1585160 | tf_op jit(solution)/shard_map/ppermute | solution.py:444
  9.2 13.5 %collective-permute-start.2 = (f32[264,128]{1,0:T(8,128)S(1)}, f32[264,128]{1,0:T(8,128)S(1)}, u32[]{:S(2)}, u32[]{:S(2)}) collective-permute-start(f32[264,128]{1,0:T(8,128)S(1)} %get-tuple-element.62), channel_id=1, source_target_pairs={{0,8},{4,12},{8,16},{12,20},{16,24},{20,28},{24,0},{28,4},{32,40},... | collective-permute-start | bytes 405512 | tf_op jit(solution)/shard_map/ppermute | solution.py:448
  11.2 12.0 %collective-permute-start.3 = (f32[264,128]{1,0:T(8,128)S(1)}, f32[264,128]{1,0:T(8,128)S(1)}, u32[]{:S(2)}, u32[]{:S(2)}) collective-permute-start(f32[264,128]{1,0:T(8,128)S(1)} %get-tuple-element.63), channel_id=1, source_target_pairs={{0,24},{4,28},{8,0},{12,4},{16,8},{20,12},{24,16},{28,20},{32,56},... | collective-permute-start | bytes 405512 | tf_op jit(solution)/shard_map/ppermute | solution.py:448
  13.4 9.8 %collective-permute-start.4 = (f32[264,128]{1,0:T(8,128)S(1)}, f32[264,128]{1,0:T(8,128)S(1)}, u32[]{:S(2)}, u32[]{:S(2)}) collective-permute-start(f32[264,128]{1,0:T(8,128)S(1)} %get-tuple-element.64), channel_id=1, source_target_pairs={{0,16},{4,20},{8,24},{12,28},{16,0},{20,4},{24,8},{28,12},{32,48},... | collective-permute-start | bytes 405512 | tf_op jit(solution)/shard_map/ppermute | solution.py:448
  15.8 10.6 %collective-permute-start.11 = (f32[264,128]{1,0:T(8,128)S(1)}, f32[264,128]{1,0:T(8,128)S(1)}, u32[]{:S(2)}, u32[]{:S(2)}) collective-permute-start(f32[264,128]{1,0:T(8,128)S(1)} %get-tuple-element.70), channel_id=1, source_target_pairs={{0,8},{4,12},{8,16},{12,20},{16,24},{20,28},{24,0},{28,4},{32,40},... | collective-permute-start | bytes 405512 | tf_op jit(solution)/shard_map/ppermute | solution.py:448
  16.9 10.8 %collective-permute-start.12 = (f32[264,128]{1,0:T(8,128)S(1)}, f32[264,128]{1,0:T(8,128)S(1)}, u32[]{:S(2)}, u32[]{:S(2)}) collective-permute-start(f32[264,128]{1,0:T(8,128)S(1)} %get-tuple-element.71), channel_id=1, source_target_pairs={{0,24},{4,28},{8,0},{12,4},{16,8},{20,12},{24,16},{28,20},{32,56},... | collective-permute-start | bytes 405512 | tf_op jit(solution)/shard_map/ppermute | solution.py:448
  22.6 6.6 %collective-permute-start.13 = (f32[264,128]{1,0:T(8,128)S(1)}, f32[264,128]{1,0:T(8,128)S(1)}, u32[]{:S(2)}, u32[]{:S(2)}) collective-permute-start(f32[264,128]{1,0:T(8,128)S(1)} %get-tuple-element.72), channel_id=1, source_target_pairs={{0,16},{4,20},{8,24},{12,28},{16,0},{20,4},{24,8},{28,12},{32,48},... | collective-permute-start | bytes 405512 | tf_op jit(solution)/shard_map/ppermute | solution.py:448
  23.9 8.6 %collective-permute-start.7 = (f32[264,128]{1,0:T(8,128)S(1)}, f32[264,128]{1,0:T(8,128)S(1)}, u32[]{:S(2)}, u32[]{:S(2)}) collective-permute-start(f32[264,128]{1,0:T(8,128)S(1)} %row_total.2), channel_id=1, source_target_pairs={{4,68},{12,76},{20,84},{28,92},{36,100},{44,108},{52,116},{60,124}... | collective-permute-start | bytes 405512 | tf_op jit(solution)/shard_map/ppermute | solution.py:464
  25.2 9.1 %collective-permute-start.6 = (f32[264,128]{1,0:T(8,128)S(1)}, f32[264,128]{1,0:T(8,128)S(1)}, u32[]{:S(2)}, u32[]{:S(2)}) collective-permute-start(f32[264,128]{1,0:T(8,128)S(1)} %row_total.2), channel_id=1, source_target_pairs={{4,100},{12,108},{20,116},{28,124},{96,0},{104,8},{112,16},{120,24... | collective-permute-start | bytes 405512 | tf_op jit(solution)/shard_map/ppermute | solution.py:464
  26.5 7.8 %collective-permute-start.5 = (f32[264,128]{1,0:T(8,128)S(1)}, f32[264,128]{1,0:T(8,128)S(1)}, u32[]{:S(2)}, u32[]{:S(2)}) collective-permute-start(f32[264,128]{1,0:T(8,128)S(1)} %row_total.2), channel_id=1, source_target_pairs={{4,36},{12,44},{20,52},{28,60},{32,0},{36,68},{40,8},{44,76},{48,1... | collective-permute-start | bytes 405512 | tf_op jit(solution)/shard_map/ppermute | solution.py:464
  29.8 9.7 %collective-permute-start.16 = (f32[264,128]{1,0:T(8,128)S(1)}, f32[264,128]{1,0:T(8,128)S(1)}, u32[]{:S(2)}, u32[]{:S(2)}) collective-permute-start(f32[264,128]{1,0:T(8,128)S(1)} %row_total.3), channel_id=1, source_target_pairs={{4,68},{12,76},{20,84},{28,92},{36,100},{44,108},{52,116},{60,124}... | collective-permute-start | bytes 405512 | tf_op jit(solution)/shard_map/ppermute | solution.py:464
  31.1 9.5 %collective-permute-start.15 = (f32[264,128]{1,0:T(8,128)S(1)}, f32[264,128]{1,0:T(8,128)S(1)}, u32[]{:S(2)}, u32[]{:S(2)}) collective-permute-start(f32[264,128]{1,0:T(8,128)S(1)} %row_total.3), channel_id=1, source_target_pairs={{4,100},{12,108},{20,116},{28,124},{96,0},{104,8},{112,16},{120,24... | collective-permute-start | bytes 405512 | tf_op jit(solution)/shard_map/ppermute | solution.py:464
  32.4 8.2 %collective-permute-start.14 = (f32[264,128]{1,0:T(8,128)S(1)}, f32[264,128]{1,0:T(8,128)S(1)}, u32[]{:S(2)}, u32[]{:S(2)}) collective-permute-start(f32[264,128]{1,0:T(8,128)S(1)} %row_total.3), channel_id=1, source_target_pairs={{4,36},{12,44},{20,52},{28,60},{32,0},{36,68},{40,8},{44,76},{48,1... | collective-permute-start | bytes 405512 | tf_op jit(solution)/shard_map/ppermute | solution.py:464
  35.0 8.8 %collective-permute-start.8 = (f32[256,128]{1,0:T(8,128)S(1)}, f32[256,128]{1,0:T(8,128)S(1)}, u32[]{:S(2)}, u32[]{:S(2)}) collective-permute-start(f32[256,128]{1,0:T(8,128)S(1)} %get-tuple-element.66), channel_id=1, source_target_pairs={{0,24},{4,28},{8,0},{12,4},{16,8},{20,12},{24,16},{28,20},{32,56},... | collective-permute-start | bytes 393224 | tf_op jit(solution)/shard_map/ppermute | solution.py:448
  37.0 10.9 %collective-permute-start.9 = (f32[256,128]{1,0:T(8,128)S(1)}, f32[256,128]{1,0:T(8,128)S(1)}, u32[]{:S(2)}, u32[]{:S(2)}) collective-permute-start(f32[256,128]{1,0:T(8,128)S(1)} %get-tuple-element.68), channel_id=1, source_target_pairs={{0,16},{4,20},{8,24},{12,28},{16,0},{20,4},{24,8},{28,12},{32,48},... | collective-permute-start | bytes 393224 | tf_op jit(solution)/shard_map/ppermute | solution.py:448
  39.5 8.4 %collective-permute-start.10 = (f32[256,128]{1,0:T(8,128)S(1)}, f32[256,128]{1,0:T(8,128)S(1)}, u32[]{:S(2)}, u32[]{:S(2)}) collective-permute-start(f32[256,128]{1,0:T(8,128)S(1)} %get-tuple-element.69), channel_id=1, source_target_pairs={{0,8},{4,12},{8,16},{12,20},{16,24},{20,28},{24,0},{28,4},{32,40},... | collective-permute-start | bytes 393224 | tf_op jit(solution)/shard_map/ppermute | solution.py:448
  41.4 8.0 %collective-permute-start.18 = (f32[256,128]{1,0:T(8,128)S(1)}, f32[256,128]{1,0:T(8,128)S(1)}, u32[]{:S(2)}, u32[]{:S(2)}) collective-permute-start(f32[256,128]{1,0:T(8,128)S(1)} %get-tuple-element.81), channel_id=1, source_target_pairs={{0,24},{4,28},{8,0},{12,4},{16,8},{20,12},{24,16},{28,20},{32,56},... | collective-permute-start | bytes 393224 | tf_op jit(solution)/shard_map/ppermute | solution.py:448
  43.6 7.9 %collective-permute-start.19 = (f32[256,128]{1,0:T(8,128)S(1)}, f32[256,128]{1,0:T(8,128)S(1)}, u32[]{:S(2)}, u32[]{:S(2)}) collective-permute-start(f32[256,128]{1,0:T(8,128)S(1)} %get-tuple-element.82), channel_id=1, source_target_pairs={{0,16},{4,20},{8,24},{12,28},{16,0},{20,4},{24,8},{28,12},{32,48},... | collective-permute-start | bytes 393224 | tf_op jit(solution)/shard_map/ppermute | solution.py:448
  43.8 9.5 %collective-permute-start.20 = (f32[256,128]{1,0:T(8,128)S(1)}, f32[256,128]{1,0:T(8,128)S(1)}, u32[]{:S(2)}, u32[]{:S(2)}) collective-permute-start(f32[256,128]{1,0:T(8,128)S(1)} %get-tuple-element.83), channel_id=1, source_target_pairs={{0,8},{4,12},{8,16},{12,20},{16,24},{20,28},{24,0},{28,4},{32,40},... | collective-permute-start | bytes 393224 | tf_op jit(solution)/shard_map/ppermute | solution.py:448
  59.1 6.1 %collective-permute-start.25 = (f32[32,128]{1,0:T(8,128)S(1)}, f32[32,128]{1,0:T(8,128)S(1)}, u32[]{:S(2)}, u32[]{:S(2)}) collective-permute-start(f32[32,128]{1,0:T(8,128)S(1)} %chip_heads.1), channel_id=1, source_target_pairs={{0,24},{4,28},{8,0},{12,4},{16,8},{20,12},{24,16},{28,20},{32,56},... | collective-permute-start | bytes 49160 | tf_op jit(solution)/shard_map/ppermute | solution.py:448
  59.6 6.5 %collective-permute-start.24 = (f32[32,128]{1,0:T(8,128)S(1)}, f32[32,128]{1,0:T(8,128)S(1)}, u32[]{:S(2)}, u32[]{:S(2)}) collective-permute-start(f32[32,128]{1,0:T(8,128)S(1)} %chip_heads.1), channel_id=1, source_target_pairs={{0,16},{4,20},{8,24},{12,28},{16,0},{20,4},{24,8},{28,12},{32,48},... | collective-permute-start | bytes 49160 | tf_op jit(solution)/shard_map/ppermute | solution.py:448
  61.6 13.2 %collective-permute-start.31 = (f32[2,128,128]{2,1,0:T(8,128)S(1)}, f32[2,128,128]{2,1,0:T(8,128)S(1)}, u32[]{:S(2)}, u32[]{:S(2)}) collective-permute-start(f32[2,128,128]{2,1,0:T(8,128)S(1)} %sums.3.refs_0_.refs_1_.refs_2_.bc), channel_id=1, source_target_pairs={{0,3},{1,0},{2,1},{3,2},{4,7},{5,4},{6,5},{7,6},{8,11},{9,8},{10,9... | collective-permute-start | bytes 393224 | tf_op jit(solution)/shard_map/ppermute | solution.py:628
  64.4 10.5 %collective-permute-start.30 = (f32[2,128,128]{2,1,0:T(8,128)S(1)}, f32[2,128,128]{2,1,0:T(8,128)S(1)}, u32[]{:S(2)}, u32[]{:S(2)}) collective-permute-start(f32[2,128,128]{2,1,0:T(8,128)S(1)} %sums.3.refs_0_.refs_1_.refs_2_.bc), channel_id=1, source_target_pairs={{0,2},{1,3},{2,0},{3,1},{4,6},{5,7},{6,4},{7,5},{8,10},{9,11},{10,... | collective-permute-start | bytes 393224 | tf_op jit(solution)/shard_map/ppermute | solution.py:628
  65.2 9.7 %collective-permute-start.29 = (f32[2,128,128]{2,1,0:T(8,128)S(1)}, f32[2,128,128]{2,1,0:T(8,128)S(1)}, u32[]{:S(2)}, u32[]{:S(2)}) collective-permute-start(f32[2,128,128]{2,1,0:T(8,128)S(1)} %sums.3.refs_0_.refs_1_.refs_2_.bc), channel_id=1, source_target_pairs={{0,1},{1,2},{2,3},{3,0},{4,5},{5,6},{6,7},{7,4},{8,9},{9,10},{10,1... | collective-permute-start | bytes 393224 | tf_op jit(solution)/shard_map/ppermute | solution.py:628
  (19 other events, 42.3 us)

commit v5 on v4

--- a/solution.py
+++ b/solution.py
@@ -23,9 +23,9 @@
 VMEM = pl.BlockSpec(memory_space=pltpu.VMEM)
 SMEM = pl.BlockSpec(memory_space=pltpu.SMEM)
 ORDER_ROW = (3, 1, 2, 0)
-ORDER_ENTRY = (3, 0, 1, 2)
-ORDER_ASSEMBLE = (1, 0, 2, 3)
-ORDER_Y = (0, 2, 1)
+ORDER_ENTRY = (3, 2, 1, 0)
+ORDER_ASSEMBLE = (2, 1, 3, 0)
+ORDER_Y = (0, 1, 2)
 ANY = pl.BlockSpec(memory_space=pl.ANY)
 SPACES = (VMEM, SMEM, ANY)
 VMEM_LIMIT = 24 << 20
@@ -610,8 +610,7 @@
         (heads,) = call(
             functools.partial(logs_kernel, part),
             [(0, v) for v in [u, w, kappa, start, entry, leave]]
-            + ([(0, heads)] if part else [])
-            + [(2, bc)],
+            + ([(0, heads)] if part else []),
             [((2 * PART_PAIRS * (part + 1), 128), F32)],
             "logs",
         )

time: 76.3 us -> 75.4 us (0.988)
  waiting for transfers between devices: 15 us -> 9.93 us
  starting transfers between devices: 35.1 us -> 39.3 us
    ppermute x15, waiting for transfers between devices: 6.01 us -> 2.52 us  [along_z(): lax.ppermute(value, 'seq', seq_pairs(lambda y, z, core: (y, (z + distance...]
    ppermute x15, starting transfers between devices: 19.5 us -> 22.9 us  [along_z(): lax.ppermute(value, 'seq', seq_pairs(lambda y, z, core: (y, (z + distance...]
    ppermute x5, waiting for transfers between devices: 2.66 us -> 1.56 us  [other_core(): lax.ppermute(value, 'seq', seq_pairs(lambda y, z, core: (y, z, 1 - core)))]
  transfers between devices with their start and end apart: 32 -> 32, of which waited for: 12 -> 9; matrix products, arithmetic and copies ran while one was open for 0% -> 0% of each run, Pallas kernels for 20% -> 22%
where the time goes in v5:
time: 75.4 us; the launch traced here: 74.8 us
  starting transfers between devices  39.3 us (52%)
  Pallas kernels  21.1 us (28%)
  waiting for transfers between devices  9.93 us (13%)
  local copies, waits for them, and re-layouts  3.42 us (5%)
  between operations  0.99 us (1%)
    ppermute x15, starting transfers between devices, along_z(): lax.ppermute(value, 'seq', seq_pairs(lambda y, z, core: (y, (z + distance...  22.9 us
    pallas_call x22, Pallas kernels, call(): pl.pallas_call(kernel, out_shape=shapes, in_specs=[SPACES[space] for spac...  21.1 us
    ppermute x6, starting transfers between devices, onward_y(): return lax.ppermute(value, 'seq', seq_pairs(move))  7.74 us
    ppermute x3, starting transfers between devices, local(): lax.ppermute(bc, 'head', [(i, (i + k) % 4) for i in range(4)])  4.44 us
    unnamed x22, local copies, waits for them, and re-layouts  3.42 us
    ppermute x6, waiting for transfers between devices, onward_y(): return lax.ppermute(value, 'seq', seq_pairs(move))  3.09 us
    ppermute x3, starting transfers between devices, along_y(): lax.ppermute(value, 'seq', seq_pairs(lambda y, z, core: ((y + distance) %...  2.88 us
    ppermute x3, waiting for transfers between devices, along_y(): lax.ppermute(value, 'seq', seq_pairs(lambda y, z, core: ((y + distance) %...  2.75 us
  transfers between devices with their start and end apart: 32, of which 9 were waited for; matrix products, arithmetic and copies ran while one was open for 0% of the time, Pallas kernels for 22%

profile of v5, /device:TPU:0, one launch (start us, length us, event | category | flops | bytes accessed | tf_op | source)
XLA Modules:
  0.0 74.8 jit_solution(15563814288066012199)
XLA Ops:
  3.6 3.0 %states.1 = (bf16[128,2048]{1,0:T(8,128)(2,1)S(1)}, f32[6,32,128]{2,1,0:T(8,128)S(1)}, f32[128,128]{1,0:T(8,128)S(1)}, f32[16,128]{1,0:T(8,128)S(1)}, f32[1032,1...) custom-call(s32[3]{0:T(128)S(1)} %pad_add_fusion.place, ...), custom_call_target="tpu_custom_call" | custom-call | flops 65536 | bytes 4096 | tf_op jit(solution)/shard_map/states/pallas_call | solution.py:469
  7.1 1.4 %collective-permute-done.1.recv = f32[1032,128]{1,0:T(8,128)S(1)} collective-permute-done((f32[1032,128]{1,0:T(8,128)S(1)}, f32[1032,128]{1,0:T(8,128)S(1)}, u32[]{:S(2)}, u32[]{:S(2)}) %collective-permute-start.1) | collective-permute-done | bytes 528416 | tf_op jit(solution)/shard_map/ppermute | solution.py:444
  9.2 2.1 %collective-permute-start.2 = (f32[264,128]{1,0:T(8,128)S(1)}, f32[264,128]{1,0:T(8,128)S(1)}, u32[]{:S(2)}, u32[]{:S(2)}) collective-permute-start(f32[264,128]{1,0:T(8,128)S(1)} %get-tuple-element.62), channel_id=1, source_target_pairs={{0,8},{4,12},{8,16},{12,20},{16,24},{20,28},{24,0},{28,4},{32,40},... | collective-permute-start | bytes 405512 | tf_op jit(solution)/shard_map/ppermute | solution.py:448
  11.2 2.2 %collective-permute-start.3 = (f32[264,128]{1,0:T(8,128)S(1)}, f32[264,128]{1,0:T(8,128)S(1)}, u32[]{:S(2)}, u32[]{:S(2)}) collective-permute-start(f32[264,128]{1,0:T(8,128)S(1)} %get-tuple-element.63), channel_id=1, source_target_pairs={{0,24},{4,28},{8,0},{12,4},{16,8},{20,12},{24,16},{28,20},{32,56},... | collective-permute-start | bytes 405512 | tf_op jit(solution)/shard_map/ppermute | solution.py:448
  13.4 1.8 %collective-permute-start.4 = (f32[264,128]{1,0:T(8,128)S(1)}, f32[264,128]{1,0:T(8,128)S(1)}, u32[]{:S(2)}, u32[]{:S(2)}) collective-permute-start(f32[264,128]{1,0:T(8,128)S(1)} %get-tuple-element.64), channel_id=1, source_target_pairs={{0,16},{4,20},{8,24},{12,28},{16,0},{20,4},{24,8},{28,12},{32,48},... | collective-permute-start | bytes 405512 | tf_op jit(solution)/shard_map/ppermute | solution.py:448
  16.9 2.2 %collective-permute-start.12 = (f32[264,128]{1,0:T(8,128)S(1)}, f32[264,128]{1,0:T(8,128)S(1)}, u32[]{:S(2)}, u32[]{:S(2)}) collective-permute-start(f32[264,128]{1,0:T(8,128)S(1)} %get-tuple-element.71), channel_id=1, source_target_pairs={{0,24},{4,28},{8,0},{12,4},{16,8},{20,12},{24,16},{28,20},{32,56},... | collective-permute-start | bytes 405512 | tf_op jit(solution)/shard_map/ppermute | solution.py:448
  20.4 2.8 %within.2 = (f32[128,1024]{1,0:T(8,128)S(1)}, f32[2,16,128]{2,1,0:T(8,128)S(1)}, f32[2,128,128]{2,1,0:T(8,128)S(1)}, f32[1024,128]{1,0:T(8,128)S(1)}, f32[1024,128]{1,0:T(8,128)S(1)}, /*index=5*/f32[16,128]{1,0:T(8,128)S(1)}) custom-call(s32[1,2]{1,0:T(1,128)S(1)} %copy-done.7, f32[32]{0:T(128)S(1)} %copy-done.9, bf16[128,2048]{1,0:T(8,128)(2,1)S(1)} %get-tuple-element.52.x, ...), custom_call_target="tpu_custom_call" | custom-call | flops 65536 | bytes 4096 | tf_op jit(solution)/shard_map/within/pallas_call | solution.py:469
  23.8 1.3 %collective-permute-start.7 = (f32[264,128]{1,0:T(8,128)S(1)}, f32[264,128]{1,0:T(8,128)S(1)}, u32[]{:S(2)}, u32[]{:S(2)}) collective-permute-start(f32[264,128]{1,0:T(8,128)S(1)} %row_total.2), channel_id=1, source_target_pairs={{4,100},{12,108},{20,116},{28,124},{96,0},{104,8},{112,16},{120,24... | collective-permute-start | bytes 405512 | tf_op jit(solution)/shard_map/ppermute | solution.py:464
  25.1 1.3 %collective-permute-start.6 = (f32[264,128]{1,0:T(8,128)S(1)}, f32[264,128]{1,0:T(8,128)S(1)}, u32[]{:S(2)}, u32[]{:S(2)}) collective-permute-start(f32[264,128]{1,0:T(8,128)S(1)} %row_total.2), channel_id=1, source_target_pairs={{4,68},{12,76},{20,84},{28,92},{36,100},{44,108},{52,116},{60,124}... | collective-permute-start | bytes 405512 | tf_op jit(solution)/shard_map/ppermute | solution.py:464
  26.4 1.3 %collective-permute-start.5 = (f32[264,128]{1,0:T(8,128)S(1)}, f32[264,128]{1,0:T(8,128)S(1)}, u32[]{:S(2)}, u32[]{:S(2)}) collective-permute-start(f32[264,128]{1,0:T(8,128)S(1)} %row_total.2), channel_id=1, source_target_pairs={{4,36},{12,44},{20,52},{28,60},{32,0},{36,68},{40,8},{44,76},{48,1... | collective-permute-start | bytes 405512 | tf_op jit(solution)/shard_map/ppermute | solution.py:464
  28.3 1.3 %collective-permute-start.16 = (f32[264,128]{1,0:T(8,128)S(1)}, f32[264,128]{1,0:T(8,128)S(1)}, u32[]{:S(2)}, u32[]{:S(2)}) collective-permute-start(f32[264,128]{1,0:T(8,128)S(1)} %row_total.3), channel_id=1, source_target_pairs={{4,100},{12,108},{20,116},{28,124},{96,0},{104,8},{112,16},{120,24... | collective-permute-start | bytes 405512 | tf_op jit(solution)/shard_map/ppermute | solution.py:464
  29.6 1.3 %collective-permute-start.15 = (f32[264,128]{1,0:T(8,128)S(1)}, f32[264,128]{1,0:T(8,128)S(1)}, u32[]{:S(2)}, u32[]{:S(2)}) collective-permute-start(f32[264,128]{1,0:T(8,128)S(1)} %row_total.3), channel_id=1, source_target_pairs={{4,68},{12,76},{20,84},{28,92},{36,100},{44,108},{52,116},{60,124}... | collective-permute-start | bytes 405512 | tf_op jit(solution)/shard_map/ppermute | solution.py:464
  33.2 1.7 %collective-permute-done.6.refs_1_ = f32[264,128]{1,0:T(8,128)S(1)} collective-permute-done((f32[264,128]{1,0:T(8,128)S(1)}, f32[264,128]{1,0:T(8,128)S(1)}, u32[]{:S(2)}, u32[]{:S(2)}) %collective-permute-start.6) | collective-permute-done | bytes 135200 | tf_op jit(solution)/shard_map/ppermute | solution.py:464
  35.7 2.8 %collective-permute-start.8 = (f32[256,128]{1,0:T(8,128)S(1)}, f32[256,128]{1,0:T(8,128)S(1)}, u32[]{:S(2)}, u32[]{:S(2)}) collective-permute-start(f32[256,128]{1,0:T(8,128)S(1)} %get-tuple-element.66), channel_id=1, source_target_pairs={{0,16},{4,20},{8,24},{12,28},{16,0},{20,4},{24,8},{28,12},{32,48},... | collective-permute-start | bytes 393224 | tf_op jit(solution)/shard_map/ppermute | solution.py:448
  41.3 2.3 %collective-permute-start.18 = (f32[256,128]{1,0:T(8,128)S(1)}, f32[256,128]{1,0:T(8,128)S(1)}, u32[]{:S(2)}, u32[]{:S(2)}) collective-permute-start(f32[256,128]{1,0:T(8,128)S(1)} %get-tuple-element.81), channel_id=1, source_target_pairs={{0,16},{4,20},{8,24},{12,28},{16,0},{20,4},{24,8},{28,12},{32,48},... | collective-permute-start | bytes 393224 | tf_op jit(solution)/shard_map/ppermute | solution.py:448
  43.6 2.2 %collective-permute-start.19 = (f32[256,128]{1,0:T(8,128)S(1)}, f32[256,128]{1,0:T(8,128)S(1)}, u32[]{:S(2)}, u32[]{:S(2)}) collective-permute-start(f32[256,128]{1,0:T(8,128)S(1)} %get-tuple-element.82), channel_id=1, source_target_pairs={{0,24},{4,28},{8,0},{12,4},{16,8},{20,12},{24,16},{28,20},{32,56},... | collective-permute-start | bytes 393224 | tf_op jit(solution)/shard_map/ppermute | solution.py:448
  45.8 1.6 %collective-permute-done.10.refs_2_ = f32[256,128]{1,0:T(8,128)S(1)} collective-permute-done((f32[256,128]{1,0:T(8,128)S(1)}, f32[256,128]{1,0:T(8,128)S(1)}, u32[]{:S(2)}, u32[]{:S(2)}) %collective-permute-start.10) | collective-permute-done | bytes 131104 | tf_op jit(solution)/shard_map/ppermute | solution.py:448
  48.3 2.8 %within.3 = (f32[128,1024]{1,0:T(8,128)S(1)}, f32[2,16,128]{2,1,0:T(8,128)S(1)}, f32[2,128,128]{2,1,0:T(8,128)S(1)}, f32[1024,128]{1,0:T(8,128)S(1)}, f32[1024,128]{1,0:T(8,128)S(1)}, /*index=5*/f32[16,128]{1,0:T(8,128)S(1)}) custom-call(s32[1,2]{1,0:T(1,128)S(1)} %copy-done.7, f32[32]{0:T(128)S(1)} %copy-done.9, bf16[128,2048]{1,0:T(8,128)(2,1)S(1)} %get-tuple-element.52.x, ...), custom_call_target="tpu_custom_call" | custom-call | flops 65536 | bytes 4096 | tf_op jit(solution)/shard_map/within/pallas_call | solution.py:469
  56.8 1.4 %collective-permute-start.25 = (f32[32,128]{1,0:T(8,128)S(1)}, f32[32,128]{1,0:T(8,128)S(1)}, u32[]{:S(2)}, u32[]{:S(2)}) collective-permute-start(f32[32,128]{1,0:T(8,128)S(1)} %chip_heads.1), channel_id=1, source_target_pairs={{0,24},{4,28},{8,0},{12,4},{16,8},{20,12},{24,16},{28,20},{32,56},... | collective-permute-start | bytes 49160 | tf_op jit(solution)/shard_map/ppermute | solution.py:448
  58.2 1.7 %collective-permute-start.24 = (f32[32,128]{1,0:T(8,128)S(1)}, f32[32,128]{1,0:T(8,128)S(1)}, u32[]{:S(2)}, u32[]{:S(2)}) collective-permute-start(f32[32,128]{1,0:T(8,128)S(1)} %chip_heads.1), channel_id=1, source_target_pairs={{0,16},{4,20},{8,24},{12,28},{16,0},{20,4},{24,8},{28,12},{32,48},... | collective-permute-start | bytes 49160 | tf_op jit(solution)/shard_map/ppermute | solution.py:448
  60.7 2.8 %collective-permute-start.31 = (f32[2,128,128]{2,1,0:T(8,128)S(1)}, f32[2,128,128]{2,1,0:T(8,128)S(1)}, u32[]{:S(2)}, u32[]{:S(2)}) collective-permute-start(f32[2,128,128]{2,1,0:T(8,128)S(1)} %sums.3.refs_0_.refs_2_.bc), channel_id=1, source_target_pairs={{0,3},{1,0},{2,1},{3,2},{4,7},{5,4},{6,5},{7,6},{8,11},{9,8},{10,9... | collective-permute-start | bytes 393224 | tf_op jit(solution)/shard_map/ppermute | solution.py:627
  65.2 2.2 %collective-permute-start.28 = (f32[32,128]{1,0:T(8,128)S(1)}, f32[32,128]{1,0:T(8,128)S(1)}, u32[]{:S(2)}, u32[]{:S(2)}) collective-permute-start(f32[32,128]{1,0:T(8,128)S(1)} %add_add_fusion.refs_4_.own), channel_id=1, source_target_pairs={{0,96},{4,100},{8,104},{12,108},{16,112},{20,116},{24,120},{28,124... | collective-permute-start | bytes 49160 | tf_op jit(solution)/shard_map/ppermute | solution.py:454
  67.7 1.3 %collective-permute-done.28.three = f32[32,128]{1,0:T(8,128)S(1)} collective-permute-done((f32[32,128]{1,0:T(8,128)S(1)}, f32[32,128]{1,0:T(8,128)S(1)}, u32[]{:S(2)}, u32[]{:S(2)}) %collective-permute-start.28) | collective-permute-done | bytes 16416 | tf_op jit(solution)/shard_map/ppermute | solution.py:454
  72.6 1.4 %collective-permute-done.26.one = f32[32,128]{1,0:T(8,128)S(1)} collective-permute-done((f32[32,128]{1,0:T(8,128)S(1)}, f32[32,128]{1,0:T(8,128)S(1)}, u32[]{:S(2)}, u32[]{:S(2)}) %collective-permute-start.26) | collective-permute-done | bytes 16416 | tf_op jit(solution)/shard_map/ppermute | solution.py:454
  (86 shorter events, 27.5 us)
Async XLA Ops:
  6.6 8.6 %collective-permute-start = (f32[1032,128]{1,0:T(8,128)S(1)}, f32[1032,128]{1,0:T(8,128)S(1)}, u32[]{:S(2)}, u32[]{:S(2)}) collective-permute-start(f32[1032,128]{1,0:T(8,128)S(1)} %get-tuple-element.56), channel_id=1, source_target_pairs={{0,4},{4,0},{8,12},{12,8},{16,20},{20,16},{24,28},{28,24},{32,36},... | collective-permute-start | bytes 1585160 | tf_op jit(solution)/shard_map/ppermute | solution.py:444
  9.2 10.0 %collective-permute-start.2 = (f32[264,128]{1,0:T(8,128)S(1)}, f32[264,128]{1,0:T(8,128)S(1)}, u32[]{:S(2)}, u32[]{:S(2)}) collective-permute-start(f32[264,128]{1,0:T(8,128)S(1)} %get-tuple-element.62), channel_id=1, source_target_pairs={{0,8},{4,12},{8,16},{12,20},{16,24},{20,28},{24,0},{28,4},{32,40},... | collective-permute-start | bytes 405512 | tf_op jit(solution)/shard_map/ppermute | solution.py:448
  11.2 11.9 %collective-permute-start.3 = (f32[264,128]{1,0:T(8,128)S(1)}, f32[264,128]{1,0:T(8,128)S(1)}, u32[]{:S(2)}, u32[]{:S(2)}) collective-permute-start(f32[264,128]{1,0:T(8,128)S(1)} %get-tuple-element.63), channel_id=1, source_target_pairs={{0,24},{4,28},{8,0},{12,4},{16,8},{20,12},{24,16},{28,20},{32,56},... | collective-permute-start | bytes 405512 | tf_op jit(solution)/shard_map/ppermute | solution.py:448
  13.4 9.7 %collective-permute-start.4 = (f32[264,128]{1,0:T(8,128)S(1)}, f32[264,128]{1,0:T(8,128)S(1)}, u32[]{:S(2)}, u32[]{:S(2)}) collective-permute-start(f32[264,128]{1,0:T(8,128)S(1)} %get-tuple-element.64), channel_id=1, source_target_pairs={{0,16},{4,20},{8,24},{12,28},{16,0},{20,4},{24,8},{28,12},{32,48},... | collective-permute-start | bytes 405512 | tf_op jit(solution)/shard_map/ppermute | solution.py:448
  15.8 10.5 %collective-permute-start.11 = (f32[264,128]{1,0:T(8,128)S(1)}, f32[264,128]{1,0:T(8,128)S(1)}, u32[]{:S(2)}, u32[]{:S(2)}) collective-permute-start(f32[264,128]{1,0:T(8,128)S(1)} %get-tuple-element.70), channel_id=1, source_target_pairs={{0,8},{4,12},{8,16},{12,20},{16,24},{20,28},{24,0},{28,4},{32,40},... | collective-permute-start | bytes 405512 | tf_op jit(solution)/shard_map/ppermute | solution.py:448
  16.9 10.8 %collective-permute-start.12 = (f32[264,128]{1,0:T(8,128)S(1)}, f32[264,128]{1,0:T(8,128)S(1)}, u32[]{:S(2)}, u32[]{:S(2)}) collective-permute-start(f32[264,128]{1,0:T(8,128)S(1)} %get-tuple-element.71), channel_id=1, source_target_pairs={{0,24},{4,28},{8,0},{12,4},{16,8},{20,12},{24,16},{28,20},{32,56},... | collective-permute-start | bytes 405512 | tf_op jit(solution)/shard_map/ppermute | solution.py:448
  19.2 8.6 %collective-permute-start.13 = (f32[264,128]{1,0:T(8,128)S(1)}, f32[264,128]{1,0:T(8,128)S(1)}, u32[]{:S(2)}, u32[]{:S(2)}) collective-permute-start(f32[264,128]{1,0:T(8,128)S(1)} %get-tuple-element.72), channel_id=1, source_target_pairs={{0,16},{4,20},{8,24},{12,28},{16,0},{20,4},{24,8},{28,12},{32,48},... | collective-permute-start | bytes 405512 | tf_op jit(solution)/shard_map/ppermute | solution.py:448
  23.8 8.1 %collective-permute-start.7 = (f32[264,128]{1,0:T(8,128)S(1)}, f32[264,128]{1,0:T(8,128)S(1)}, u32[]{:S(2)}, u32[]{:S(2)}) collective-permute-start(f32[264,128]{1,0:T(8,128)S(1)} %row_total.2), channel_id=1, source_target_pairs={{4,100},{12,108},{20,116},{28,124},{96,0},{104,8},{112,16},{120,24... | collective-permute-start | bytes 405512 | tf_op jit(solution)/shard_map/ppermute | solution.py:464
  25.1 9.8 %collective-permute-start.6 = (f32[264,128]{1,0:T(8,128)S(1)}, f32[264,128]{1,0:T(8,128)S(1)}, u32[]{:S(2)}, u32[]{:S(2)}) collective-permute-start(f32[264,128]{1,0:T(8,128)S(1)} %row_total.2), channel_id=1, source_target_pairs={{4,68},{12,76},{20,84},{28,92},{36,100},{44,108},{52,116},{60,124}... | collective-permute-start | bytes 405512 | tf_op jit(solution)/shard_map/ppermute | solution.py:464
  26.4 8.5 %collective-permute-start.5 = (f32[264,128]{1,0:T(8,128)S(1)}, f32[264,128]{1,0:T(8,128)S(1)}, u32[]{:S(2)}, u32[]{:S(2)}) collective-permute-start(f32[264,128]{1,0:T(8,128)S(1)} %row_total.2), channel_id=1, source_target_pairs={{4,36},{12,44},{20,52},{28,60},{32,0},{36,68},{40,8},{44,76},{48,1... | collective-permute-start | bytes 405512 | tf_op jit(solution)/shard_map/ppermute | solution.py:464
  28.3 10.9 %collective-permute-start.16 = (f32[264,128]{1,0:T(8,128)S(1)}, f32[264,128]{1,0:T(8,128)S(1)}, u32[]{:S(2)}, u32[]{:S(2)}) collective-permute-start(f32[264,128]{1,0:T(8,128)S(1)} %row_total.3), channel_id=1, source_target_pairs={{4,100},{12,108},{20,116},{28,124},{96,0},{104,8},{112,16},{120,24... | collective-permute-start | bytes 405512 | tf_op jit(solution)/shard_map/ppermute | solution.py:464
  29.6 10.9 %collective-permute-start.15 = (f32[264,128]{1,0:T(8,128)S(1)}, f32[264,128]{1,0:T(8,128)S(1)}, u32[]{:S(2)}, u32[]{:S(2)}) collective-permute-start(f32[264,128]{1,0:T(8,128)S(1)} %row_total.3), channel_id=1, source_target_pairs={{4,68},{12,76},{20,84},{28,92},{36,100},{44,108},{52,116},{60,124}... | collective-permute-start | bytes 405512 | tf_op jit(solution)/shard_map/ppermute | solution.py:464
  31.9 8.6 %collective-permute-start.14 = (f32[264,128]{1,0:T(8,128)S(1)}, f32[264,128]{1,0:T(8,128)S(1)}, u32[]{:S(2)}, u32[]{:S(2)}) collective-permute-start(f32[264,128]{1,0:T(8,128)S(1)} %row_total.3), channel_id=1, source_target_pairs={{4,36},{12,44},{20,52},{28,60},{32,0},{36,68},{40,8},{44,76},{48,1... | collective-permute-start | bytes 405512 | tf_op jit(solution)/shard_map/ppermute | solution.py:464
  35.7 10.2 %collective-permute-start.8 = (f32[256,128]{1,0:T(8,128)S(1)}, f32[256,128]{1,0:T(8,128)S(1)}, u32[]{:S(2)}, u32[]{:S(2)}) collective-permute-start(f32[256,128]{1,0:T(8,128)S(1)} %get-tuple-element.66), channel_id=1, source_target_pairs={{0,16},{4,20},{8,24},{12,28},{16,0},{20,4},{24,8},{28,12},{32,48},... | collective-permute-start | bytes 393224 | tf_op jit(solution)/shard_map/ppermute | solution.py:448
  38.5 7.3 %collective-permute-start.9 = (f32[256,128]{1,0:T(8,128)S(1)}, f32[256,128]{1,0:T(8,128)S(1)}, u32[]{:S(2)}, u32[]{:S(2)}) collective-permute-start(f32[256,128]{1,0:T(8,128)S(1)} %get-tuple-element.67), channel_id=1, source_target_pairs={{0,24},{4,28},{8,0},{12,4},{16,8},{20,12},{24,16},{28,20},{32,56},... | collective-permute-start | bytes 393224 | tf_op jit(solution)/shard_map/ppermute | solution.py:448
  39.3 8.2 %collective-permute-start.10 = (f32[256,128]{1,0:T(8,128)S(1)}, f32[256,128]{1,0:T(8,128)S(1)}, u32[]{:S(2)}, u32[]{:S(2)}) collective-permute-start(f32[256,128]{1,0:T(8,128)S(1)} %get-tuple-element.68), channel_id=1, source_target_pairs={{0,8},{4,12},{8,16},{12,20},{16,24},{20,28},{24,0},{28,4},{32,40},... | collective-permute-start | bytes 393224 | tf_op jit(solution)/shard_map/ppermute | solution.py:448
  41.3 9.9 %collective-permute-start.18 = (f32[256,128]{1,0:T(8,128)S(1)}, f32[256,128]{1,0:T(8,128)S(1)}, u32[]{:S(2)}, u32[]{:S(2)}) collective-permute-start(f32[256,128]{1,0:T(8,128)S(1)} %get-tuple-element.81), channel_id=1, source_target_pairs={{0,16},{4,20},{8,24},{12,28},{16,0},{20,4},{24,8},{28,12},{32,48},... | collective-permute-start | bytes 393224 | tf_op jit(solution)/shard_map/ppermute | solution.py:448
  43.6 7.5 %collective-permute-start.19 = (f32[256,128]{1,0:T(8,128)S(1)}, f32[256,128]{1,0:T(8,128)S(1)}, u32[]{:S(2)}, u32[]{:S(2)}) collective-permute-start(f32[256,128]{1,0:T(8,128)S(1)} %get-tuple-element.82), channel_id=1, source_target_pairs={{0,24},{4,28},{8,0},{12,4},{16,8},{20,12},{24,16},{28,20},{32,56},... | collective-permute-start | bytes 393224 | tf_op jit(solution)/shard_map/ppermute | solution.py:448
  45.8 6.2 %collective-permute-start.20 = (f32[256,128]{1,0:T(8,128)S(1)}, f32[256,128]{1,0:T(8,128)S(1)}, u32[]{:S(2)}, u32[]{:S(2)}) collective-permute-start(f32[256,128]{1,0:T(8,128)S(1)} %get-tuple-element.83), channel_id=1, source_target_pairs={{0,8},{4,12},{8,16},{12,20},{16,24},{20,28},{24,0},{28,4},{32,40},... | collective-permute-start | bytes 393224 | tf_op jit(solution)/shard_map/ppermute | solution.py:448
  56.8 7.5 %collective-permute-start.25 = (f32[32,128]{1,0:T(8,128)S(1)}, f32[32,128]{1,0:T(8,128)S(1)}, u32[]{:S(2)}, u32[]{:S(2)}) collective-permute-start(f32[32,128]{1,0:T(8,128)S(1)} %chip_heads.1), channel_id=1, source_target_pairs={{0,24},{4,28},{8,0},{12,4},{16,8},{20,12},{24,16},{28,20},{32,56},... | collective-permute-start | bytes 49160 | tf_op jit(solution)/shard_map/ppermute | solution.py:448
  58.2 6.9 %collective-permute-start.24 = (f32[32,128]{1,0:T(8,128)S(1)}, f32[32,128]{1,0:T(8,128)S(1)}, u32[]{:S(2)}, u32[]{:S(2)}) collective-permute-start(f32[32,128]{1,0:T(8,128)S(1)} %chip_heads.1), channel_id=1, source_target_pairs={{0,16},{4,20},{8,24},{12,28},{16,0},{20,4},{24,8},{28,12},{32,48},... | collective-permute-start | bytes 49160 | tf_op jit(solution)/shard_map/ppermute | solution.py:448
  60.7 13.3 %collective-permute-start.31 = (f32[2,128,128]{2,1,0:T(8,128)S(1)}, f32[2,128,128]{2,1,0:T(8,128)S(1)}, u32[]{:S(2)}, u32[]{:S(2)}) collective-permute-start(f32[2,128,128]{2,1,0:T(8,128)S(1)} %sums.3.refs_0_.refs_2_.bc), channel_id=1, source_target_pairs={{0,3},{1,0},{2,1},{3,2},{4,7},{5,4},{6,5},{7,6},{8,11},{9,8},{10,9... | collective-permute-start | bytes 393224 | tf_op jit(solution)/shard_map/ppermute | solution.py:627
  63.5 10.6 %collective-permute-start.30 = (f32[2,128,128]{2,1,0:T(8,128)S(1)}, f32[2,128,128]{2,1,0:T(8,128)S(1)}, u32[]{:S(2)}, u32[]{:S(2)}) collective-permute-start(f32[2,128,128]{2,1,0:T(8,128)S(1)} %sums.3.refs_0_.refs_2_.bc), channel_id=1, source_target_pairs={{0,2},{1,3},{2,0},{3,1},{4,6},{5,7},{6,4},{7,5},{8,10},{9,11},{10,... | collective-permute-start | bytes 393224 | tf_op jit(solution)/shard_map/ppermute | solution.py:627
  64.3 9.8 %collective-permute-start.29 = (f32[2,128,128]{2,1,0:T(8,128)S(1)}, f32[2,128,128]{2,1,0:T(8,128)S(1)}, u32[]{:S(2)}, u32[]{:S(2)}) collective-permute-start(f32[2,128,128]{2,1,0:T(8,128)S(1)} %sums.3.refs_0_.refs_2_.bc), channel_id=1, source_target_pairs={{0,1},{1,2},{2,3},{3,0},{4,5},{5,6},{6,7},{7,4},{8,9},{9,10},{10,1... | collective-permute-start | bytes 393224 | tf_op jit(solution)/shard_map/ppermute | solution.py:627
  (19 other events, 41.5 us)
